TPU v7x, 32 devices: a whole 2x2x4 slice. The times are simulated.
32 devices in a mesh: freq: 4 (over y, x), tm: 8 (over z, core).
Axes of the slice: x: 2, y: 2, z: 4, core: 2. Of those that a mesh axis runs over, the one named last changes fastest.
Arguments:
- visibilities: bfloat16 [4, 8, 2, 512, 512], P('freq', 'tm'), may hold values from -1.796875 to 1.796875
- model_vis: bfloat16 [4, 8, 2, 512, 512], P('freq'), may hold values from -0.1796875 to 0.1796875
- station_flags: int32 [4, 8, 512], P('freq', 'tm'), may hold values 0 or 1
- initial_gains: float32 [4, 8, 2, 8, 512], P('freq', 'tm'), may hold values from -6 to 6
- initial_duals: float32 [4, 8, 2, 8, 512], P('freq', 'tm'), may hold values from -1.8 to 1.8
Outputs:
- solved_gains: float32 [4, 8, 2, 8, 512], P('freq', 'tm')
- consensus: float32 [4, 8, 2, 8, 512], P('freq', 'tm')
- final_duals: float32 [4, 8, 2, 8, 512], P('freq', 'tm')
All inputs are finite; a program needn't handle non-finite values. No bound on the sum of `station_flags` on one device may be relied on, other than what follows from the above.
Results may differ from a plain program's by a relative error of at most 0.0003.
Values sent between devices are 32-bit elements; how exact they have to be, the bound alone decides.
No kernel may reach another device: no remote copies, remote signals or barrier semaphores. Data moves between devices by JAX's collectives and lax.ppermute only.
A program may use at most 64 MiB of HBM per device.

v0:
```python
import math

import jax
import jax.numpy as jnp
from jax import lax
from jax.sharding import PartitionSpec as P

ITERS = 2


penalty = 1.0


def poly_basis(length, position, order_count):
    centre = position - (length - 1) / 2.0
    constant = jnp.ones_like(position) / math.sqrt(length)
    linear = centre / math.sqrt(length * (length * length - 1) / 12.0)
    stacked = [constant, linear]
    if order_count == 3:
        quadratic = (centre * centre - (length * length - 1) / 12.0) / math.sqrt(
            length * (length * length - 1) * (length * length - 4) / 180.0
        )
        stacked.append(quadratic)
    return jnp.stack(stacked, axis=0)


def local_solve(vis_block, model_block, flag_block, gains_block, target_block):
    real_vis = vis_block[0].astype(jnp.float32)
    imag_vis = vis_block[1].astype(jnp.float32)
    model_real = model_block[:, 0].astype(jnp.float32)
    model_imag = model_block[:, 1].astype(jnp.float32)
    gain_real = gains_block[0]
    gain_imag = gains_block[1]
    weight = flag_block.astype(jnp.float32)
    outer_real = (
        gain_real[:, :, None] * gain_real[:, None, :]
        + gain_imag[:, :, None] * gain_imag[:, None, :]
    )
    outer_imag = (
        gain_imag[:, :, None] * gain_real[:, None, :]
        - gain_real[:, :, None] * gain_imag[:, None, :]
    )
    pred_real = jnp.sum(model_real * outer_real - model_imag * outer_imag, axis=0)
    pred_imag = jnp.sum(model_real * outer_imag + model_imag * outer_real, axis=0)
    pair_weight = weight[:, None] * weight[None, :]
    resid_real = (real_vis - pred_real) * pair_weight
    resid_imag = (imag_vis - pred_imag) * pair_weight
    proj_real = model_real * gain_real[:, None, :] + model_imag * gain_imag[:, None, :]
    proj_imag = model_real * gain_imag[:, None, :] - model_imag * gain_real[:, None, :]
    numer_real = jnp.sum(resid_real[None] * proj_real - resid_imag[None] * proj_imag, axis=2)
    numer_imag = jnp.sum(resid_real[None] * proj_imag + resid_imag[None] * proj_real, axis=2)
    gain_power = (gain_real * gain_real + gain_imag * gain_imag) * weight
    curvature = weight[None, :] * jnp.sum(
        (model_real * model_real + model_imag * model_imag) * gain_power[:, None, :], axis=2
    )
    divisor = curvature + penalty
    new_real = (numer_real + curvature * gain_real + penalty * target_block[0]) / divisor
    new_imag = (numer_imag + curvature * gain_imag + penalty * target_block[1]) / divisor
    return jnp.stack([new_real, new_imag], axis=0)


def polynomial_fit(merged, freq_basis, time_basis):
    time_terms = time_basis[:, None] * merged[None, :]
    time_part = lax.psum_scatter(time_terms, "tm", scatter_dimension=1, tiled=True)
    both_terms = (freq_basis[:, None, None] * time_part[None]).reshape(-1, time_part.shape[1])
    both_part = lax.psum_scatter(both_terms, "freq", scatter_dimension=1, tiled=True)
    both_whole = lax.all_gather(both_part, "freq", axis=1, tiled=True).reshape(
        freq_basis.shape[0], time_basis.shape[0], -1
    )
    time_values = jnp.sum(freq_basis[:, None, None] * both_whole, axis=0)
    time_whole = lax.all_gather(time_values, "tm", axis=1, tiled=True)
    return jnp.sum(time_basis[:, None] * time_whole, axis=0)


def per_device(visibilities, model_vis, station_flags, initial_gains, initial_duals):
    freq_count = lax.axis_size("freq")
    time_count = lax.axis_size("tm")
    freq_basis = poly_basis(freq_count, lax.axis_index("freq").astype(jnp.float32), 3)
    time_basis = poly_basis(time_count, lax.axis_index("tm").astype(jnp.float32), 2)
    vis_block = visibilities[0, 0]
    model_block = model_vis[0]
    flag_block = station_flags[0, 0]
    current = initial_gains[0, 0]
    scaled_dual = initial_duals[0, 0]
    consensus = current
    for iteration in range(ITERS):
        merged = (current + scaled_dual).reshape(-1)
        consensus = polynomial_fit(merged, freq_basis, time_basis).reshape(current.shape)
        scaled_dual = scaled_dual + current - consensus
        target = consensus - scaled_dual
        current = local_solve(vis_block, model_block, flag_block, current, target)
    return (current[None, None], consensus[None, None], scaled_dual[None, None])


def solution(mesh):
    in_specs = (
        P("freq", "tm", None, None, None),
        P("freq", None, None, None, None),
        P("freq", "tm", None),
        P("freq", "tm", None, None, None),
        P("freq", "tm", None, None, None),
    )
    out_specs = (
        P("freq", "tm", None, None, None),
        P("freq", "tm", None, None, None),
        P("freq", "tm", None, None, None),
    )
    return jax.shard_map(
        per_device, mesh=mesh, in_specs=in_specs, out_specs=out_specs, check_vma=False
    )
```

profile of v0, /device:TPU:1, one launch (start us, length us, event | category | flops | bytes accessed | tf_op | source)
XLA Modules:
  0.0 219.3 jit_solution(4383496662875238428)
XLA Ops:
  7.2 0.8 add.233
  8.0 0.1 pad_maximum_fusion.1
  8.1 0.1 broadcast_multiply_fusion.1
  8.2 2.6 %copy.12 = f32[2,8192]{0,1:T(8,128)} copy(f32[2,8192]{1,0:T(2,128)S(1)} %broadcast_multiply_fusion.1) | data formatting | bytes 131072
  11.0 0.1 pad_maximum_fusion.2
  11.1 0.1 mul.599
  11.2 7.0 %fusion.1 = (f32[512,512]{1,0:T(8,128)S(1)}, f32[512,512]{1,0:T(8,128)S(1)}) fusion(f32[8,512]{1,0:T(8,128)S(1)} %get-tuple-element.25, f32[8,512]{1,0:T(8,128)S(1)} %get-tuple-element.24, bf16[8,2,512,512]{3,2,1,0:T(8,128)(2,1)} %bitcast.144), kind=kLoop, calls=%fused_computation.19 | loop fusion | flops 33030144 | bytes 10551296 | tf_op jit(solution)/shard_map/reduce_sum | solution.py:43
  18.3 0.3 multiply_multiply_fusion.3
  18.6 42.4 %reduce-scatter.13.cloned.1.call-done = f32[1024,2]{1,0:T(8,128)} async-done(((f32[8192,2]{1,0:T(8,128)}), f32[1024,2]{1,0:T(8,128)}) %reduce-scatter.13.cloned.1.call-update) | async-done | bytes 8208
  61.0 1.2 copy.13
  62.2 0.7 broadcast_multiply_fusion.3
  63.0 10.8 %subtract_reduce_fusion.1 = (f32[8,512]{1,0:T(8,128)S(1)}, f32[8,512]{1,0:T(8,128)S(1)}, f32[8,512]{1,0:T(8,128)S(1)}) fusion(f32[512,512]{1,0:T(8,128)S(1)} %get-tuple-element.19, f32[512,512]{1,0:T(8,128)S(1)} %get-tuple-element.18, f32[8,512]{1,0:T(8,128)S(1)} %get-tuple-element.25, f32[8,512]{1,0:T(8,128)S(1)} %get-tuple-element.24, ...), kind=kLoop, calls=%fused_computation.38 | loop fusion | flops 44027904 | bytes 10584064 | tf_op jit(solution)/shard_map/reduce_sum | solution.py:50
  73.8 13.9 %reduce-scatter.9.cloned.1.call-done = f32[6,256]{1,0:T(8,128)} async-done(((f32[6,1024]{1,0:T(8,128)}), f32[6,256]{1,0:T(8,128)}) %reduce-scatter.9.cloned.1.call-update) | async-done | bytes 6160 | tf_op jit(solution)/shard_map/reduce_scatter | solution.py:66
  87.7 6.1 %all_gather.12 = f32[6,1024]{1,0:T(8,128)S(1)} all-gather(f32[6,256]{1,0:T(8,128)} %reduce-scatter.9.cloned.1.call-done), channel_id=1, replica_groups=mesh['freq'=4,'tm'=8] {'freq'}, dimensions={1}, use_global_device_ids=true | all-gather | bytes 30720 | tf_op jit(solution)/shard_map/all_gather | solution.py:67
  93.8 0.1 multiply_reduce_fusion.5
  93.8 17.0 %all_gather.13 = f32[2,8192]{1,0:T(2,128)S(1)} all-gather(f32[2,1024]{1,0:T(2,128)S(1)} %multiply_reduce_fusion.5), channel_id=1, replica_groups=mesh['freq'=4,'tm'=8] {'tm'}, dimensions={1}, use_global_device_ids=true | all-gather | bytes 73728 | tf_op jit(solution)/shard_map/all_gather | solution.py:71
  110.8 0.1 multiply_reduce_fusion.3
  111.1 0.1 broadcast_multiply_fusion
  111.2 2.6 %copy.14 = f32[2,8192]{0,1:T(8,128)} copy(f32[2,8192]{1,0:T(2,128)S(1)} %broadcast_multiply_fusion) | data formatting | bytes 131072
  113.9 7.0 %fusion.8 = (f32[512,512]{1,0:T(8,128)S(1)}, f32[512,512]{1,0:T(8,128)S(1)}) fusion(f32[8,512]{1,0:T(8,128)S(1)} %get-tuple-element.15, f32[8,512]{1,0:T(8,128)S(1)} %get-tuple-element.14, bf16[8,2,512,512]{3,2,1,0:T(8,128)(2,1)} %bitcast.146), kind=kLoop, calls=%fused_computation.26 | loop fusion | flops 33030144 | bytes 10551296 | tf_op jit(solution)/shard_map/reduce_sum | solution.py:43
  120.9 0.3 multiply_multiply_fusion.1
  121.3 40.1 %reduce-scatter.15.cloned.1.call-done = f32[1024,2]{1,0:T(8,128)} async-done(((f32[8192,2]{1,0:T(8,128)}), f32[1024,2]{1,0:T(8,128)}) %reduce-scatter.15.cloned.1.call-update) | async-done | bytes 8208
  161.3 1.2 copy.15
  162.6 0.7 broadcast_multiply_fusion.2
  163.3 10.8 %subtract_reduce_fusion = (f32[8,512]{1,0:T(8,128)S(1)}, f32[8,512]{1,0:T(8,128)S(1)}, f32[8,512]{1,0:T(8,128)S(1)}) fusion(f32[512,512]{1,0:T(8,128)S(1)} %get-tuple-element.17, f32[512,512]{1,0:T(8,128)S(1)} %get-tuple-element.16, f32[8,512]{1,0:T(8,128)S(1)} %get-tuple-element.15, f32[8,512]{1,0:T(8,128)S(1)} %get-tuple-element.14, ...), kind=kLoop, calls=%fused_computation.33 | loop fusion | flops 44027904 | bytes 10584064 | tf_op jit(solution)/shard_map/reduce_sum | solution.py:50
  174.1 14.0 %reduce-scatter.11.cloned.1.call-done = f32[6,256]{1,0:T(8,128)} async-done(((f32[6,1024]{1,0:T(8,128)}), f32[6,256]{1,0:T(8,128)}) %reduce-scatter.11.cloned.1.call-update) | async-done | bytes 6160 | tf_op jit(solution)/shard_map/reduce_scatter | solution.py:66
  188.1 6.1 %all_gather.14 = f32[6,1024]{1,0:T(8,128)S(1)} all-gather(f32[6,256]{1,0:T(8,128)} %reduce-scatter.11.cloned.1.call-done), channel_id=1, replica_groups=mesh['freq'=4,'tm'=8] {'freq'}, dimensions={1}, use_global_device_ids=true | all-gather | bytes 30720 | tf_op jit(solution)/shard_map/all_gather | solution.py:67
  194.3 0.1 multiply_reduce_fusion.4
  194.3 16.9 %all_gather.15 = f32[2,8192]{1,0:T(2,128)S(1)} all-gather(f32[2,1024]{1,0:T(2,128)S(1)} %multiply_reduce_fusion.4), channel_id=1, replica_groups=mesh['freq'=4,'tm'=8] {'tm'}, dimensions={1}, use_global_device_ids=true | all-gather | bytes 73728 | tf_op jit(solution)/shard_map/all_gather | solution.py:71
  211.3 0.1 multiply_reduce_fusion.2
  211.5 0.6 maximum_bitcast_fusion
  212.2 0.6 fusion.13
  (39 shorter events, 0.6 us)
Async XLA Ops:
  7.2 3.7 %copy-start.1 = (f32[1,1,2,8,512]{4,3,2,1,0:T(8,128)S(1)}, f32[1,1,2,8,512]{4,3,2,1,0:T(8,128)}, u32[]{:S(2)}) copy-start(f32[1,1,2,8,512]{4,3,2,1,0:T(8,128)} %param.8) | copy-start | bytes 98308
  7.2 3.8 %copy-start.3 = (s32[1,1,512]{2,1,0:T(1,128)S(1)}, s32[1,1,512]{2,1,0:T(1,128)}, u32[]{:S(2)}) copy-start(s32[1,1,512]{2,1,0:T(1,128)} %param.7) | copy-start | bytes 6148
  7.2 53.8 %reduce-scatter.13.cloned.1.call-start = ((), (), s32[]{:S(2)}) async-start(), calls=%async_computation.6 | async-start | bytes 4718592
  10.8 7.4 %copy-start = (bf16[1,1,2,512,512]{4,3,2,1,0:T(8,128)(2,1)S(1)}, bf16[1,1,2,512,512]{4,3,2,1,0:T(8,128)(2,1)}, u32[]{:S(2)}) copy-start(bf16[1,1,2,512,512]{4,3,2,1,0:T(8,128)(2,1)} %param.5) | copy-start | bytes 3145732
  10.8 76.8 %reduce-scatter.9.cloned.1.call-start = ((), (), s32[]{:S(2)}) async-start(), calls=%async_computation.4 | async-start | bytes 40960 | tf_op jit(solution)/shard_map/reduce_scatter | solution.py:66
  62.9 98.4 %reduce-scatter.15.cloned.1.call-start = ((), (), s32[]{:S(2)}) async-start(), calls=%async_computation.7 | async-start | bytes 4718592
  113.8 74.3 %reduce-scatter.11.cloned.1.call-start = ((), (), s32[]{:S(2)}) async-start(), calls=%async_computation.5 | async-start | bytes 40960 | tf_op jit(solution)/shard_map/reduce_scatter | solution.py:66
  211.5 1.3 copy-start.2
Sparse Core Ops, SparseCore 0:
  11.0 49.9 reduce-scatter.12
  64.3 23.3 reduce-scatter.8
  114.0 47.3 reduce-scatter.14
  164.7 23.3 reduce-scatter.10
where the time goes:
time: 220 us; the launch traced here: 219 us
  waiting for transfers between devices  110 us (50%)
  blocking collectives  46.1 us (21%)
  other arithmetic  40.5 us (18%)
  between operations  14.1 us (6%)
  local copies, waits for them, and re-layouts  8.01 us (4%)
    unnamed x6, waiting for transfers between devices  82.5 us
    all_gather x2, blocking collectives, polynomial_fit(): time_whole = lax.all_gather(time_values, 'tm', axis=1, tiled=True)  33.9 us
    reduce_scatter x2, waiting for transfers between devices, polynomial_fit(): lax.psum_scatter(both_terms, 'freq', scatter_dimension=1, tiled=True)  27.9 us
    reduce_sum x2, other arithmetic, local_solve(): jnp.sum(resid_real[None] * proj_real - resid_imag[None] * proj_imag, axis=2)  21.5 us
    reduce_sum x2, other arithmetic, local_solve(): jnp.sum(model_real * outer_real - model_imag * outer_imag, axis=0)  14.1 us
    all_gather x2, blocking collectives, polynomial_fit(): lax.all_gather(both_part, 'freq', axis=1, tiled=True)  12.2 us
    unnamed x14, local copies, waits for them, and re-layouts  7.72 us
  transfers between devices with their start and end apart: 4, of which 4 were waited for; matrix products, arithmetic and copies ran while one was open for 17% of the time, Pallas kernels for 0%

commit v1 on v0

v1 whole, which is shorter than its diff:
```python
import functools
import math

import jax
import jax.numpy as jnp
from jax import lax
from jax.experimental import pallas as pl
from jax.experimental.pallas import tpu as pltpu
from jax.sharding import PartitionSpec as P

ITERS = 2
LANES = 128
ROWS = 16
FREQ_ORDERS = 3
TIME_ORDERS = 2

penalty = 1.0
f32 = jnp.float32


def poly_basis(length, position, order_count):
    centre = position - (length - 1) / 2.0
    stacked = [jnp.ones_like(position) * (1.0 / math.sqrt(length)), centre * (1.0 / math.sqrt(length * (length * length - 1) / 12.0))]
    if order_count == 3:
        scale = math.sqrt(length * (length * length - 1) * (length * length - 4) / 180.0)
        stacked.append((centre * centre - (length * length - 1) / 12.0) * (1.0 / scale))
    return stacked


def whole_vmem(count):
    return [pl.BlockSpec(memory_space=pltpu.VMEM)] * count


def exchange(array, axis, distance):
    size = lax.axis_size(axis)
    return lax.ppermute(array, axis, [(place, place ^ distance) for place in range(size)])


def axis_plan(size, orders, distances):
    steps = []
    held, sums = 1, False
    for at in range(len(distances)):
        if at == len(distances) - 1:
            steps.append((1, False, held, sums))
            break
        sent = held
        if sums:
            steps.append((sent, False, held, sums))
            continue
        held = 2 * held
        turn = held > orders and at < len(distances) - 2
        steps.append((sent, turn, held, sums))
        if turn:
            held, sums = orders, True
    return steps


def heard_places(index, distances):
    places = [index]
    for distance in distances:
        places = places + [place ^ distance for place in places]
    return places


def axis_weights(size, orders, distances, index):
    weights = []

    def basis(place):
        return poly_basis(size, lax.convert_element_type(place, f32), orders)

    def products(one, other):
        return sum(a * b for a, b in zip(one, other))

    plan = axis_plan(size, orders, distances)
    raw = [index]
    for at, (sent, turn, held, sums) in enumerate(plan):
        if at == len(plan) - 1:
            for target in (index ^ distances[at], index):
                if sums:
                    weights += basis(target)
                else:
                    weights += [products(basis(target), basis(place)) for place in raw]
        elif not sums:
            raw = raw + [place ^ distances[at] for place in raw]
            if turn:
                for place in raw:
                    weights += basis(place)
    return weights


def weight_count(size, orders, distances):
    total, raw = 0, 1
    plan = axis_plan(size, orders, distances)
    for at, (sent, turn, held, sums) in enumerate(plan):
        if at == len(plan) - 1:
            total += 2 * (orders if sums else raw)
        elif not sums:
            raw *= 2
            if turn:
                total += raw * orders
    return total


def tied(array, others):
    return lax.optimization_barrier((array, others))


class Work:
    def __init__(self, parts):
        self.parts = parts
        self.results = []

    def beside(self, sent):
        part = self.parts[len(self.results)]
        result, sent = part(sent)
        self.results.append(result)
        return result


def axis_exchange(state, axis, orders, distances, weights, work, finish):
    size = lax.axis_size(axis)
    plan = axis_plan(size, orders, distances)
    weights = list(weights)
    held = [state]
    for at, (sent, turn, _, sums) in enumerate(plan):
        if at == len(plan) - 1:
            away = weights[: len(held)]
            own = weights[len(held) :]
            message = sum(w * a for w, a in zip(away, held))
            got = work(message, axis, distances[at])
            if not finish:
                return None, list(zip(own, held)), got
            return sum(w * a for w, a in zip(own, held)) + got, None, None
        message = held[0] if len(held) == 1 else jnp.stack(held)
        got = work(message, axis, distances[at])
        got = [got] if len(held) == 1 else [got[i] for i in range(len(held))]
        if sums:
            held = [a + b for a, b in zip(held, got)]
            continue
        held = held + got
        if turn:
            taken, weights = weights[: len(held) * orders], weights[len(held) * orders :]
            held = [sum(taken[i * orders + j] * a for i, a in enumerate(held)) for j in range(orders)]


def setup_kernel(plans, gains_ref, duals_ref, flags_ref, merged_ref, masked_ref, turned_ref, mask_ref, *weight_refs):
    gains = gains_ref[...]
    mask = flags_ref[...].astype(f32)
    mask_ref[...] = mask
    merged_ref[...] = gains + duals_ref[...]
    masked_ref[...] = gains * mask[None]
    turned_ref[...] = turn(gains)
    at = 0
    shape = weight_refs[0].shape
    for axis, size, orders, distances in plans:
        index = jnp.full((8, LANES), lax.axis_index(axis), jnp.int32)
        for weight in axis_weights(size, orders, distances, index):
            weight_refs[at][...] = jnp.broadcast_to(jnp.tile(weight, (shape[1] // 8, shape[2] // LANES))[None], shape)
            at += 1


def turn(gains):
    flat = gains.reshape(-1, gains.shape[-1])
    padded = jnp.concatenate([flat, jnp.zeros((LANES - flat.shape[0], flat.shape[1]), f32)], axis=0)
    return padded.T


def part_kernel(start, unroll, model_ref, vis_ref, masked_ref, turned_ref, sums_ref):
    directions = model_ref.shape[0]
    receptors = model_ref.shape[3]

    def rows_of(at, carry):
        first = pl.multiple_of(at * ROWS, ROWS)
        rows = pl.ds(pl.multiple_of(start + first, ROWS), ROWS)
        turned = turned_ref[rows, :]
        near = [jnp.broadcast_to(turned[:, k : k + 1], (ROWS, LANES)) for k in range(2 * directions)]
        sums = [None] * (3 * directions)
        for block in range(receptors // LANES):
            columns = pl.ds(block * LANES, LANES)
            resid_real = vis_ref[0, rows, columns].astype(f32)
            resid_imag = vis_ref[1, rows, columns].astype(f32)
            moved = []
            for k in range(directions):
                model_real = model_ref[k, 0, rows, columns].astype(f32)
                model_imag = model_ref[k, 1, rows, columns].astype(f32)
                gain_real = masked_ref[0, k : k + 1, columns]
                gain_imag = masked_ref[1, k : k + 1, columns]
                moved_real = model_real * gain_real + model_imag * gain_imag
                moved_imag = model_imag * gain_real - model_real * gain_imag
                moved.append((moved_real, moved_imag))
                resid_real = resid_real - (near[k] * moved_real - near[directions + k] * moved_imag)
                resid_imag = resid_imag - (near[k] * moved_imag + near[directions + k] * moved_real)
            for k, (moved_real, moved_imag) in enumerate(moved):
                terms = (
                    resid_real * moved_real + resid_imag * moved_imag,
                    resid_imag * moved_real - resid_real * moved_imag,
                    moved_real * moved_real + moved_imag * moved_imag,
                )
                for kind, term in enumerate(terms):
                    place = kind * directions + k
                    sums[place] = term if block == 0 else sums[place] + term
        lane = lax.broadcasted_iota(jnp.int32, (ROWS, LANES), 1)
        out = jnp.zeros((ROWS, LANES), f32)
        for place, total in enumerate(sums):
            out = jnp.where(lane == place, jnp.sum(total, axis=1, keepdims=True), out)
        sums_ref[pl.ds(first, ROWS), :] = out
        return carry

    lax.fori_loop(0, sums_ref.shape[0] // ROWS, rows_of, 0, unroll=unroll)


def update_kernel(parts, terms, last, *refs):
    sums_refs, refs = refs[:parts], refs[parts:]
    weight_refs, held_refs, refs = refs[:terms], refs[terms : 2 * terms], refs[2 * terms :]
    got_ref, merged_ref, gains_ref, mask_ref = refs[:4]
    outs = refs[4:]
    sums = jnp.concatenate([ref[...] for ref in sums_refs], axis=0).T
    gains = gains_ref[...]
    mask = mask_ref[...]
    directions = gains.shape[1]
    consensus = got_ref[...]
    for weight_ref, held_ref in zip(weight_refs, held_refs):
        consensus = consensus + weight_ref[...] * held_ref[...]
    duals = merged_ref[...] - consensus
    target = consensus - duals
    curvature = sums[2 * directions : 3 * directions] * mask
    divisor = curvature + penalty
    solved = []
    for part in range(2):
        numer = sums[part * directions : (part + 1) * directions] * mask
        solved.append((numer + curvature * gains[part] + penalty * target[part]) / divisor)
    solved = jnp.stack(solved)
    if last:
        for ref, value in zip(outs, (solved, consensus, duals)):
            ref[...] = value
    else:
        for ref, value in zip(outs, (solved, solved + duals, solved * mask[None], turn(solved))):
            ref[...] = value


def cut(total, shares):
    whole = sum(shares)
    ends = [0]
    done = 0.0
    for share in shares:
        done += share
        ends.append(round(total * done / whole))
    return [max(0, b - a) for a, b in zip(ends, ends[1:])]


def per_device(visibilities, model_vis, station_flags, initial_gains, initial_duals):
    vis_block = visibilities[0, 0]
    model_block = model_vis[0]
    flag_block = station_flags[0]
    gains = initial_gains[0, 0]
    duals = initial_duals[0, 0]
    _, directions, receptors = gains.shape
    state = jax.ShapeDtypeStruct(gains.shape, f32)
    turned_shape = jax.ShapeDtypeStruct((receptors, LANES), f32)

    freq_count, time_count = lax.axis_size("freq"), lax.axis_size("tm")
    freq_steps = [1 << b for b in range(freq_count.bit_length() - 1)]
    time_steps = [1 << b for b in reversed(range(time_count.bit_length() - 1))]
    plans = (
        ("freq", freq_count, FREQ_ORDERS, tuple(freq_steps)),
        ("tm", time_count, TIME_ORDERS, tuple(time_steps)),
    )
    counts = [weight_count(*plan[1:]) for plan in plans]

    merged, masked, turned, mask, *weights = pl.pallas_call(
        functools.partial(setup_kernel, plans),
        out_shape=[state, state, turned_shape, jax.ShapeDtypeStruct((1, receptors), f32)] + [state] * sum(counts),
        in_specs=whole_vmem(3),
        out_specs=whole_vmem(4 + sum(counts)),
        compiler_params=pltpu.CompilerParams(vmem_limit_bytes=16 * 2**20),
        name="setup",
    )(gains, duals, flag_block)
    freq_weights, time_weights = weights[: counts[0]], weights[counts[0] :]

    steps = len(freq_steps) + len(time_steps)
    shares = [1.0] * (steps - 1) + [0.45]
    lengths = [ROWS * units for units in cut(receptors // ROWS, shares)]
    starts = [sum(lengths[:i]) for i in range(steps)]
    pairs = directions * receptors

    def part(number, masked, turned):
        length = lengths[number]
        return pl.pallas_call(
            functools.partial(part_kernel, starts[number], 4),
            out_shape=jax.ShapeDtypeStruct((length, LANES), f32),
            in_specs=whole_vmem(4),
            out_specs=pl.BlockSpec(memory_space=pltpu.VMEM),
            compiler_params=pltpu.CompilerParams(vmem_limit_bytes=32 * 2**20),
            cost_estimate=pl.CostEstimate(flops=28 * pairs * length, bytes_accessed=4 * pairs * length, transcendentals=0),
            name=f"part{number}",
        )(model_block, vis_block, masked, turned)

    for iteration in range(ITERS):
        last = iteration == ITERS - 1
        results = []

        def work(message, axis, distance):
            message, one, two = lax.optimization_barrier((message, masked, turned))
            got = exchange(message, axis, distance)
            result = part(len(results), one, two)
            got, result = lax.optimization_barrier((got, result))
            results.append(result)
            return got

        along_freq, _, _ = axis_exchange(merged, "freq", FREQ_ORDERS, freq_steps, freq_weights, work, True)
        _, terms, got = axis_exchange(along_freq, "tm", TIME_ORDERS, time_steps, time_weights, work, False)
        outs = [state] * 3 + ([] if last else [turned_shape])
        operands = results + [w for w, _ in terms] + [a for _, a in terms] + [got, merged, gains, mask]
        outputs = pl.pallas_call(
            functools.partial(update_kernel, len(results), len(terms), last),
            out_shape=outs,
            in_specs=whole_vmem(len(operands)),
            out_specs=whole_vmem(len(outs)),
            compiler_params=pltpu.CompilerParams(vmem_limit_bytes=16 * 2**20),
            name="finish" if last else "update",
        )(*operands)
        if last:
            return tuple(out[None, None] for out in outputs)
        gains, merged, masked, turned = outputs


def solution(mesh):
    in_specs = (
        P("freq", "tm", None, None, None),
        P("freq", None, None, None, None),
        P("freq", "tm", None),
        P("freq", "tm", None, None, None),
        P("freq", "tm", None, None, None),
    )
    out_specs = (
        P("freq", "tm", None, None, None),
        P("freq", "tm", None, None, None),
        P("freq", "tm", None, None, None),
    )
    return jax.shard_map(
        per_device, mesh=mesh, in_specs=in_specs, out_specs=out_specs, check_vma=False
    )
```

time: 220 us -> 47.2 us (0.21)
  waiting for transfers between devices: 110 us -> 0.03 us
  blocking collectives: 46.1 us -> 0 us
  other arithmetic: 40.5 us -> 0.12 us
  Pallas kernels: 0 us -> 20.1 us
  starting transfers between devices: 0.16 us -> 18 us
  between operations: 14.1 us -> 0.87 us
    unnamed x6 -> x0, waiting for transfers between devices: 82.5 us -> none
    all_gather x4 -> x0, blocking collectives: 46.1 us -> none  [the longest x2 33.9 us: polynomial_fit(): time_whole = lax.all_gather(time_values, 'tm', axis=1, tiled=True)]
    reduce_sum x8 -> x0, other arithmetic: 36.1 us -> none  [the longest x2 21.5 us: local_solve(): jnp.sum(resid_real[None] * proj_real - resid_imag[None] * proj_imag, axis=2)]
    reduce_scatter x2 -> x0, waiting for transfers between devices: 27.9 us -> none  [polynomial_fit(): lax.psum_scatter(both_terms, 'freq', scatter_dimension=1, tiled=True)]
    pallas_call x0 -> x13, Pallas kernels: none -> 20.1 us  [the longest x10 19 us: part(): pl.pallas_call(functools.partial(part_kernel, starts[number], 4), out_sha...]
    ppermute x0 -> x10, starting transfers between devices: none -> 18 us  [exchange(): lax.ppermute(array, axis, [(place, place ^ distance) for place in range(s...]
    mul x8 -> x0, other arithmetic: 2.2 us -> none  [the longest x2 1.37 us: polynomial_fit(): freq_basis[:, None, None] * time_part[None]]
    unnamed x14 -> x18, local copies, waits for them, and re-layouts: 7.72 us -> 7.45 us
  transfers between devices with their start and end apart: 4 -> 10, of which waited for: 4 -> 0; matrix products, arithmetic and copies ran while one was open for 17% -> 0% of each run, Pallas kernels for 0% -> 41%
where the time goes in v1:
time: 47.2 us; the launch traced here: 46.6 us
  Pallas kernels  20.1 us (43%)
  starting transfers between devices  18 us (38%)
  local copies, waits for them, and re-layouts  7.46 us (16%)
  between operations  0.87 us (2%)
    pallas_call x10, Pallas kernels, part(): pl.pallas_call(functools.partial(part_kernel, starts[number], 4), out_sha...  19 us
    ppermute x10, starting transfers between devices, exchange(): lax.ppermute(array, axis, [(place, place ^ distance) for place in range(s...  18 us
    unnamed x18, local copies, waits for them, and re-layouts  7.45 us
    pallas_call x2, Pallas kernels, per_device(): pl.pallas_call(functools.partial(update_kernel, len(results), len(terms),...  0.97 us
  transfers between devices with their start and end apart: 10, of which 0 were waited for; matrix products, arithmetic and copies ran while one was open for 0% of the time, Pallas kernels for 41%

profile of v1, /device:TPU:1, one launch (start us, length us, event | category | flops | bytes accessed | tf_op | source)
XLA Modules:
  0.0 46.6 jit_solution(524192019473939854)
XLA Ops:
  0.6 0.0 copy-start.3
  0.6 0.7 %copy-done.3 = f32[1,1,2,8,512]{4,3,2,1,0:T(8,128)S(1)} copy-done((f32[1,1,2,8,512]{4,3,2,1,0:T(8,128)S(1)}, f32[1,1,2,8,512]{4,3,2,1,0:T(8,128)}, u32[]{:S(2)}) %copy-start.3) | copy-done | bytes 32792
  1.4 0.8 %copy-done.5 = f32[1,1,2,8,512]{4,3,2,1,0:T(8,128)S(1)} copy-done((f32[1,1,2,8,512]{4,3,2,1,0:T(8,128)S(1)}, f32[1,1,2,8,512]{4,3,2,1,0:T(8,128)}, u32[]{:S(2)}) %copy-start.5) | copy-done | bytes 32792
  2.2 0.7 %copy-done.6 = s32[1,1,512]{2,1,0:T(1,128)S(1)} copy-done((s32[1,1,512]{2,1,0:T(1,128)S(1)}, s32[1,1,512]{2,1,0:T(1,128)}, u32[]{:S(2)}) %copy-start.6) | copy-done | bytes 2072
  2.8 0.1 setup.1
  3.0 2.1 %collective-permute-start = (f32[2,8,512]{2,1,0:T(8,128)S(1)}, f32[2,8,512]{2,1,0:T(8,128)S(1)}, u32[]{:S(2)}, u32[]{:S(2)}) collective-permute-start(f32[2,8,512]{2,1,0:T(8,128)S(1)} %get-tuple-element.79.refs_14_), channel_id=1, source_target_pairs={{0,8},{8,0},{16,24},{24,16},{1,9},{9,1},{17,25},{25,17},{2,10},{10... | collective-permute-start | bytes 98312 | tf_op jit(solution)/shard_map/ppermute | solution.py:36
  5.1 3.4 %copy-done = bf16[1,8,2,512,512]{4,3,2,1,0:T(8,128)(2,1)S(1)} copy-done((bf16[1,8,2,512,512]{4,3,2,1,0:T(8,128)(2,1)S(1)}, bf16[1,8,2,512,512]{4,3,2,1,0:T(8,128)(2,1)}, u32[]{:S(2)}) %copy-start) | copy-done | bytes 8388632
  8.5 1.2 %copy-done.1 = bf16[1,1,2,512,512]{4,3,2,1,0:T(8,128)(2,1)S(1)} copy-done((bf16[1,1,2,512,512]{4,3,2,1,0:T(8,128)(2,1)S(1)}, bf16[1,1,2,512,512]{4,3,2,1,0:T(8,128)(2,1)}, u32[]{:S(2)}) %copy-start.1) | copy-done | bytes 1048600
  9.7 2.1 %part0.2.refs_0_ = f32[112,128]{1,0:T(8,128)S(1)} custom-call(bf16[8,2,512,512]{3,2,1,0:T(8,128)(2,1)S(1)} %bitcast.28, bf16[2,512,512]{2,1,0:T(8,128)(2,1)S(1)} %bitcast.40, f32[2,8,512]{2,1,0:T(8,128)S(1)} %get-tuple-element.108.masked_ref, f32[512,128]{1,0:T(8,128)S(1)} %get-tuple-element.109.turned_ref), custom_call_target="tpu_custom_call" | custom-call | flops 12845056 | bytes 1835008 | tf_op jit(solution)/shard_map/part0/pallas_call | solution.py:288
  11.8 1.3 %collective-permute-start.1 = (f32[2,8,512]{2,1,0:T(8,128)S(1)}, f32[2,8,512]{2,1,0:T(8,128)S(1)}, u32[]{:S(2)}, u32[]{:S(2)}) collective-permute-start(f32[2,8,512]{2,1,0:T(8,128)S(1)} %multiply_add_fusion.3), channel_id=1, source_target_pairs={{0,16},{8,24},{16,0},{24,8},{1,17},{9,25},{17,1},{25,9},{2,18},{10... | collective-permute-start | bytes 98312 | tf_op jit(solution)/shard_map/ppermute | solution.py:36
  13.1 2.1 %part1.2.refs_1_ = f32[112,128]{1,0:T(8,128)S(1)} custom-call(bf16[8,2,512,512]{3,2,1,0:T(8,128)(2,1)S(1)} %bitcast.29, bf16[2,512,512]{2,1,0:T(8,128)(2,1)S(1)} %bitcast.41, f32[2,8,512]{2,1,0:T(8,128)S(1)} %get-tuple-element.108.masked_ref, f32[512,128]{1,0:T(8,128)S(1)} %get-tuple-element.109.turned_ref), custom_call_target="tpu_custom_call" | custom-call | flops 12845056 | bytes 1835008 | tf_op jit(solution)/shard_map/part1/pallas_call | solution.py:288
  15.2 2.4 %collective-permute-start.2 = (f32[2,8,512]{2,1,0:T(8,128)S(1)}, f32[2,8,512]{2,1,0:T(8,128)S(1)}, u32[]{:S(2)}, u32[]{:S(2)}) collective-permute-start(f32[2,8,512]{2,1,0:T(8,128)S(1)} %add_add_fusion.1.refs_9_), channel_id=1, source_target_pairs={{0,4},{1,5},{2,6},{3,7},{4,0},{5,1},{6,2},{7,3},{8,12},{9,13},{10,... | collective-permute-start | bytes 98312 | tf_op jit(solution)/shard_map/ppermute | solution.py:36
  17.6 2.2 %part2.2.refs_2_ = f32[128,128]{1,0:T(8,128)S(1)} custom-call(bf16[8,2,512,512]{3,2,1,0:T(8,128)(2,1)S(1)} %bitcast.30, bf16[2,512,512]{2,1,0:T(8,128)(2,1)S(1)} %bitcast.42, f32[2,8,512]{2,1,0:T(8,128)S(1)} %get-tuple-element.108.masked_ref, f32[512,128]{1,0:T(8,128)S(1)} %get-tuple-element.109.turned_ref), custom_call_target="tpu_custom_call" | custom-call | flops 14680064 | bytes 2097152 | tf_op jit(solution)/shard_map/part2/pallas_call | solution.py:288
  19.9 0.0 copy-start.4
  19.9 0.0 slice-start
  19.9 1.4 %collective-permute-start.3 = (f32[2,2,8,512]{3,2,1,0:T(8,128)S(1)}, f32[2,2,8,512]{3,2,1,0:T(8,128)S(1)}, u32[]{:S(2)}, u32[]{:S(2)}) collective-permute-start(f32[2,2,8,512]{3,2,1,0:T(8,128)S(1)} %pad_maximum_fusion), channel_id=1, source_target_pairs={{0,2},{1,3},{2,0},{3,1},{4,6},{5,7},{6,4},{7,5},{8,10},{9,11},{10,... | collective-permute-start | bytes 196616 | tf_op jit(solution)/shard_map/ppermute | solution.py:36
  21.3 2.1 %part3.2.refs_3_ = f32[112,128]{1,0:T(8,128)S(1)} custom-call(bf16[8,2,512,512]{3,2,1,0:T(8,128)(2,1)S(1)} %bitcast.31, bf16[2,512,512]{2,1,0:T(8,128)(2,1)S(1)} %bitcast.43, f32[2,8,512]{2,1,0:T(8,128)S(1)} %get-tuple-element.108.masked_ref, f32[512,128]{1,0:T(8,128)S(1)} %get-tuple-element.109.turned_ref), custom_call_target="tpu_custom_call" | custom-call | flops 12845056 | bytes 1835008 | tf_op jit(solution)/shard_map/part3/pallas_call | solution.py:288
  23.4 2.7 %collective-permute-start.4 = (f32[2,8,512]{2,1,0:T(8,128)S(1)}, f32[2,8,512]{2,1,0:T(8,128)S(1)}, u32[]{:S(2)}, u32[]{:S(2)}) collective-permute-start(f32[2,8,512]{2,1,0:T(8,128)S(1)} %multiply_add_fusion.2), channel_id=1, source_target_pairs={{0,1},{1,0},{2,3},{3,2},{4,5},{5,4},{6,7},{7,6},{8,9},{9,8},{10,11... | collective-permute-start | bytes 98312 | tf_op jit(solution)/shard_map/ppermute | solution.py:36
  26.2 1.0 %part4.2.refs_4_ = f32[48,128]{1,0:T(8,128)S(1)} custom-call(bf16[8,2,512,512]{3,2,1,0:T(8,128)(2,1)S(1)} %bitcast.32, bf16[2,512,512]{2,1,0:T(8,128)(2,1)S(1)} %bitcast.44, f32[2,8,512]{2,1,0:T(8,128)S(1)} %get-tuple-element.108.masked_ref, f32[512,128]{1,0:T(8,128)S(1)} %get-tuple-element.109.turned_ref), custom_call_target="tpu_custom_call" | custom-call | flops 5505024 | bytes 786432 | tf_op jit(solution)/shard_map/part4/pallas_call | solution.py:288
  27.1 0.2 update.1
  27.4 0.3 collective-permute-start.5
  27.7 0.6 %slice-done.1 = s8[4194304]{0:T(1024)(128)(4,1)S(1)} async-done(((s8[8388608]{0:T(1024)(128)(4,1)}), s8[4194304]{0:T(1024)(128)(4,1)S(1)}, s32[]{:S(2)}) %slice-start.1) | async-done | bytes 4194328
  28.3 2.1 %part0.3.refs_0_ = f32[112,128]{1,0:T(8,128)S(1)} custom-call(bf16[8,2,512,512]{3,2,1,0:T(8,128)(2,1)S(1)} %bitcast.35, bf16[2,512,512]{2,1,0:T(8,128)(2,1)S(1)} %bitcast.45, f32[2,8,512]{2,1,0:T(8,128)S(1)} %get-tuple-element.141.masked_ref, f32[512,128]{1,0:T(8,128)S(1)} %get-tuple-element.142.turned_ref), custom_call_target="tpu_custom_call" | custom-call | flops 12845056 | bytes 1835008 | tf_op jit(solution)/shard_map/part0/pallas_call | solution.py:288
  30.5 1.3 %collective-permute-start.6 = (f32[2,8,512]{2,1,0:T(8,128)S(1)}, f32[2,8,512]{2,1,0:T(8,128)S(1)}, u32[]{:S(2)}, u32[]{:S(2)}) collective-permute-start(f32[2,8,512]{2,1,0:T(8,128)S(1)} %multiply_add_fusion.1), channel_id=1, source_target_pairs={{0,16},{8,24},{16,0},{24,8},{1,17},{9,25},{17,1},{25,9},{2,18},{10... | collective-permute-start | bytes 98312 | tf_op jit(solution)/shard_map/ppermute | solution.py:36
  31.8 2.1 %part1.3.refs_1_ = f32[112,128]{1,0:T(8,128)S(1)} custom-call(bf16[8,2,512,512]{3,2,1,0:T(8,128)(2,1)S(1)} %bitcast.36, bf16[2,512,512]{2,1,0:T(8,128)(2,1)S(1)} %bitcast.46, f32[2,8,512]{2,1,0:T(8,128)S(1)} %get-tuple-element.141.masked_ref, f32[512,128]{1,0:T(8,128)S(1)} %get-tuple-element.142.turned_ref), custom_call_target="tpu_custom_call" | custom-call | flops 12845056 | bytes 1835008 | tf_op jit(solution)/shard_map/part1/pallas_call | solution.py:288
  33.9 2.3 %collective-permute-start.7 = (f32[2,8,512]{2,1,0:T(8,128)S(1)}, f32[2,8,512]{2,1,0:T(8,128)S(1)}, u32[]{:S(2)}, u32[]{:S(2)}) collective-permute-start(f32[2,8,512]{2,1,0:T(8,128)S(1)} %add_add_fusion.refs_9_), channel_id=1, source_target_pairs={{0,4},{1,5},{2,6},{3,7},{4,0},{5,1},{6,2},{7,3},{8,12},{9,13},{10,... | collective-permute-start | bytes 98312 | tf_op jit(solution)/shard_map/ppermute | solution.py:36
  36.3 2.2 %part2.3.refs_2_ = f32[128,128]{1,0:T(8,128)S(1)} custom-call(bf16[8,2,512,512]{3,2,1,0:T(8,128)(2,1)S(1)} %bitcast.37, bf16[2,512,512]{2,1,0:T(8,128)(2,1)S(1)} %bitcast.47, f32[2,8,512]{2,1,0:T(8,128)S(1)} %get-tuple-element.141.masked_ref, f32[512,128]{1,0:T(8,128)S(1)} %get-tuple-element.142.turned_ref), custom_call_target="tpu_custom_call" | custom-call | flops 14680064 | bytes 2097152 | tf_op jit(solution)/shard_map/part2/pallas_call | solution.py:288
  38.5 1.6 %collective-permute-start.8 = (f32[2,2,8,512]{3,2,1,0:T(8,128)S(1)}, f32[2,2,8,512]{3,2,1,0:T(8,128)S(1)}, u32[]{:S(2)}, u32[]{:S(2)}) collective-permute-start(f32[2,2,8,512]{3,2,1,0:T(8,128)S(1)} %pad_maximum_fusion.1), channel_id=1, source_target_pairs={{0,2},{1,3},{2,0},{3,1},{4,6},{5,7},{6,4},{7,5},{8,10},{9,11},{10,... | collective-permute-start | bytes 196616 | tf_op jit(solution)/shard_map/ppermute | solution.py:36
  40.1 2.1 %part3.3.refs_3_ = f32[112,128]{1,0:T(8,128)S(1)} custom-call(bf16[8,2,512,512]{3,2,1,0:T(8,128)(2,1)S(1)} %bitcast.38, bf16[2,512,512]{2,1,0:T(8,128)(2,1)S(1)} %bitcast.48, f32[2,8,512]{2,1,0:T(8,128)S(1)} %get-tuple-element.141.masked_ref, f32[512,128]{1,0:T(8,128)S(1)} %get-tuple-element.142.turned_ref), custom_call_target="tpu_custom_call" | custom-call | flops 12845056 | bytes 1835008 | tf_op jit(solution)/shard_map/part3/pallas_call | solution.py:288
  42.3 2.6 %collective-permute-start.9 = (f32[2,8,512]{2,1,0:T(8,128)S(1)}, f32[2,8,512]{2,1,0:T(8,128)S(1)}, u32[]{:S(2)}, u32[]{:S(2)}) collective-permute-start(f32[2,8,512]{2,1,0:T(8,128)S(1)} %multiply_add_fusion), channel_id=1, source_target_pairs={{0,1},{1,0},{2,3},{3,2},{4,5},{5,4},{6,7},{7,6},{8,9},{9,8},{10,11... | collective-permute-start | bytes 98312 | tf_op jit(solution)/shard_map/ppermute | solution.py:36
  44.9 1.0 %part4.3.refs_4_ = f32[48,128]{1,0:T(8,128)S(1)} custom-call(bf16[8,2,512,512]{3,2,1,0:T(8,128)(2,1)S(1)} %bitcast.39, bf16[2,512,512]{2,1,0:T(8,128)(2,1)S(1)} %bitcast.49, f32[2,8,512]{2,1,0:T(8,128)S(1)} %get-tuple-element.141.masked_ref, f32[512,128]{1,0:T(8,128)S(1)} %get-tuple-element.142.turned_ref), custom_call_target="tpu_custom_call" | custom-call | flops 5505024 | bytes 786432 | tf_op jit(solution)/shard_map/part4/pallas_call | solution.py:288
  45.9 0.7 %finish.1 = (f32[2,8,512]{2,1,0:T(8,128)}, f32[2,8,512]{2,1,0:T(8,128)}, f32[2,8,512]{2,1,0:T(8,128)}) custom-call(f32[112,128]{1,0:T(8,128)S(1)} %part0.3.refs_0_, f32[112,128]{1,0:T(8,128)S(1)} %part1.3.refs_1_, f32[128,128]{1,0:T(8,128)S(1)} %part2.3.refs_2_, f32[112,128]{1,0:T(8,128)S(1)} %part3.3.refs_3_, f32[48,128]{1,0:T(8,128)S(1)} %part4.3.refs_4_, ...), custom_call_target="tpu_custom_call" | custom-call | tf_op jit(solution)/shard_map/finish/pallas_call | solution.py:314
  (30 shorter events, 0.2 us)
Async XLA Ops:
  0.6 0.8 %copy-start.3 = (f32[1,1,2,8,512]{4,3,2,1,0:T(8,128)S(1)}, f32[1,1,2,8,512]{4,3,2,1,0:T(8,128)}, u32[]{:S(2)}) copy-start(f32[1,1,2,8,512]{4,3,2,1,0:T(8,128)} %param.8) | copy-start | bytes 98308
  1.4 0.8 %copy-start.5 = (f32[1,1,2,8,512]{4,3,2,1,0:T(8,128)S(1)}, f32[1,1,2,8,512]{4,3,2,1,0:T(8,128)}, u32[]{:S(2)}) copy-start(f32[1,1,2,8,512]{4,3,2,1,0:T(8,128)} %param.9) | copy-start | bytes 98308
  2.1 0.7 %copy-start.6 = (s32[1,1,512]{2,1,0:T(1,128)S(1)}, s32[1,1,512]{2,1,0:T(1,128)}, u32[]{:S(2)}) copy-start(s32[1,1,512]{2,1,0:T(1,128)} %param.7) | copy-start | bytes 6148
  3.0 8.8 %collective-permute-start = (f32[2,8,512]{2,1,0:T(8,128)S(1)}, f32[2,8,512]{2,1,0:T(8,128)S(1)}, u32[]{:S(2)}, u32[]{:S(2)}) collective-permute-start(f32[2,8,512]{2,1,0:T(8,128)S(1)} %get-tuple-element.79.refs_14_), channel_id=1, source_target_pairs={{0,8},{8,0},{16,24},{24,16},{1,9},{9,1},{17,25},{25,17},{2,10},{10... | collective-permute-start | bytes 98312 | tf_op jit(solution)/shard_map/ppermute | solution.py:36
  5.1 3.4 %copy-start = (bf16[1,8,2,512,512]{4,3,2,1,0:T(8,128)(2,1)S(1)}, bf16[1,8,2,512,512]{4,3,2,1,0:T(8,128)(2,1)}, u32[]{:S(2)}) copy-start(bf16[1,8,2,512,512]{4,3,2,1,0:T(8,128)(2,1)} %param.6) | copy-start | bytes 25165828
  8.5 1.2 %copy-start.1 = (bf16[1,1,2,512,512]{4,3,2,1,0:T(8,128)(2,1)S(1)}, bf16[1,1,2,512,512]{4,3,2,1,0:T(8,128)(2,1)}, u32[]{:S(2)}) copy-start(bf16[1,1,2,512,512]{4,3,2,1,0:T(8,128)(2,1)} %param.5) | copy-start | bytes 3145732
  11.8 3.4 %collective-permute-start.1 = (f32[2,8,512]{2,1,0:T(8,128)S(1)}, f32[2,8,512]{2,1,0:T(8,128)S(1)}, u32[]{:S(2)}, u32[]{:S(2)}) collective-permute-start(f32[2,8,512]{2,1,0:T(8,128)S(1)} %multiply_add_fusion.3), channel_id=1, source_target_pairs={{0,16},{8,24},{16,0},{24,8},{1,17},{9,25},{17,1},{25,9},{2,18},{10... | collective-permute-start | bytes 98312 | tf_op jit(solution)/shard_map/ppermute | solution.py:36
  15.2 4.6 %collective-permute-start.2 = (f32[2,8,512]{2,1,0:T(8,128)S(1)}, f32[2,8,512]{2,1,0:T(8,128)S(1)}, u32[]{:S(2)}, u32[]{:S(2)}) collective-permute-start(f32[2,8,512]{2,1,0:T(8,128)S(1)} %add_add_fusion.1.refs_9_), channel_id=1, source_target_pairs={{0,4},{1,5},{2,6},{3,7},{4,0},{5,1},{6,2},{7,3},{8,12},{9,13},{10,... | collective-permute-start | bytes 98312 | tf_op jit(solution)/shard_map/ppermute | solution.py:36
  19.9 7.2 %copy-start.4 = (f32[1,1,2,8,512]{4,3,2,1,0:T(8,128)S(1)}, f32[1,1,2,8,512]{4,3,2,1,0:T(8,128)}, u32[]{:S(2)}) copy-start(f32[1,1,2,8,512]{4,3,2,1,0:T(8,128)} %param.8) | copy-start | bytes 98308
  19.9 7.8 %slice-start = ((s8[8388608]{0:T(1024)(128)(4,1)}), s8[4194304]{0:T(1024)(128)(4,1)S(1)}, s32[]{:S(2)}) async-start(s8[8388608]{0:T(1024)(128)(4,1)} %bitcast.33), calls=%async_computation | async-start | bytes 8388608
  19.9 7.8 %copy-start.2 = (bf16[1,1,2,512,512]{4,3,2,1,0:T(8,128)(2,1)S(1)}, bf16[1,1,2,512,512]{4,3,2,1,0:T(8,128)(2,1)}, u32[]{:S(2)}) copy-start(bf16[1,1,2,512,512]{4,3,2,1,0:T(8,128)(2,1)} %param.5) | copy-start | bytes 3145732
  19.9 3.5 %collective-permute-start.3 = (f32[2,2,8,512]{3,2,1,0:T(8,128)S(1)}, f32[2,2,8,512]{3,2,1,0:T(8,128)S(1)}, u32[]{:S(2)}, u32[]{:S(2)}) collective-permute-start(f32[2,2,8,512]{3,2,1,0:T(8,128)S(1)} %pad_maximum_fusion), channel_id=1, source_target_pairs={{0,2},{1,3},{2,0},{3,1},{4,6},{5,7},{6,4},{7,5},{8,10},{9,11},{10,... | collective-permute-start | bytes 196616 | tf_op jit(solution)/shard_map/ppermute | solution.py:36
  23.4 3.7 %collective-permute-start.4 = (f32[2,8,512]{2,1,0:T(8,128)S(1)}, f32[2,8,512]{2,1,0:T(8,128)S(1)}, u32[]{:S(2)}, u32[]{:S(2)}) collective-permute-start(f32[2,8,512]{2,1,0:T(8,128)S(1)} %multiply_add_fusion.2), channel_id=1, source_target_pairs={{0,1},{1,0},{2,3},{3,2},{4,5},{5,4},{6,7},{7,6},{8,9},{9,8},{10,11... | collective-permute-start | bytes 98312 | tf_op jit(solution)/shard_map/ppermute | solution.py:36
  26.2 2.2 %slice-start.1 = ((s8[8388608]{0:T(1024)(128)(4,1)}), s8[4194304]{0:T(1024)(128)(4,1)S(1)}, s32[]{:S(2)}) async-start(s8[8388608]{0:T(1024)(128)(4,1)} %bitcast.33), calls=%async_computation.1 | async-start | bytes 8388608
  27.4 3.1 %collective-permute-start.5 = (f32[2,8,512]{2,1,0:T(8,128)S(1)}, f32[2,8,512]{2,1,0:T(8,128)S(1)}, u32[]{:S(2)}, u32[]{:S(2)}) collective-permute-start(f32[2,8,512]{2,1,0:T(8,128)S(1)} %get-tuple-element.120.refs_14_), channel_id=1, source_target_pairs={{0,8},{8,0},{16,24},{24,16},{1,9},{9,1},{17,25},{25,17},{2,10},{10... | collective-permute-start | bytes 98312 | tf_op jit(solution)/shard_map/ppermute | solution.py:36
  30.5 3.4 %collective-permute-start.6 = (f32[2,8,512]{2,1,0:T(8,128)S(1)}, f32[2,8,512]{2,1,0:T(8,128)S(1)}, u32[]{:S(2)}, u32[]{:S(2)}) collective-permute-start(f32[2,8,512]{2,1,0:T(8,128)S(1)} %multiply_add_fusion.1), channel_id=1, source_target_pairs={{0,16},{8,24},{16,0},{24,8},{1,17},{9,25},{17,1},{25,9},{2,18},{10... | collective-permute-start | bytes 98312 | tf_op jit(solution)/shard_map/ppermute | solution.py:36
  33.9 4.6 %collective-permute-start.7 = (f32[2,8,512]{2,1,0:T(8,128)S(1)}, f32[2,8,512]{2,1,0:T(8,128)S(1)}, u32[]{:S(2)}, u32[]{:S(2)}) collective-permute-start(f32[2,8,512]{2,1,0:T(8,128)S(1)} %add_add_fusion.refs_9_), channel_id=1, source_target_pairs={{0,4},{1,5},{2,6},{3,7},{4,0},{5,1},{6,2},{7,3},{8,12},{9,13},{10,... | collective-permute-start | bytes 98312 | tf_op jit(solution)/shard_map/ppermute | solution.py:36
  38.5 3.7 %collective-permute-start.8 = (f32[2,2,8,512]{3,2,1,0:T(8,128)S(1)}, f32[2,2,8,512]{3,2,1,0:T(8,128)S(1)}, u32[]{:S(2)}, u32[]{:S(2)}) collective-permute-start(f32[2,2,8,512]{3,2,1,0:T(8,128)S(1)} %pad_maximum_fusion.1), channel_id=1, source_target_pairs={{0,2},{1,3},{2,0},{3,1},{4,6},{5,7},{6,4},{7,5},{8,10},{9,11},{10,... | collective-permute-start | bytes 196616 | tf_op jit(solution)/shard_map/ppermute | solution.py:36
  42.3 3.6 %collective-permute-start.9 = (f32[2,8,512]{2,1,0:T(8,128)S(1)}, f32[2,8,512]{2,1,0:T(8,128)S(1)}, u32[]{:S(2)}, u32[]{:S(2)}) collective-permute-start(f32[2,8,512]{2,1,0:T(8,128)S(1)} %multiply_add_fusion), channel_id=1, source_target_pairs={{0,1},{1,0},{2,3},{3,2},{4,5},{5,4},{6,7},{7,6},{8,9},{9,8},{10,11... | collective-permute-start | bytes 98312 | tf_op jit(solution)/shard_map/ppermute | solution.py:36

commit v2 on v0

v2 whole, which is shorter than its diff:
```python
import functools
import math

import jax
import jax.numpy as jnp
from jax import lax
from jax.experimental import pallas as pl
from jax.experimental.pallas import tpu as pltpu
from jax.sharding import PartitionSpec as P

LANES = 128
ROWS = 16
FREQ_ORDERS = 3
TIME_ORDERS = 2
MIB = 2**20

penalty = 1.0
f32 = jnp.float32


def poly_basis(length, position, order_count):
    centre = position - (length - 1) / 2.0
    linear = centre * (1.0 / math.sqrt(length * (length * length - 1) / 12.0))
    stacked = [jnp.ones_like(position) * (1.0 / math.sqrt(length)), linear]
    if order_count == 3:
        scale = math.sqrt(length * (length * length - 1) * (length * length - 4) / 180.0)
        stacked.append((centre * centre - (length * length - 1) / 12.0) * (1.0 / scale))
    return stacked


def whole_vmem(count):
    return [pl.BlockSpec(memory_space=pltpu.VMEM)] * count


def exchange(array, axis, distance):
    size = lax.axis_size(axis)
    return lax.ppermute(array, axis, [(place, place ^ distance) for place in range(size)])


def time_plan(distances):
    steps = []
    held, sums = 1, False
    for at in range(len(distances)):
        last = at == len(distances) - 1
        turn = not last and not sums and 2 * held > TIME_ORDERS and at < len(distances) - 2
        steps.append((held, sums, turn))
        if turn:
            held, sums = TIME_ORDERS, True
        elif not sums:
            held = 2 * held
    return steps


def time_weights(size, distances, index):
    weights = []

    def basis(place):
        return poly_basis(size, lax.convert_element_type(place, f32), TIME_ORDERS)

    def product(one, other):
        return sum(a * b for a, b in zip(basis(one), basis(other)))

    raw = [index]
    for at, (held, sums, turn) in enumerate(time_plan(distances)):
        if at == len(distances) - 1:
            for target in (index ^ distances[at], index):
                weights += basis(target) if sums else [product(target, place) for place in raw]
        elif not sums:
            raw = raw + [place ^ distances[at] for place in raw]
            if turn:
                for place in raw:
                    weights += basis(place)
    return weights


def time_weight_count(distances):
    total, raw = 0, 1
    for at, (held, sums, turn) in enumerate(time_plan(distances)):
        if at == len(distances) - 1:
            total += 2 * held
        elif not sums:
            raw = 2 * raw
            total += raw * TIME_ORDERS if turn else 0
    return total


def time_exchange(state, distances, weights, work):
    weights = list(weights)
    held = [state]
    for at, (_, sums, turn) in enumerate(time_plan(distances)):
        if at == len(distances) - 1:
            away, own = weights[: len(held)], weights[len(held) :]
            got = work(at, sum(w * a for w, a in zip(away, held)), distances[at])
            return held, own, got
        message = held[0] if len(held) == 1 else jnp.stack(held)
        got = work(at, message, distances[at])
        got = [got] if len(held) == 1 else [got[i] for i in range(len(held))]
        if sums:
            held = [a + b for a, b in zip(held, got)]
            continue
        held = held + got
        if turn:
            taken, weights = weights[: len(held) * TIME_ORDERS], weights[len(held) * TIME_ORDERS :]
            held = [sum(taken[i * TIME_ORDERS + j] * a for i, a in enumerate(held)) for j in range(TIME_ORDERS)]


def freq_gather(state):
    size = lax.axis_size("freq")
    if size <= 4:
        return [state] + [exchange(state, "freq", distance) for distance in range(1, size)]
    distance = 1
    while distance < size:
        state = jnp.concatenate([state, exchange(state, "freq", distance)], axis=0)
        distance *= 2
    return [state]


def turn(gains):
    flat = gains.reshape(-1, gains.shape[-1])
    padded = jnp.concatenate([flat, jnp.zeros((LANES - flat.shape[0], flat.shape[1]), f32)], axis=0)
    return padded.T


def sum_rows(rows, model_ref, vis_ref, masked_ref, turned_ref):
    directions, receptors = model_ref.shape[0], model_ref.shape[3]
    turned = turned_ref[rows, :]
    near = [jnp.broadcast_to(turned[:, k : k + 1], (ROWS, LANES)) for k in range(2 * directions)]
    near_sum = [near[k] + near[directions + k] for k in range(directions)]
    near_gap = [near[directions + k] - near[k] for k in range(directions)]
    sums = [None] * (3 * directions)
    shared = [None] * directions

    def add(total, term):
        return term if total is None else total + term

    for block in range(receptors // LANES):
        columns = pl.ds(block * LANES, LANES)
        moved = []
        whole = by_imag = by_real = None
        for k in range(directions):
            model_real = model_ref[k, 0, rows, columns].astype(f32)
            model_imag = model_ref[k, 1, rows, columns].astype(f32)
            gain_real = masked_ref[0, k : k + 1, columns]
            gain_imag = masked_ref[1, k : k + 1, columns]
            real = model_real * gain_real + model_imag * gain_imag
            imag = model_imag * gain_real - model_real * gain_imag
            both = real + imag
            moved.append((real, imag, both))
            whole = add(whole, near[k] * both)
            by_imag = add(by_imag, imag * near_sum[k])
            by_real = add(by_real, real * near_gap[k])
        resid_real = vis_ref[0, rows, columns].astype(f32) - (whole - by_imag)
        resid_imag = vis_ref[1, rows, columns].astype(f32) - (whole + by_real)
        resid_sum = resid_imag + resid_real
        resid_gap = resid_imag - resid_real
        for k, (real, imag, both) in enumerate(moved):
            shared[k] = add(shared[k], resid_real * both)
            sums[k] = add(sums[k], imag * resid_gap)
            sums[directions + k] = add(sums[directions + k], real * resid_sum)
            sums[2 * directions + k] = add(sums[2 * directions + k], real * real + imag * imag)
    for k in range(directions):
        sums[k] = sums[k] + shared[k]
        sums[directions + k] = sums[directions + k] - shared[k]
    lane = lax.broadcasted_iota(jnp.int32, (ROWS, LANES), 1)
    out = jnp.zeros((ROWS, LANES), f32)
    for place, total in enumerate(sums):
        out = jnp.where(lane == place, jnp.sum(total, axis=1, keepdims=True), out)
    return out


def sum_range(start, count, unroll, sums_ref, model_ref, vis_ref, masked_ref, turned_ref, offset=0):
    def step(at, carry):
        first = pl.multiple_of(at * ROWS, ROWS)
        rows = pl.ds(pl.multiple_of(start + first, ROWS), ROWS)
        sums_ref[pl.ds(pl.multiple_of(offset + first, ROWS), ROWS), :] = sum_rows(rows, model_ref, vis_ref, masked_ref, turned_ref)
        return carry

    lax.fori_loop(0, count // ROWS, step, 0, unroll=unroll)


def part_kernel(start, unroll, model_ref, vis_ref, masked_ref, turned_ref, sums_ref):
    sum_range(start, sums_ref.shape[0], unroll, sums_ref, model_ref, vis_ref, masked_ref, turned_ref)


def begin_kernel(plan, chunks, unroll, gains_in, duals_in, flags_in, model_in, vis_in, *refs):
    gains_ref, merged_ref, masked_ref, turned_ref, mask_ref, model_ref, vis_ref, sums_ref = refs[:8]
    *weight_refs, duals_ref, flags_ref, sems = refs[8:]

    def copy(at, source, target):
        return pltpu.make_async_copy(source, target, sems.at[at])

    small = [copy(0, gains_in, gains_ref), copy(1, duals_in, duals_ref), copy(2, flags_in, flags_ref)]
    large = []
    for at, (first, length) in enumerate(chunks):
        rows = pl.ds(first, length)
        large.append(
            (
                copy(3 + 2 * at, model_in.at[:, :, rows, :], model_ref.at[:, :, rows, :]),
                copy(4 + 2 * at, vis_in.at[:, rows, :], vis_ref.at[:, rows, :]),
            )
        )
    for one in small:
        one.start()
    for pair in large:
        for one in pair:
            one.start()

    axis, size, distances = plan
    index = jnp.full((8, LANES), lax.axis_index(axis), jnp.int32)
    for ref, weight in zip(weight_refs, time_weights(size, distances, index)):
        ref[...] = jnp.broadcast_to(jnp.tile(weight, (ref.shape[1] // 8, ref.shape[2] // LANES))[None], ref.shape)

    for one in small:
        one.wait()
    gains = gains_ref[...]
    mask = flags_ref[...].astype(f32)
    mask_ref[...] = mask
    merged_ref[...] = gains + duals_ref[...]
    masked_ref[...] = gains * mask[None]
    turned_ref[...] = turn(gains)

    for (first, length), pair in zip(chunks, large):
        for one in pair:
            one.wait()
        if first < sums_ref.shape[0]:
            sum_range(first, length, unroll, sums_ref, model_ref, vis_ref, masked_ref, turned_ref, offset=first)


def transposed_sums(refs):
    return jnp.concatenate([ref[...] for ref in refs], axis=0).T


def projected(weight_refs, held_refs, got_ref):
    total = got_ref[...]
    for weight_ref, held_ref in zip(weight_refs, held_refs):
        total = total + weight_ref[...] * held_ref[...]
    return total


def middle_kernel(parts, terms, *refs):
    sums_refs, weight_refs, held_refs = refs[:parts], refs[parts : parts + terms], refs[parts + terms : parts + 2 * terms]
    got_ref, merged_ref, gains_ref, mask_ref, out_ref = refs[parts + 2 * terms :]
    sums = transposed_sums(sums_refs)
    mask = mask_ref[...]
    directions = gains_ref.shape[1]
    curvature = sums[2 * directions : 3 * directions] * mask
    inverse = 1.0 / (curvature + penalty)
    along_time = projected(weight_refs, held_refs, got_ref)
    for part in range(2):
        numer = sums[part * directions : (part + 1) * directions] * mask
        fixed = numer + curvature * gains_ref[part] - penalty * merged_ref[part]
        out_ref[0, part] = along_time[part]
        out_ref[0, 2 + part] = fixed * inverse
    out_ref[0, 4] = (2.0 * penalty) * inverse


def update_kernel(size, *refs):
    *gathered, merged_ref, mask_ref, gains_ref, duals_ref, along_ref, masked_ref, turned_ref = refs
    rows, lanes = merged_ref.shape[1:]
    index = lax.axis_index("freq")
    held, bases = [], []
    for ref in gathered:
        for at in range(ref.shape[0]):
            held.append((ref, at))
            place = jnp.full((8, LANES), index ^ (len(held) - 1), jnp.int32).astype(f32)
            basis = poly_basis(size, place, FREQ_ORDERS)
            bases.append([jnp.tile(weight, (rows // 8, lanes // LANES)) for weight in basis])
    gains, duals, along = [], [], []
    for part in range(2):
        values = [ref[at, part] for ref, at in held]
        coeffs = [sum(basis[i] * value for basis, value in zip(bases, values)) for i in range(FREQ_ORDERS)]
        solved = []
        for (ref, at), basis in zip(held, bases):
            consensus = sum(weight * coeff for weight, coeff in zip(basis, coeffs))
            if not solved:
                duals.append(merged_ref[part] - consensus)
            solved.append(ref[at, 2 + part] + ref[at, 4] * consensus)
        coeffs = [sum(basis[i] * value for basis, value in zip(bases, solved)) for i in range(FREQ_ORDERS)]
        gains.append(solved[0])
        along.append(sum(weight * coeff for weight, coeff in zip(bases[0], coeffs)))
    gains = jnp.stack(gains)
    gains_ref[...] = gains
    duals_ref[...] = jnp.stack(duals)
    along_ref[...] = jnp.stack(along)
    masked_ref[...] = gains * mask_ref[...][None]
    turned_ref[...] = turn(gains)


def finish_kernel(parts, terms, *refs):
    sums_refs, weight_refs, held_refs = refs[:parts], refs[parts : parts + terms], refs[parts + terms : parts + 2 * terms]
    got_ref, gains_ref, duals_ref, mask_ref, solved_ref, consensus_ref, final_ref = refs[parts + 2 * terms :]
    sums = transposed_sums(sums_refs)
    gains = gains_ref[...]
    mask = mask_ref[...]
    directions = gains.shape[1]
    consensus = projected(weight_refs, held_refs, got_ref)
    duals = duals_ref[...] + gains - consensus
    target = consensus - duals
    curvature = sums[2 * directions : 3 * directions] * mask
    divisor = curvature + penalty
    for part in range(2):
        numer = sums[part * directions : (part + 1) * directions] * mask
        solved_ref[part] = (numer + curvature * gains[part] + penalty * target[part]) / divisor
    consensus_ref[...] = consensus
    final_ref[...] = duals


def cut(total, shares):
    ends, done = [0], 0.0
    for share in shares:
        done += share
        ends.append(round(total * done / sum(shares)))
    return [(a, b - a) for a, b in zip(ends, ends[1:])]


def per_device(visibilities, model_vis, station_flags, initial_gains, initial_duals):
    vis_block = visibilities[0, 0]
    model_block = model_vis[0]
    flag_block = station_flags[0]
    _, directions, receptors = initial_gains.shape[2:]
    state = jax.ShapeDtypeStruct((2, directions, receptors), f32)
    turned_shape = jax.ShapeDtypeStruct((receptors, LANES), f32)
    pairs = directions * receptors

    freq_count, time_count = lax.axis_size("freq"), lax.axis_size("tm")
    distances = [1 << b for b in reversed(range(time_count.bit_length() - 1))]
    steps = len(distances)
    units = receptors // ROWS

    def sums_shape(length):
        return jax.ShapeDtypeStruct((length, LANES), f32)

    def cost(length):
        return pl.CostEstimate(flops=28 * pairs * length, bytes_accessed=4 * pairs * length, transcendentals=0)

    first, *beside = [(ROWS * a, ROWS * n) for a, n in cut(units, [11.0] + [9.0] * (steps - 1) + [4.0])]
    chunks = [(ROWS * a, ROWS * n) for a, n in cut(first[1] // ROWS, [1.0, 2.0, 2.0, 2.0]) if n]
    rest = receptors - first[1]
    chunks += [(first[1] + ROWS * a, ROWS * n) for a, n in cut(rest // ROWS, [1.0, 1.0])]
    gains, merged, masked, turned, mask, model_near, vis_near, sums, *weights = pl.pallas_call(
        functools.partial(begin_kernel, ("tm", time_count, distances), chunks, True),
        out_shape=[state] * 3
        + [
            turned_shape,
            jax.ShapeDtypeStruct((1, receptors), f32),
            jax.ShapeDtypeStruct(model_block.shape, model_block.dtype),
            jax.ShapeDtypeStruct(vis_block.shape, vis_block.dtype),
            sums_shape(first[1]),
        ]
        + [state] * time_weight_count(distances),
        in_specs=[pl.BlockSpec(memory_space=pltpu.HBM)] * 5,
        out_specs=whole_vmem(8 + time_weight_count(distances)),
        scratch_shapes=[
            pltpu.VMEM(state.shape, f32),
            pltpu.VMEM((1, receptors), jnp.int32),
            pltpu.SemaphoreType.DMA((3 + 2 * len(chunks),)),
        ],
        compiler_params=pltpu.CompilerParams(vmem_limit_bytes=32 * MIB),
        cost_estimate=cost(first[1]),
        name="begin",
    )(initial_gains[0, 0], initial_duals[0, 0], flag_block, model_block, vis_block)
    sums = [sums]

    def part(name, start, length, masked, turned):
        return pl.pallas_call(
            functools.partial(part_kernel, start, True),
            out_shape=sums_shape(length),
            in_specs=whole_vmem(4),
            out_specs=pl.BlockSpec(memory_space=pltpu.VMEM),
            compiler_params=pltpu.CompilerParams(vmem_limit_bytes=32 * MIB),
            cost_estimate=cost(length),
            name=name,
        )(model_near, vis_near, masked, turned)

    def worker(name, ranges, results, masked, turned):
        def work(at, message, distance):
            message, one, two = lax.optimization_barrier((message, masked, turned))
            got = exchange(message, "tm", distance)
            result = part(f"{name}{at}", *ranges[at], one, two)
            got, result = lax.optimization_barrier((got, result))
            results.append(result)
            return got

        return work

    def small_kernel(kernel, name, operands, outs):
        return pl.pallas_call(
            kernel,
            out_shape=outs,
            in_specs=whole_vmem(len(operands)),
            out_specs=whole_vmem(len(outs)),
            compiler_params=pltpu.CompilerParams(vmem_limit_bytes=16 * MIB),
            name=name,
        )(*operands)

    held, own, got = time_exchange(merged, distances, weights, worker("first", beside, sums, masked, turned))
    operands = sums + own + held + [got, merged, gains, mask]
    (payload,) = small_kernel(
        functools.partial(middle_kernel, len(sums), len(held)),
        "middle",
        operands,
        [jax.ShapeDtypeStruct((1, 5, directions, receptors), f32)],
    )
    gathered = freq_gather(payload)
    gains, duals, along_freq, masked, turned = small_kernel(
        functools.partial(update_kernel, freq_count),
        "update",
        gathered + [merged, mask],
        [state] * 4 + [turned_shape],
    )

    beside = [(ROWS * a, ROWS * n) for a, n in cut(units, [11.0] * (steps - 1) + [10.0])]
    sums = []
    held, own, got = time_exchange(along_freq, distances, weights, worker("second", beside, sums, masked, turned))
    operands = sums + own + held + [got, gains, duals, mask]
    outputs = small_kernel(functools.partial(finish_kernel, len(sums), len(held)), "finish", operands, [state] * 3)
    return tuple(out[None, None] for out in outputs)


def solution(mesh):
    in_specs = (
        P("freq", "tm", None, None, None),
        P("freq", None, None, None, None),
        P("freq", "tm", None),
        P("freq", "tm", None, None, None),
        P("freq", "tm", None, None, None),
    )
    out_specs = (
        P("freq", "tm", None, None, None),
        P("freq", "tm", None, None, None),
        P("freq", "tm", None, None, None),
    )
    return jax.shard_map(
        per_device, mesh=mesh, in_specs=in_specs, out_specs=out_specs, check_vma=False
    )
```

time: 220 us -> 46.7 us (0.21)
  waiting for transfers between devices: 110 us -> 4.18 us
  blocking collectives: 46.1 us -> 0 us
  other arithmetic: 40.5 us -> 0.06 us
  Pallas kernels: 0 us -> 19.2 us
  starting transfers between devices: 0.16 us -> 15.3 us
  between operations: 14.1 us -> 0.75 us
    unnamed x6 -> x0, waiting for transfers between devices: 82.5 us -> none
    all_gather x4 -> x0, blocking collectives: 46.1 us -> none  [the longest x2 33.9 us: polynomial_fit(): time_whole = lax.all_gather(time_values, 'tm', axis=1, tiled=True)]
    reduce_sum x8 -> x0, other arithmetic: 36.1 us -> none  [the longest x2 21.5 us: local_solve(): jnp.sum(resid_real[None] * proj_real - resid_imag[None] * proj_imag, axis=2)]
    reduce_scatter x2 -> x0, waiting for transfers between devices: 27.9 us -> none  [polynomial_fit(): lax.psum_scatter(both_terms, 'freq', scatter_dimension=1, tiled=True)]
    pallas_call x0 -> x10, Pallas kernels: none -> 19.2 us  [the longest x6 13.7 us: part(): pl.pallas_call(functools.partial(part_kernel, start, True), out_shape=sum...]
    ppermute x0 -> x9, starting transfers between devices: none -> 15.3 us  [exchange(): lax.ppermute(array, axis, [(place, place ^ distance) for place in range(s...]
    ppermute x0 -> x9, waiting for transfers between devices: none -> 4.18 us  [exchange(): lax.ppermute(array, axis, [(place, place ^ distance) for place in range(s...]
    mul x8 -> x0, other arithmetic: 2.2 us -> none  [the longest x2 1.37 us: polynomial_fit(): freq_basis[:, None, None] * time_part[None]]
  transfers between devices with their start and end apart: 4 -> 9, of which waited for: 4 -> 3; matrix products, arithmetic and copies ran while one was open for 17% -> 0% of each run, Pallas kernels for 0% -> 30%
where the time goes in v2:
time: 46.7 us; the launch traced here: 46.3 us
  Pallas kernels  19.2 us (41%)
  starting transfers between devices  15.3 us (33%)
  local copies, waits for them, and re-layouts  6.81 us (15%)
  waiting for transfers between devices  4.18 us (9%)
  between operations  0.75 us (2%)
    ppermute x9, starting transfers between devices, exchange(): lax.ppermute(array, axis, [(place, place ^ distance) for place in range(s...  15.3 us
    pallas_call x6, Pallas kernels, part(): pl.pallas_call(functools.partial(part_kernel, start, True), out_shape=sum...  13.7 us
    unnamed x10, local copies, waits for them, and re-layouts  6.79 us
    pallas_call x1, Pallas kernels, per_device(): pl.pallas_call(functools.partial(begin_kernel, ('tm', time_count, distanc...  4.38 us
    ppermute x9, waiting for transfers between devices, exchange(): lax.ppermute(array, axis, [(place, place ^ distance) for place in range(s...  4.18 us
    pallas_call x3, Pallas kernels, small_kernel(): pl.pallas_call(kernel, out_shape=outs, in_specs=whole_vmem(len(operands))...  1.06 us
  transfers between devices with their start and end apart: 9, of which 3 were waited for; matrix products, arithmetic and copies ran while one was open for 0% of the time, Pallas kernels for 30%

profile of v2, /device:TPU:1, one launch (start us, length us, event | category | flops | bytes accessed | tf_op | source)
XLA Modules:
  0.0 46.3 jit_solution(14238285144427968862)
XLA Ops:
  0.6 3.4 %copy-done = bf16[1,8,2,512,512]{4,3,2,1,0:T(8,128)(2,1)S(1)} copy-done((bf16[1,8,2,512,512]{4,3,2,1,0:T(8,128)(2,1)S(1)}, bf16[1,8,2,512,512]{4,3,2,1,0:T(8,128)(2,1)}, u32[]{:S(2)}) %copy-start) | copy-done | bytes 8388632
  4.0 1.2 %copy-done.1 = bf16[1,1,2,512,512]{4,3,2,1,0:T(8,128)(2,1)S(1)} copy-done((bf16[1,1,2,512,512]{4,3,2,1,0:T(8,128)(2,1)S(1)}, bf16[1,1,2,512,512]{4,3,2,1,0:T(8,128)(2,1)}, u32[]{:S(2)}) %copy-start.1) | copy-done | bytes 1048600
  5.2 0.8 %copy-done.2 = f32[1,1,2,8,512]{4,3,2,1,0:T(8,128)S(1)} copy-done((f32[1,1,2,8,512]{4,3,2,1,0:T(8,128)S(1)}, f32[1,1,2,8,512]{4,3,2,1,0:T(8,128)}, u32[]{:S(2)}) %copy-start.2) | copy-done | bytes 32792
  6.0 0.8 %copy-done.3 = f32[1,1,2,8,512]{4,3,2,1,0:T(8,128)S(1)} copy-done((f32[1,1,2,8,512]{4,3,2,1,0:T(8,128)S(1)}, f32[1,1,2,8,512]{4,3,2,1,0:T(8,128)}, u32[]{:S(2)}) %copy-start.3) | copy-done | bytes 32792
  6.8 0.7 %copy-done.4 = s32[1,1,512]{2,1,0:T(1,128)S(1)} copy-done((s32[1,1,512]{2,1,0:T(1,128)S(1)}, s32[1,1,512]{2,1,0:T(1,128)}, u32[]{:S(2)}) %copy-start.4) | copy-done | bytes 2072
  7.4 4.4 %begin.1 = (f32[2,8,512]{2,1,0:T(8,128)S(1)}, f32[2,8,512]{2,1,0:T(8,128)S(1)}, f32[2,8,512]{2,1,0:T(8,128)S(1)}, f32[512,128]{1,0:T(8,128)S(1)}, f32[1,512]{1,0...) custom-call(f32[2,8,512]{2,1,0:T(8,128)S(1)} %bitcast.34, ...), custom_call_target="tpu_custom_call" | custom-call | flops 20185088 | bytes 2883584 | tf_op jit(solution)/shard_map/begin/pallas_call | solution.py:340
  11.8 3.2 %collective-permute-start = (f32[2,8,512]{2,1,0:T(8,128)S(1)}, f32[2,8,512]{2,1,0:T(8,128)S(1)}, u32[]{:S(2)}, u32[]{:S(2)}) collective-permute-start(f32[2,8,512]{2,1,0:T(8,128)S(1)} %get-tuple-element.61.refs_8_.refs_13_.refs_4_), channel_id=1, source_target_pairs={{0,4},{1,5},{2,6},{3,7},{4,0},{5,1},{6,2},{7,3},{8,12},{9,13},{10,... | collective-permute-start | bytes 98312 | tf_op jit(solution)/shard_map/ppermute | solution.py:37
  15.0 2.0 %first0.1.refs_1_ = f32[128,128]{1,0:T(8,128)S(1)} custom-call(bf16[8,2,512,512]{3,2,1,0:T(8,128)(2,1)S(1)} %get-tuple-element.62.model_ref, bf16[2,512,512]{2,1,0:T(8,128)(2,1)S(1)} %get-tuple-element.63.vis_ref, f32[2,8,512]{2,1,0:T(8,128)S(1)} %get-tuple-element.78.masked_ref, f32[512,128]{1,0:T(8,128)S(1)} %get-tuple-element.79.turned_ref), custom_call_target="tpu_custom_call" | custom-call | flops 14680064 | bytes 2097152 | tf_op jit(solution)/shard_map/first0/pallas_call | solution.py:365
  17.1 0.0 collective-permute-done.refs_9_
  17.1 1.4 %collective-permute-start.1 = (f32[2,2,8,512]{3,2,1,0:T(8,128)S(1)}, f32[2,2,8,512]{3,2,1,0:T(8,128)S(1)}, u32[]{:S(2)}, u32[]{:S(2)}) collective-permute-start(f32[2,2,8,512]{3,2,1,0:T(8,128)S(1)} %pad_maximum_fusion), channel_id=1, source_target_pairs={{0,2},{1,3},{2,0},{3,1},{4,6},{5,7},{6,4},{7,5},{8,10},{9,11},{10,... | collective-permute-start | bytes 196616 | tf_op jit(solution)/shard_map/ppermute | solution.py:37
  18.5 2.3 %first1.1.refs_2_ = f32[144,128]{1,0:T(8,128)S(1)} custom-call(bf16[8,2,512,512]{3,2,1,0:T(8,128)(2,1)S(1)} %get-tuple-element.62.model_ref, bf16[2,512,512]{2,1,0:T(8,128)(2,1)S(1)} %get-tuple-element.63.vis_ref, f32[2,8,512]{2,1,0:T(8,128)S(1)} %get-tuple-element.78.masked_ref, f32[512,128]{1,0:T(8,128)S(1)} %get-tuple-element.79.turned_ref), custom_call_target="tpu_custom_call" | custom-call | flops 16515072 | bytes 2359296 | tf_op jit(solution)/shard_map/first1/pallas_call | solution.py:365
  20.8 0.0 collective-permute-done.1
  20.8 1.8 %collective-permute-start.2 = (f32[2,8,512]{2,1,0:T(8,128)S(1)}, f32[2,8,512]{2,1,0:T(8,128)S(1)}, u32[]{:S(2)}, u32[]{:S(2)}) collective-permute-start(f32[2,8,512]{2,1,0:T(8,128)S(1)} %multiply_add_fusion.1), channel_id=1, source_target_pairs={{0,1},{1,0},{2,3},{3,2},{4,5},{5,4},{6,7},{7,6},{8,9},{9,8},{10,11... | collective-permute-start | bytes 98312 | tf_op jit(solution)/shard_map/ppermute | solution.py:37
  22.6 1.1 %first2.1.refs_3_ = f32[64,128]{1,0:T(8,128)S(1)} custom-call(bf16[8,2,512,512]{3,2,1,0:T(8,128)(2,1)S(1)} %get-tuple-element.62.model_ref, bf16[2,512,512]{2,1,0:T(8,128)(2,1)S(1)} %get-tuple-element.63.vis_ref, f32[2,8,512]{2,1,0:T(8,128)S(1)} %get-tuple-element.78.masked_ref, f32[512,128]{1,0:T(8,128)S(1)} %get-tuple-element.79.turned_ref), custom_call_target="tpu_custom_call" | custom-call | flops 7340032 | bytes 1048576 | tf_op jit(solution)/shard_map/first2/pallas_call | solution.py:365
  23.7 0.0 collective-permute-done.2.refs_12_
  23.7 0.1 middle.1.refs_0_
  23.8 1.5 %collective-permute-start.3 = (f32[1,5,8,512]{3,2,1,0:T(8,128)S(1)}, f32[1,5,8,512]{3,2,1,0:T(8,128)S(1)}, u32[]{:S(2)}, u32[]{:S(2)}) collective-permute-start(f32[1,5,8,512]{3,2,1,0:T(8,128)S(1)} %middle.1.refs_0_), channel_id=1, source_target_pairs={{0,8},{8,0},{16,24},{24,16},{1,9},{9,1},{17,25},{25,17},{2,10},{10... | collective-permute-start | bytes 245768 | tf_op jit(solution)/shard_map/ppermute | solution.py:37
  25.3 1.2 %collective-permute-start.4 = (f32[1,5,8,512]{3,2,1,0:T(8,128)S(1)}, f32[1,5,8,512]{3,2,1,0:T(8,128)S(1)}, u32[]{:S(2)}, u32[]{:S(2)}) collective-permute-start(f32[1,5,8,512]{3,2,1,0:T(8,128)S(1)} %middle.1.refs_0_), channel_id=1, source_target_pairs={{0,16},{8,24},{16,0},{24,8},{1,17},{9,25},{17,1},{25,9},{2,18},{10... | collective-permute-start | bytes 245768 | tf_op jit(solution)/shard_map/ppermute | solution.py:37
  26.5 0.0 collective-permute-start.5
  26.5 1.2 %collective-permute-done.3.refs_1_ = f32[1,5,8,512]{3,2,1,0:T(8,128)S(1)} collective-permute-done((f32[1,5,8,512]{3,2,1,0:T(8,128)S(1)}, f32[1,5,8,512]{3,2,1,0:T(8,128)S(1)}, u32[]{:S(2)}, u32[]{:S(2)}) %collective-permute-start.3) | collective-permute-done | bytes 81952 | tf_op jit(solution)/shard_map/ppermute | solution.py:37
  27.8 0.8 %collective-permute-done.4.refs_2_ = f32[1,5,8,512]{3,2,1,0:T(8,128)S(1)} collective-permute-done((f32[1,5,8,512]{3,2,1,0:T(8,128)S(1)}, f32[1,5,8,512]{3,2,1,0:T(8,128)S(1)}, u32[]{:S(2)}, u32[]{:S(2)}) %collective-permute-start.4) | collective-permute-done | bytes 81952 | tf_op jit(solution)/shard_map/ppermute | solution.py:37
  28.6 2.1 %collective-permute-done.5.refs_3_ = f32[1,5,8,512]{3,2,1,0:T(8,128)S(1)} collective-permute-done((f32[1,5,8,512]{3,2,1,0:T(8,128)S(1)}, f32[1,5,8,512]{3,2,1,0:T(8,128)S(1)}, u32[]{:S(2)}, u32[]{:S(2)}) %collective-permute-start.5) | collective-permute-done | bytes 81952 | tf_op jit(solution)/shard_map/ppermute | solution.py:37
  30.7 0.2 update.1
  30.9 2.2 %collective-permute-start.6 = (f32[2,8,512]{2,1,0:T(8,128)S(1)}, f32[2,8,512]{2,1,0:T(8,128)S(1)}, u32[]{:S(2)}, u32[]{:S(2)}) collective-permute-start(f32[2,8,512]{2,1,0:T(8,128)S(1)} %get-tuple-element.91.refs_7_), channel_id=1, source_target_pairs={{0,4},{1,5},{2,6},{3,7},{4,0},{5,1},{6,2},{7,3},{8,12},{9,13},{10,... | collective-permute-start | bytes 98312 | tf_op jit(solution)/shard_map/ppermute | solution.py:37
  33.1 3.0 %second0.1.refs_0_ = f32[176,128]{1,0:T(8,128)S(1)} custom-call(bf16[8,2,512,512]{3,2,1,0:T(8,128)(2,1)S(1)} %get-tuple-element.62.model_ref, bf16[2,512,512]{2,1,0:T(8,128)(2,1)S(1)} %get-tuple-element.63.vis_ref, f32[2,8,512]{2,1,0:T(8,128)S(1)} %get-tuple-element.102.masked_ref, f32[512,128]{1,0:T(8,128)S(1)} %get-tuple-element.103.turned_ref), custom_call_target="tpu_custom_call" | custom-call | flops 20185088 | bytes 2883584 | tf_op jit(solution)/shard_map/second0/pallas_call | solution.py:365
  36.1 0.0 collective-permute-done.6.refs_8_
  36.1 1.6 %collective-permute-start.7 = (f32[2,2,8,512]{3,2,1,0:T(8,128)S(1)}, f32[2,2,8,512]{3,2,1,0:T(8,128)S(1)}, u32[]{:S(2)}, u32[]{:S(2)}) collective-permute-start(f32[2,2,8,512]{3,2,1,0:T(8,128)S(1)} %pad_maximum_fusion.1), channel_id=1, source_target_pairs={{0,2},{1,3},{2,0},{3,1},{4,6},{5,7},{6,4},{7,5},{8,10},{9,11},{10,... | collective-permute-start | bytes 196616 | tf_op jit(solution)/shard_map/ppermute | solution.py:37
  37.7 2.8 %second1.1.refs_1_ = f32[176,128]{1,0:T(8,128)S(1)} custom-call(bf16[8,2,512,512]{3,2,1,0:T(8,128)(2,1)S(1)} %get-tuple-element.62.model_ref, bf16[2,512,512]{2,1,0:T(8,128)(2,1)S(1)} %get-tuple-element.63.vis_ref, f32[2,8,512]{2,1,0:T(8,128)S(1)} %get-tuple-element.102.masked_ref, f32[512,128]{1,0:T(8,128)S(1)} %get-tuple-element.103.turned_ref), custom_call_target="tpu_custom_call" | custom-call | flops 20185088 | bytes 2883584 | tf_op jit(solution)/shard_map/second1/pallas_call | solution.py:365
  40.5 2.5 %collective-permute-start.8 = (f32[2,8,512]{2,1,0:T(8,128)S(1)}, f32[2,8,512]{2,1,0:T(8,128)S(1)}, u32[]{:S(2)}, u32[]{:S(2)}) collective-permute-start(f32[2,8,512]{2,1,0:T(8,128)S(1)} %multiply_add_fusion), channel_id=1, source_target_pairs={{0,1},{1,0},{2,3},{3,2},{4,5},{5,4},{6,7},{7,6},{8,9},{9,8},{10,11... | collective-permute-start | bytes 98312 | tf_op jit(solution)/shard_map/ppermute | solution.py:37
  43.0 2.5 %second2.1.refs_2_ = f32[160,128]{1,0:T(8,128)S(1)} custom-call(bf16[8,2,512,512]{3,2,1,0:T(8,128)(2,1)S(1)} %get-tuple-element.62.model_ref, bf16[2,512,512]{2,1,0:T(8,128)(2,1)S(1)} %get-tuple-element.63.vis_ref, f32[2,8,512]{2,1,0:T(8,128)S(1)} %get-tuple-element.102.masked_ref, f32[512,128]{1,0:T(8,128)S(1)} %get-tuple-element.103.turned_ref), custom_call_target="tpu_custom_call" | custom-call | flops 18350080 | bytes 2621440 | tf_op jit(solution)/shard_map/second2/pallas_call | solution.py:365
  45.5 0.0 collective-permute-done.8.refs_11_
  45.6 0.7 %finish.1 = (f32[2,8,512]{2,1,0:T(8,128)}, f32[2,8,512]{2,1,0:T(8,128)}, f32[2,8,512]{2,1,0:T(8,128)}) custom-call(f32[176,128]{1,0:T(8,128)S(1)} %second0.1.refs_0_, f32[176,128]{1,0:T(8,128)S(1)} %second1.1.refs_1_, f32[160,128]{1,0:T(8,128)S(1)} %second2.1.refs_2_, f32[2,8,512]{2,1,0:T(8,128)S(1)} %get-tuple-element.81.refs_4_.refs_3_, ...), custom_call_target="tpu_custom_call" | custom-call | tf_op jit(solution)/shard_map/finish/pallas_call | solution.py:387
  (12 shorter events, 0.1 us)
Async XLA Ops:
  0.6 3.4 %copy-start = (bf16[1,8,2,512,512]{4,3,2,1,0:T(8,128)(2,1)S(1)}, bf16[1,8,2,512,512]{4,3,2,1,0:T(8,128)(2,1)}, u32[]{:S(2)}) copy-start(bf16[1,8,2,512,512]{4,3,2,1,0:T(8,128)(2,1)} %param.6) | copy-start | bytes 25165828
  4.0 1.2 %copy-start.1 = (bf16[1,1,2,512,512]{4,3,2,1,0:T(8,128)(2,1)S(1)}, bf16[1,1,2,512,512]{4,3,2,1,0:T(8,128)(2,1)}, u32[]{:S(2)}) copy-start(bf16[1,1,2,512,512]{4,3,2,1,0:T(8,128)(2,1)} %param.5) | copy-start | bytes 3145732
  5.2 0.8 %copy-start.2 = (f32[1,1,2,8,512]{4,3,2,1,0:T(8,128)S(1)}, f32[1,1,2,8,512]{4,3,2,1,0:T(8,128)}, u32[]{:S(2)}) copy-start(f32[1,1,2,8,512]{4,3,2,1,0:T(8,128)} %param.8) | copy-start | bytes 98308
  6.0 0.8 %copy-start.3 = (f32[1,1,2,8,512]{4,3,2,1,0:T(8,128)S(1)}, f32[1,1,2,8,512]{4,3,2,1,0:T(8,128)}, u32[]{:S(2)}) copy-start(f32[1,1,2,8,512]{4,3,2,1,0:T(8,128)} %param.9) | copy-start | bytes 98308
  6.8 0.7 %copy-start.4 = (s32[1,1,512]{2,1,0:T(1,128)S(1)}, s32[1,1,512]{2,1,0:T(1,128)}, u32[]{:S(2)}) copy-start(s32[1,1,512]{2,1,0:T(1,128)} %param.7) | copy-start | bytes 6148
  11.8 5.3 %collective-permute-start = (f32[2,8,512]{2,1,0:T(8,128)S(1)}, f32[2,8,512]{2,1,0:T(8,128)S(1)}, u32[]{:S(2)}, u32[]{:S(2)}) collective-permute-start(f32[2,8,512]{2,1,0:T(8,128)S(1)} %get-tuple-element.61.refs_8_.refs_13_.refs_4_), channel_id=1, source_target_pairs={{0,4},{1,5},{2,6},{3,7},{4,0},{5,1},{6,2},{7,3},{8,12},{9,13},{10,... | collective-permute-start | bytes 98312 | tf_op jit(solution)/shard_map/ppermute | solution.py:37
  17.1 3.7 %collective-permute-start.1 = (f32[2,2,8,512]{3,2,1,0:T(8,128)S(1)}, f32[2,2,8,512]{3,2,1,0:T(8,128)S(1)}, u32[]{:S(2)}, u32[]{:S(2)}) collective-permute-start(f32[2,2,8,512]{3,2,1,0:T(8,128)S(1)} %pad_maximum_fusion), channel_id=1, source_target_pairs={{0,2},{1,3},{2,0},{3,1},{4,6},{5,7},{6,4},{7,5},{8,10},{9,11},{10,... | collective-permute-start | bytes 196616 | tf_op jit(solution)/shard_map/ppermute | solution.py:37
  20.8 2.9 %collective-permute-start.2 = (f32[2,8,512]{2,1,0:T(8,128)S(1)}, f32[2,8,512]{2,1,0:T(8,128)S(1)}, u32[]{:S(2)}, u32[]{:S(2)}) collective-permute-start(f32[2,8,512]{2,1,0:T(8,128)S(1)} %multiply_add_fusion.1), channel_id=1, source_target_pairs={{0,1},{1,0},{2,3},{3,2},{4,5},{5,4},{6,7},{7,6},{8,9},{9,8},{10,11... | collective-permute-start | bytes 98312 | tf_op jit(solution)/shard_map/ppermute | solution.py:37
  23.8 4.0 %collective-permute-start.3 = (f32[1,5,8,512]{3,2,1,0:T(8,128)S(1)}, f32[1,5,8,512]{3,2,1,0:T(8,128)S(1)}, u32[]{:S(2)}, u32[]{:S(2)}) collective-permute-start(f32[1,5,8,512]{3,2,1,0:T(8,128)S(1)} %middle.1.refs_0_), channel_id=1, source_target_pairs={{0,8},{8,0},{16,24},{24,16},{1,9},{9,1},{17,25},{25,17},{2,10},{10... | collective-permute-start | bytes 245768 | tf_op jit(solution)/shard_map/ppermute | solution.py:37
  25.3 3.3 %collective-permute-start.4 = (f32[1,5,8,512]{3,2,1,0:T(8,128)S(1)}, f32[1,5,8,512]{3,2,1,0:T(8,128)S(1)}, u32[]{:S(2)}, u32[]{:S(2)}) collective-permute-start(f32[1,5,8,512]{3,2,1,0:T(8,128)S(1)} %middle.1.refs_0_), channel_id=1, source_target_pairs={{0,16},{8,24},{16,0},{24,8},{1,17},{9,25},{17,1},{25,9},{2,18},{10... | collective-permute-start | bytes 245768 | tf_op jit(solution)/shard_map/ppermute | solution.py:37
  26.5 4.2 %collective-permute-start.5 = (f32[1,5,8,512]{3,2,1,0:T(8,128)S(1)}, f32[1,5,8,512]{3,2,1,0:T(8,128)S(1)}, u32[]{:S(2)}, u32[]{:S(2)}) collective-permute-start(f32[1,5,8,512]{3,2,1,0:T(8,128)S(1)} %middle.1.refs_0_), channel_id=1, source_target_pairs={{0,24},{8,16},{16,8},{24,0},{1,25},{9,17},{17,9},{25,1},{2,26},{10... | collective-permute-start | bytes 245768 | tf_op jit(solution)/shard_map/ppermute | solution.py:37
  30.9 5.2 %collective-permute-start.6 = (f32[2,8,512]{2,1,0:T(8,128)S(1)}, f32[2,8,512]{2,1,0:T(8,128)S(1)}, u32[]{:S(2)}, u32[]{:S(2)}) collective-permute-start(f32[2,8,512]{2,1,0:T(8,128)S(1)} %get-tuple-element.91.refs_7_), channel_id=1, source_target_pairs={{0,4},{1,5},{2,6},{3,7},{4,0},{5,1},{6,2},{7,3},{8,12},{9,13},{10,... | collective-permute-start | bytes 98312 | tf_op jit(solution)/shard_map/ppermute | solution.py:37
  36.1 4.4 %collective-permute-start.7 = (f32[2,2,8,512]{3,2,1,0:T(8,128)S(1)}, f32[2,2,8,512]{3,2,1,0:T(8,128)S(1)}, u32[]{:S(2)}, u32[]{:S(2)}) collective-permute-start(f32[2,2,8,512]{3,2,1,0:T(8,128)S(1)} %pad_maximum_fusion.1), channel_id=1, source_target_pairs={{0,2},{1,3},{2,0},{3,1},{4,6},{5,7},{6,4},{7,5},{8,10},{9,11},{10,... | collective-permute-start | bytes 196616 | tf_op jit(solution)/shard_map/ppermute | solution.py:37
  40.5 5.0 %collective-permute-start.8 = (f32[2,8,512]{2,1,0:T(8,128)S(1)}, f32[2,8,512]{2,1,0:T(8,128)S(1)}, u32[]{:S(2)}, u32[]{:S(2)}) collective-permute-start(f32[2,8,512]{2,1,0:T(8,128)S(1)} %multiply_add_fusion), channel_id=1, source_target_pairs={{0,1},{1,0},{2,3},{3,2},{4,5},{5,4},{6,7},{7,6},{8,9},{9,8},{10,11... | collective-permute-start | bytes 98312 | tf_op jit(solution)/shard_map/ppermute | solution.py:37

commit v3 on v2

--- a/solution.py
+++ b/solution.py
@@ -182,48 +182,24 @@
     sum_range(start, sums_ref.shape[0], unroll, sums_ref, model_ref, vis_ref, masked_ref, turned_ref)
 
 
-def begin_kernel(plan, chunks, unroll, gains_in, duals_in, flags_in, model_in, vis_in, *refs):
-    gains_ref, merged_ref, masked_ref, turned_ref, mask_ref, model_ref, vis_ref, sums_ref = refs[:8]
-    *weight_refs, duals_ref, flags_ref, sems = refs[8:]
-
-    def copy(at, source, target):
-        return pltpu.make_async_copy(source, target, sems.at[at])
-
-    small = [copy(0, gains_in, gains_ref), copy(1, duals_in, duals_ref), copy(2, flags_in, flags_ref)]
-    large = []
-    for at, (first, length) in enumerate(chunks):
-        rows = pl.ds(first, length)
-        large.append(
-            (
-                copy(3 + 2 * at, model_in.at[:, :, rows, :], model_ref.at[:, :, rows, :]),
-                copy(4 + 2 * at, vis_in.at[:, rows, :], vis_ref.at[:, rows, :]),
-            )
-        )
-    for one in small:
-        one.start()
-    for pair in large:
-        for one in pair:
-            one.start()
-
+def setup_kernel(plan, gains_in, duals_in, flags_in, gains_ref, merged_ref, masked_ref, turned_ref, mask_ref, *refs):
+    *weight_refs, duals_ref, flags_ref, sems = refs
+    places = ((gains_in, gains_ref), (duals_in, duals_ref), (flags_in, flags_ref))
+    copies = [pltpu.make_async_copy(source, target, sems.at[at]) for at, (source, target) in enumerate(places)]
+    for copy in copies:
+        copy.start()
     axis, size, distances = plan
     index = jnp.full((8, LANES), lax.axis_index(axis), jnp.int32)
     for ref, weight in zip(weight_refs, time_weights(size, distances, index)):
         ref[...] = jnp.broadcast_to(jnp.tile(weight, (ref.shape[1] // 8, ref.shape[2] // LANES))[None], ref.shape)
-
-    for one in small:
-        one.wait()
+    for copy in copies:
+        copy.wait()
     gains = gains_ref[...]
     mask = flags_ref[...].astype(f32)
     mask_ref[...] = mask
     merged_ref[...] = gains + duals_ref[...]
     masked_ref[...] = gains * mask[None]
     turned_ref[...] = turn(gains)
-
-    for (first, length), pair in zip(chunks, large):
-        for one in pair:
-            one.wait()
-        if first < sums_ref.shape[0]:
-            sum_range(first, length, unroll, sums_ref, model_ref, vis_ref, masked_ref, turned_ref, offset=first)
 
 
 def transposed_sums(refs):
@@ -316,7 +292,6 @@
 def per_device(visibilities, model_vis, station_flags, initial_gains, initial_duals):
     vis_block = visibilities[0, 0]
     model_block = model_vis[0]
-    flag_block = station_flags[0]
     _, directions, receptors = initial_gains.shape[2:]
     state = jax.ShapeDtypeStruct((2, directions, receptors), f32)
     turned_shape = jax.ShapeDtypeStruct((receptors, LANES), f32)
@@ -333,33 +308,23 @@
     def cost(length):
         return pl.CostEstimate(flops=28 * pairs * length, bytes_accessed=4 * pairs * length, transcendentals=0)
 
-    first, *beside = [(ROWS * a, ROWS * n) for a, n in cut(units, [11.0] + [9.0] * (steps - 1) + [4.0])]
-    chunks = [(ROWS * a, ROWS * n) for a, n in cut(first[1] // ROWS, [1.0, 2.0, 2.0, 2.0]) if n]
-    rest = receptors - first[1]
-    chunks += [(first[1] + ROWS * a, ROWS * n) for a, n in cut(rest // ROWS, [1.0, 1.0])]
-    gains, merged, masked, turned, mask, model_near, vis_near, sums, *weights = pl.pallas_call(
-        functools.partial(begin_kernel, ("tm", time_count, distances), chunks, True),
+    small = [initial_gains[0, 0], initial_duals[0, 0], station_flags[0]]
+    gains, merged, masked, turned, mask, *weights = pl.pallas_call(
+        functools.partial(setup_kernel, ("tm", time_count, distances)),
         out_shape=[state] * 3
-        + [
-            turned_shape,
-            jax.ShapeDtypeStruct((1, receptors), f32),
-            jax.ShapeDtypeStruct(model_block.shape, model_block.dtype),
-            jax.ShapeDtypeStruct(vis_block.shape, vis_block.dtype),
-            sums_shape(first[1]),
-        ]
+        + [turned_shape, jax.ShapeDtypeStruct((1, receptors), f32)]
         + [state] * time_weight_count(distances),
-        in_specs=[pl.BlockSpec(memory_space=pltpu.HBM)] * 5,
-        out_specs=whole_vmem(8 + time_weight_count(distances)),
+        in_specs=[pl.BlockSpec(memory_space=pltpu.HBM)] * 3,
+        out_specs=whole_vmem(5 + time_weight_count(distances)),
         scratch_shapes=[
             pltpu.VMEM(state.shape, f32),
             pltpu.VMEM((1, receptors), jnp.int32),
-            pltpu.SemaphoreType.DMA((3 + 2 * len(chunks),)),
+            pltpu.SemaphoreType.DMA((3,)),
         ],
-        compiler_params=pltpu.CompilerParams(vmem_limit_bytes=32 * MIB),
-        cost_estimate=cost(first[1]),
-        name="begin",
-    )(initial_gains[0, 0], initial_duals[0, 0], flag_block, model_block, vis_block)
-    sums = [sums]
+        compiler_params=pltpu.CompilerParams(vmem_limit_bytes=16 * MIB),
+        cost_estimate=pl.CostEstimate(flops=1 << 36, bytes_accessed=1 << 28, transcendentals=0),
+        name="setup",
+    )(*[pltpu.with_memory_space_constraint(one, pltpu.HBM) for one in small])
 
     def part(name, start, length, masked, turned):
         return pl.pallas_call(
@@ -370,7 +335,7 @@
             compiler_params=pltpu.CompilerParams(vmem_limit_bytes=32 * MIB),
             cost_estimate=cost(length),
             name=name,
-        )(model_near, vis_near, masked, turned)
+        )(model_block, vis_block, masked, turned)
 
     def worker(name, ranges, results, masked, turned):
         def work(at, message, distance):
@@ -393,6 +358,8 @@
             name=name,
         )(*operands)
 
+    beside = [(ROWS * a, ROWS * n) for a, n in cut(units, [11.0] * (steps - 1) + [10.0])]
+    sums = []
     held, own, got = time_exchange(merged, distances, weights, worker("first", beside, sums, masked, turned))
     operands = sums + own + held + [got, merged, gains, mask]
     (payload,) = small_kernel(
@@ -409,7 +376,6 @@
         [state] * 4 + [turned_shape],
     )
 
-    beside = [(ROWS * a, ROWS * n) for a, n in cut(units, [11.0] * (steps - 1) + [10.0])]
     sums = []
     held, own, got = time_exchange(along_freq, distances, weights, worker("second", beside, sums, masked, turned))
     operands = sums + own + held + [got, gains, duals, mask]

time: 46.7 us -> 37.2 us (0.80)
  local copies, waits for them, and re-layouts: 6.81 us -> 0.02 us
  starting transfers between devices: 15.3 us -> 13.4 us
  Pallas kernels: 19.2 us -> 18.6 us
    unnamed x10 -> x4, local copies, waits for them, and re-layouts: 6.79 us -> 0.01 us
    pallas_call x1, Pallas kernels: 4.38 us -> 1.09 us  [per_device(): pl.pallas_call(functools.partial(setup_kernel, ('tm', time_count, distanc...]
    pallas_call x6, Pallas kernels: 13.7 us -> 16.4 us  [part(): pl.pallas_call(functools.partial(part_kernel, start, True), out_shape=sum...]
    ppermute x9, starting transfers between devices: 15.3 us -> 13.4 us  [exchange(): lax.ppermute(array, axis, [(place, place ^ distance) for place in range(s...]
  transfers between devices with their start and end apart: 9 -> 9, of which waited for: 3 -> 2; matrix products, arithmetic and copies ran while one was open for 0% -> 0% of each run, Pallas kernels for 30% -> 44%
where the time goes in v3:
time: 37.2 us; the launch traced here: 37 us
  Pallas kernels  18.6 us (50%)
  starting transfers between devices  13.4 us (36%)
  waiting for transfers between devices  4.21 us (11%)
  between operations  0.75 us (2%)
    pallas_call x6, Pallas kernels, part(): pl.pallas_call(functools.partial(part_kernel, start, True), out_shape=sum...  16.4 us
    ppermute x9, starting transfers between devices, exchange(): lax.ppermute(array, axis, [(place, place ^ distance) for place in range(s...  13.4 us
    ppermute x9, waiting for transfers between devices, exchange(): lax.ppermute(array, axis, [(place, place ^ distance) for place in range(s...  4.21 us
    pallas_call x1, Pallas kernels, per_device(): pl.pallas_call(functools.partial(setup_kernel, ('tm', time_count, distanc...  1.09 us
    pallas_call x3, Pallas kernels, small_kernel(): pl.pallas_call(kernel, out_shape=outs, in_specs=whole_vmem(len(operands))...  1.06 us
  transfers between devices with their start and end apart: 9, of which 2 were waited for; matrix products, arithmetic and copies ran while one was open for 0% of the time, Pallas kernels for 44%

profile of v3, /device:TPU:1, one launch (start us, length us, event | category | flops | bytes accessed | tf_op | source)
XLA Modules:
  0.0 37.0 jit_solution(809622062986032732)
XLA Ops:
  0.6 0.0 copy-start
  0.6 0.0 copy-start.1
  0.7 1.1 %setup.1 = (f32[2,8,512]{2,1,0:T(8,128)S(1)}, f32[2,8,512]{2,1,0:T(8,128)S(1)}, f32[2,8,512]{2,1,0:T(8,128)S(1)}, f32[512,128]{1,0:T(8,128)S(1)}, f32[1,512]{1,0...) custom-call(f32[2,8,512]{2,1,0:T(8,128)} %bitcast.44, ...), custom_call_target="tpu_custom_call" | custom-call | flops 68719476736 | bytes 268435456 | tf_op jit(solution)/shard_map/setup/pallas_call | solution.py:312
  1.7 3.2 %collective-permute-start = (f32[2,8,512]{2,1,0:T(8,128)S(1)}, f32[2,8,512]{2,1,0:T(8,128)S(1)}, u32[]{:S(2)}, u32[]{:S(2)}) collective-permute-start(f32[2,8,512]{2,1,0:T(8,128)S(1)} %get-tuple-element.57.refs_7_.refs_12_.refs_4_), channel_id=1, source_target_pairs={{0,4},{1,5},{2,6},{3,7},{4,0},{5,1},{6,2},{7,3},{8,12},{9,13},{10,... | collective-permute-start | bytes 98312 | tf_op jit(solution)/shard_map/ppermute | solution.py:37
  5.0 0.0 copy-done
  5.0 0.0 copy-done.1
  5.0 2.8 %first0.1.refs_0_ = f32[176,128]{1,0:T(8,128)S(1)} custom-call(bf16[8,2,512,512]{3,2,1,0:T(8,128)(2,1)S(1)} %bitcast.28, bf16[2,512,512]{2,1,0:T(8,128)(2,1)S(1)} %bitcast.34, f32[2,8,512]{2,1,0:T(8,128)S(1)} %get-tuple-element.72.masked_ref, f32[512,128]{1,0:T(8,128)S(1)} %get-tuple-element.73.turned_ref), custom_call_target="tpu_custom_call" | custom-call | flops 20185088 | bytes 2883584 | tf_op jit(solution)/shard_map/first0/pallas_call | solution.py:330
  7.7 0.0 collective-permute-done.refs_8_
  7.8 1.5 %collective-permute-start.1 = (f32[2,2,8,512]{3,2,1,0:T(8,128)S(1)}, f32[2,2,8,512]{3,2,1,0:T(8,128)S(1)}, u32[]{:S(2)}, u32[]{:S(2)}) collective-permute-start(f32[2,2,8,512]{3,2,1,0:T(8,128)S(1)} %pad_maximum_fusion), channel_id=1, source_target_pairs={{0,2},{1,3},{2,0},{3,1},{4,6},{5,7},{6,4},{7,5},{8,10},{9,11},{10,... | collective-permute-start | bytes 196616 | tf_op jit(solution)/shard_map/ppermute | solution.py:37
  9.3 2.8 %first1.1.refs_1_ = f32[176,128]{1,0:T(8,128)S(1)} custom-call(bf16[8,2,512,512]{3,2,1,0:T(8,128)(2,1)S(1)} %bitcast.29, bf16[2,512,512]{2,1,0:T(8,128)(2,1)S(1)} %bitcast.35, f32[2,8,512]{2,1,0:T(8,128)S(1)} %get-tuple-element.72.masked_ref, f32[512,128]{1,0:T(8,128)S(1)} %get-tuple-element.73.turned_ref), custom_call_target="tpu_custom_call" | custom-call | flops 20185088 | bytes 2883584 | tf_op jit(solution)/shard_map/first1/pallas_call | solution.py:330
  12.1 0.0 collective-permute-done.1
  12.1 1.1 %collective-permute-start.2 = (f32[2,8,512]{2,1,0:T(8,128)S(1)}, f32[2,8,512]{2,1,0:T(8,128)S(1)}, u32[]{:S(2)}, u32[]{:S(2)}) collective-permute-start(f32[2,8,512]{2,1,0:T(8,128)S(1)} %multiply_add_fusion.1), channel_id=1, source_target_pairs={{0,1},{1,0},{2,3},{3,2},{4,5},{5,4},{6,7},{7,6},{8,9},{9,8},{10,11... | collective-permute-start | bytes 98312 | tf_op jit(solution)/shard_map/ppermute | solution.py:37
  13.3 2.5 %first2.1.refs_2_ = f32[160,128]{1,0:T(8,128)S(1)} custom-call(bf16[8,2,512,512]{3,2,1,0:T(8,128)(2,1)S(1)} %bitcast.30, bf16[2,512,512]{2,1,0:T(8,128)(2,1)S(1)} %bitcast.36, f32[2,8,512]{2,1,0:T(8,128)S(1)} %get-tuple-element.72.masked_ref, f32[512,128]{1,0:T(8,128)S(1)} %get-tuple-element.73.turned_ref), custom_call_target="tpu_custom_call" | custom-call | flops 18350080 | bytes 2621440 | tf_op jit(solution)/shard_map/first2/pallas_call | solution.py:330
  15.8 0.0 collective-permute-done.2.refs_11_
  15.8 0.1 middle.1.refs_0_
  15.9 2.2 %collective-permute-start.5 = (f32[1,5,8,512]{3,2,1,0:T(8,128)S(1)}, f32[1,5,8,512]{3,2,1,0:T(8,128)S(1)}, u32[]{:S(2)}, u32[]{:S(2)}) collective-permute-start(f32[1,5,8,512]{3,2,1,0:T(8,128)S(1)} %middle.1.refs_0_), channel_id=1, source_target_pairs={{0,24},{8,16},{16,8},{24,0},{1,25},{9,17},{17,9},{25,1},{2,26},{10... | collective-permute-start | bytes 245768 | tf_op jit(solution)/shard_map/ppermute | solution.py:37
  18.2 0.2 collective-permute-start.4
  18.4 0.3 collective-permute-start.3
  18.7 2.3 %collective-permute-done.5.refs_3_ = f32[1,5,8,512]{3,2,1,0:T(8,128)S(1)} collective-permute-done((f32[1,5,8,512]{3,2,1,0:T(8,128)S(1)}, f32[1,5,8,512]{3,2,1,0:T(8,128)S(1)}, u32[]{:S(2)}, u32[]{:S(2)}) %collective-permute-start.5) | collective-permute-done | bytes 81952 | tf_op jit(solution)/shard_map/ppermute | solution.py:37
  21.0 1.9 %collective-permute-done.4.refs_2_ = f32[1,5,8,512]{3,2,1,0:T(8,128)S(1)} collective-permute-done((f32[1,5,8,512]{3,2,1,0:T(8,128)S(1)}, f32[1,5,8,512]{3,2,1,0:T(8,128)S(1)}, u32[]{:S(2)}, u32[]{:S(2)}) %collective-permute-start.4) | collective-permute-done | bytes 81952 | tf_op jit(solution)/shard_map/ppermute | solution.py:37
  22.9 0.0 collective-permute-done.3.refs_1_
  22.9 0.2 update.1
  23.0 2.3 %collective-permute-start.6 = (f32[2,8,512]{2,1,0:T(8,128)S(1)}, f32[2,8,512]{2,1,0:T(8,128)S(1)}, u32[]{:S(2)}, u32[]{:S(2)}) collective-permute-start(f32[2,8,512]{2,1,0:T(8,128)S(1)} %get-tuple-element.85.refs_7_), channel_id=1, source_target_pairs={{0,4},{1,5},{2,6},{3,7},{4,0},{5,1},{6,2},{7,3},{8,12},{9,13},{10,... | collective-permute-start | bytes 98312 | tf_op jit(solution)/shard_map/ppermute | solution.py:37
  25.3 3.0 %second0.1.refs_0_ = f32[176,128]{1,0:T(8,128)S(1)} custom-call(bf16[8,2,512,512]{3,2,1,0:T(8,128)(2,1)S(1)} %bitcast.31, bf16[2,512,512]{2,1,0:T(8,128)(2,1)S(1)} %bitcast.37, f32[2,8,512]{2,1,0:T(8,128)S(1)} %get-tuple-element.96.masked_ref, f32[512,128]{1,0:T(8,128)S(1)} %get-tuple-element.97.turned_ref), custom_call_target="tpu_custom_call" | custom-call | flops 20185088 | bytes 2883584 | tf_op jit(solution)/shard_map/second0/pallas_call | solution.py:330
  28.3 0.0 collective-permute-done.6.refs_8_
  28.3 1.2 %collective-permute-start.7 = (f32[2,2,8,512]{3,2,1,0:T(8,128)S(1)}, f32[2,2,8,512]{3,2,1,0:T(8,128)S(1)}, u32[]{:S(2)}, u32[]{:S(2)}) collective-permute-start(f32[2,2,8,512]{3,2,1,0:T(8,128)S(1)} %pad_maximum_fusion.1), channel_id=1, source_target_pairs={{0,2},{1,3},{2,0},{3,1},{4,6},{5,7},{6,4},{7,5},{8,10},{9,11},{10,... | collective-permute-start | bytes 196616 | tf_op jit(solution)/shard_map/ppermute | solution.py:37
  29.5 2.8 %second1.1.refs_1_ = f32[176,128]{1,0:T(8,128)S(1)} custom-call(bf16[8,2,512,512]{3,2,1,0:T(8,128)(2,1)S(1)} %bitcast.32, bf16[2,512,512]{2,1,0:T(8,128)(2,1)S(1)} %bitcast.38, f32[2,8,512]{2,1,0:T(8,128)S(1)} %get-tuple-element.96.masked_ref, f32[512,128]{1,0:T(8,128)S(1)} %get-tuple-element.97.turned_ref), custom_call_target="tpu_custom_call" | custom-call | flops 20185088 | bytes 2883584 | tf_op jit(solution)/shard_map/second1/pallas_call | solution.py:330
  32.3 0.0 collective-permute-done.7
  32.4 1.4 %collective-permute-start.8 = (f32[2,8,512]{2,1,0:T(8,128)S(1)}, f32[2,8,512]{2,1,0:T(8,128)S(1)}, u32[]{:S(2)}, u32[]{:S(2)}) collective-permute-start(f32[2,8,512]{2,1,0:T(8,128)S(1)} %multiply_add_fusion), channel_id=1, source_target_pairs={{0,1},{1,0},{2,3},{3,2},{4,5},{5,4},{6,7},{7,6},{8,9},{9,8},{10,11... | collective-permute-start | bytes 98312 | tf_op jit(solution)/shard_map/ppermute | solution.py:37
  33.7 2.5 %second2.1.refs_2_ = f32[160,128]{1,0:T(8,128)S(1)} custom-call(bf16[8,2,512,512]{3,2,1,0:T(8,128)(2,1)S(1)} %bitcast.33, bf16[2,512,512]{2,1,0:T(8,128)(2,1)S(1)} %bitcast.39, f32[2,8,512]{2,1,0:T(8,128)S(1)} %get-tuple-element.96.masked_ref, f32[512,128]{1,0:T(8,128)S(1)} %get-tuple-element.97.turned_ref), custom_call_target="tpu_custom_call" | custom-call | flops 18350080 | bytes 2621440 | tf_op jit(solution)/shard_map/second2/pallas_call | solution.py:330
  36.3 0.0 collective-permute-done.8.refs_11_
  36.3 0.7 %finish.1 = (f32[2,8,512]{2,1,0:T(8,128)}, f32[2,8,512]{2,1,0:T(8,128)}, f32[2,8,512]{2,1,0:T(8,128)}) custom-call(f32[176,128]{1,0:T(8,128)S(1)} %second0.1.refs_0_, f32[176,128]{1,0:T(8,128)S(1)} %second1.1.refs_1_, f32[160,128]{1,0:T(8,128)S(1)} %second2.1.refs_2_, f32[2,8,512]{2,1,0:T(8,128)S(1)} %get-tuple-element.75.refs_3_, ...), custom_call_target="tpu_custom_call" | custom-call | tf_op jit(solution)/shard_map/finish/pallas_call | solution.py:352
  (6 shorter events, 0.1 us)
Async XLA Ops:
  0.6 4.3 %copy-start = (bf16[1,8,2,512,512]{4,3,2,1,0:T(8,128)(2,1)S(1)}, bf16[1,8,2,512,512]{4,3,2,1,0:T(8,128)(2,1)}, u32[]{:S(2)}) copy-start(bf16[1,8,2,512,512]{4,3,2,1,0:T(8,128)(2,1)} %param.6) | copy-start | bytes 25165828
  0.6 4.3 %copy-start.1 = (bf16[1,1,2,512,512]{4,3,2,1,0:T(8,128)(2,1)S(1)}, bf16[1,1,2,512,512]{4,3,2,1,0:T(8,128)(2,1)}, u32[]{:S(2)}) copy-start(bf16[1,1,2,512,512]{4,3,2,1,0:T(8,128)(2,1)} %param.5) | copy-start | bytes 3145732
  1.7 6.0 %collective-permute-start = (f32[2,8,512]{2,1,0:T(8,128)S(1)}, f32[2,8,512]{2,1,0:T(8,128)S(1)}, u32[]{:S(2)}, u32[]{:S(2)}) collective-permute-start(f32[2,8,512]{2,1,0:T(8,128)S(1)} %get-tuple-element.57.refs_7_.refs_12_.refs_4_), channel_id=1, source_target_pairs={{0,4},{1,5},{2,6},{3,7},{4,0},{5,1},{6,2},{7,3},{8,12},{9,13},{10,... | collective-permute-start | bytes 98312 | tf_op jit(solution)/shard_map/ppermute | solution.py:37
  7.8 4.3 %collective-permute-start.1 = (f32[2,2,8,512]{3,2,1,0:T(8,128)S(1)}, f32[2,2,8,512]{3,2,1,0:T(8,128)S(1)}, u32[]{:S(2)}, u32[]{:S(2)}) collective-permute-start(f32[2,2,8,512]{3,2,1,0:T(8,128)S(1)} %pad_maximum_fusion), channel_id=1, source_target_pairs={{0,2},{1,3},{2,0},{3,1},{4,6},{5,7},{6,4},{7,5},{8,10},{9,11},{10,... | collective-permute-start | bytes 196616 | tf_op jit(solution)/shard_map/ppermute | solution.py:37
  12.1 3.7 %collective-permute-start.2 = (f32[2,8,512]{2,1,0:T(8,128)S(1)}, f32[2,8,512]{2,1,0:T(8,128)S(1)}, u32[]{:S(2)}, u32[]{:S(2)}) collective-permute-start(f32[2,8,512]{2,1,0:T(8,128)S(1)} %multiply_add_fusion.1), channel_id=1, source_target_pairs={{0,1},{1,0},{2,3},{3,2},{4,5},{5,4},{6,7},{7,6},{8,9},{9,8},{10,11... | collective-permute-start | bytes 98312 | tf_op jit(solution)/shard_map/ppermute | solution.py:37
  15.9 5.0 %collective-permute-start.5 = (f32[1,5,8,512]{3,2,1,0:T(8,128)S(1)}, f32[1,5,8,512]{3,2,1,0:T(8,128)S(1)}, u32[]{:S(2)}, u32[]{:S(2)}) collective-permute-start(f32[1,5,8,512]{3,2,1,0:T(8,128)S(1)} %middle.1.refs_0_), channel_id=1, source_target_pairs={{0,24},{8,16},{16,8},{24,0},{1,25},{9,17},{17,9},{25,1},{2,26},{10... | collective-permute-start | bytes 245768 | tf_op jit(solution)/shard_map/ppermute | solution.py:37
  18.2 4.7 %collective-permute-start.4 = (f32[1,5,8,512]{3,2,1,0:T(8,128)S(1)}, f32[1,5,8,512]{3,2,1,0:T(8,128)S(1)}, u32[]{:S(2)}, u32[]{:S(2)}) collective-permute-start(f32[1,5,8,512]{3,2,1,0:T(8,128)S(1)} %middle.1.refs_0_), channel_id=1, source_target_pairs={{0,16},{8,24},{16,0},{24,8},{1,17},{9,25},{17,1},{25,9},{2,18},{10... | collective-permute-start | bytes 245768 | tf_op jit(solution)/shard_map/ppermute | solution.py:37
  18.4 4.4 %collective-permute-start.3 = (f32[1,5,8,512]{3,2,1,0:T(8,128)S(1)}, f32[1,5,8,512]{3,2,1,0:T(8,128)S(1)}, u32[]{:S(2)}, u32[]{:S(2)}) collective-permute-start(f32[1,5,8,512]{3,2,1,0:T(8,128)S(1)} %middle.1.refs_0_), channel_id=1, source_target_pairs={{0,8},{8,0},{16,24},{24,16},{1,9},{9,1},{17,25},{25,17},{2,10},{10... | collective-permute-start | bytes 245768 | tf_op jit(solution)/shard_map/ppermute | solution.py:37
  23.0 5.2 %collective-permute-start.6 = (f32[2,8,512]{2,1,0:T(8,128)S(1)}, f32[2,8,512]{2,1,0:T(8,128)S(1)}, u32[]{:S(2)}, u32[]{:S(2)}) collective-permute-start(f32[2,8,512]{2,1,0:T(8,128)S(1)} %get-tuple-element.85.refs_7_), channel_id=1, source_target_pairs={{0,4},{1,5},{2,6},{3,7},{4,0},{5,1},{6,2},{7,3},{8,12},{9,13},{10,... | collective-permute-start | bytes 98312 | tf_op jit(solution)/shard_map/ppermute | solution.py:37
  28.3 4.0 %collective-permute-start.7 = (f32[2,2,8,512]{3,2,1,0:T(8,128)S(1)}, f32[2,2,8,512]{3,2,1,0:T(8,128)S(1)}, u32[]{:S(2)}, u32[]{:S(2)}) collective-permute-start(f32[2,2,8,512]{3,2,1,0:T(8,128)S(1)} %pad_maximum_fusion.1), channel_id=1, source_target_pairs={{0,2},{1,3},{2,0},{3,1},{4,6},{5,7},{6,4},{7,5},{8,10},{9,11},{10,... | collective-permute-start | bytes 196616 | tf_op jit(solution)/shard_map/ppermute | solution.py:37
  32.4 3.9 %collective-permute-start.8 = (f32[2,8,512]{2,1,0:T(8,128)S(1)}, f32[2,8,512]{2,1,0:T(8,128)S(1)}, u32[]{:S(2)}, u32[]{:S(2)}) collective-permute-start(f32[2,8,512]{2,1,0:T(8,128)S(1)} %multiply_add_fusion), channel_id=1, source_target_pairs={{0,1},{1,0},{2,3},{3,2},{4,5},{5,4},{6,7},{7,6},{8,9},{9,8},{10,11... | collective-permute-start | bytes 98312 | tf_op jit(solution)/shard_map/ppermute | solution.py:37

commit v4 on v3

--- a/solution.py
+++ b/solution.py
@@ -121,23 +121,23 @@
     return padded.T
 
 
-def sum_rows(rows, model_ref, vis_ref, masked_ref, turned_ref):
-    directions, receptors = model_ref.shape[0], model_ref.shape[3]
+def sum_rows(rows, model_ref, vis_ref, masked_ref, turned_ref, square_ref=None, power_ref=None):
+    directions, blocks = model_ref.shape[0], model_ref.shape[3] // LANES
     turned = turned_ref[rows, :]
-    near = [jnp.broadcast_to(turned[:, k : k + 1], (ROWS, LANES)) for k in range(2 * directions)]
-    near_sum = [near[k] + near[directions + k] for k in range(directions)]
-    near_gap = [near[directions + k] - near[k] for k in range(directions)]
-    sums = [None] * (3 * directions)
-    shared = [None] * directions
+
+    def along_lanes(column):
+        return jnp.take_along_axis(turned, jnp.full((ROWS, LANES), column, jnp.int32), axis=1)
 
     def add(total, term):
         return term if total is None else total + term
 
-    for block in range(receptors // LANES):
-        columns = pl.ds(block * LANES, LANES)
-        moved = []
-        whole = by_imag = by_real = None
-        for k in range(directions):
+    whole, by_imag, by_real = [None] * blocks, [None] * blocks, [None] * blocks
+    moved = {}
+    for k in range(directions):
+        near_real, near_imag = along_lanes(k), along_lanes(directions + k)
+        near_sum, near_gap = near_real + near_imag, near_imag - near_real
+        for block in range(blocks):
+            columns = pl.ds(block * LANES, LANES)
             model_real = model_ref[k, 0, rows, columns].astype(f32)
             model_imag = model_ref[k, 1, rows, columns].astype(f32)
             gain_real = masked_ref[0, k : k + 1, columns]
@@ -145,41 +145,59 @@
             real = model_real * gain_real + model_imag * gain_imag
             imag = model_imag * gain_real - model_real * gain_imag
             both = real + imag
-            moved.append((real, imag, both))
-            whole = add(whole, near[k] * both)
-            by_imag = add(by_imag, imag * near_sum[k])
-            by_real = add(by_real, real * near_gap[k])
-        resid_real = vis_ref[0, rows, columns].astype(f32) - (whole - by_imag)
-        resid_imag = vis_ref[1, rows, columns].astype(f32) - (whole + by_real)
-        resid_sum = resid_imag + resid_real
-        resid_gap = resid_imag - resid_real
-        for k, (real, imag, both) in enumerate(moved):
-            shared[k] = add(shared[k], resid_real * both)
-            sums[k] = add(sums[k], imag * resid_gap)
-            sums[directions + k] = add(sums[directions + k], real * resid_sum)
-            sums[2 * directions + k] = add(sums[2 * directions + k], real * real + imag * imag)
-    for k in range(directions):
-        sums[k] = sums[k] + shared[k]
-        sums[directions + k] = sums[directions + k] - shared[k]
+            moved[k, block] = (real, imag, both)
+            whole[block] = add(whole[block], near_real * both)
+            by_imag[block] = add(by_imag[block], imag * near_sum)
+            by_real[block] = add(by_real[block], real * near_gap)
+    residuals = []
+    for block in range(blocks):
+        columns = pl.ds(block * LANES, LANES)
+        real = vis_ref[0, rows, columns].astype(f32) - (whole[block] - by_imag[block])
+        imag = vis_ref[1, rows, columns].astype(f32) - (whole[block] + by_real[block])
+        residuals.append((real, imag + real, imag - real))
     lane = lax.broadcasted_iota(jnp.int32, (ROWS, LANES), 1)
     out = jnp.zeros((ROWS, LANES), f32)
-    for place, total in enumerate(sums):
-        out = jnp.where(lane == place, jnp.sum(total, axis=1, keepdims=True), out)
+    for k in range(directions):
+        shared = by_gap = by_sum = curvature = None
+        for block in range(blocks):
+            columns = pl.ds(block * LANES, LANES)
+            real, imag, both = moved[k, block]
+            resid_real, resid_sum, resid_gap = residuals[block]
+            shared = add(shared, resid_real * both)
+            by_gap = add(by_gap, imag * resid_gap)
+            by_sum = add(by_sum, real * resid_sum)
+            if square_ref is None:
+                curvature = add(curvature, real * real + imag * imag)
+            else:
+                curvature = add(curvature, square_ref[k, rows, columns] * power_ref[k : k + 1, columns])
+        for kind, total in enumerate((by_gap + shared, by_sum - shared, curvature)):
+            out = jnp.where(lane == kind * directions + k, jnp.sum(total, axis=1, keepdims=True), out)
     return out
 
 
-def sum_range(start, count, unroll, sums_ref, model_ref, vis_ref, masked_ref, turned_ref, offset=0):
+def part_kernel(start, unroll, *refs):
+    *inputs, sums_ref = refs
+
     def step(at, carry):
         first = pl.multiple_of(at * ROWS, ROWS)
         rows = pl.ds(pl.multiple_of(start + first, ROWS), ROWS)
-        sums_ref[pl.ds(pl.multiple_of(offset + first, ROWS), ROWS), :] = sum_rows(rows, model_ref, vis_ref, masked_ref, turned_ref)
+        sums_ref[pl.ds(first, ROWS), :] = sum_rows(rows, *inputs)
         return carry
 
-    lax.fori_loop(0, count // ROWS, step, 0, unroll=unroll)
-
-
-def part_kernel(start, unroll, model_ref, vis_ref, masked_ref, turned_ref, sums_ref):
-    sum_range(start, sums_ref.shape[0], unroll, sums_ref, model_ref, vis_ref, masked_ref, turned_ref)
+    lax.fori_loop(0, sums_ref.shape[0] // ROWS, step, 0, unroll=unroll)
+
+
+def widen_kernel(model_ref, wide_ref, square_ref):
+    def step(at, carry):
+        rows = pl.ds(pl.multiple_of(at * ROWS, ROWS), ROWS)
+        for k in range(model_ref.shape[0]):
+            real, imag = model_ref[k, 0, rows, :].astype(f32), model_ref[k, 1, rows, :].astype(f32)
+            wide_ref[k, 0, rows, :] = real
+            wide_ref[k, 1, rows, :] = imag
+            square_ref[k, rows, :] = real * real + imag * imag
+        return carry
+
+    lax.fori_loop(0, model_ref.shape[2] // ROWS, step, 0, unroll=2)
 
 
 def setup_kernel(plan, gains_in, duals_in, flags_in, gains_ref, merged_ref, masked_ref, turned_ref, mask_ref, *refs):
@@ -231,7 +249,7 @@
 
 
 def update_kernel(size, *refs):
-    *gathered, merged_ref, mask_ref, gains_ref, duals_ref, along_ref, masked_ref, turned_ref = refs
+    *gathered, merged_ref, mask_ref, gains_ref, duals_ref, along_ref, masked_ref, turned_ref, power_ref = refs
     rows, lanes = merged_ref.shape[1:]
     index = lax.axis_index("freq")
     held, bases = [], []
@@ -258,8 +276,10 @@
     gains_ref[...] = gains
     duals_ref[...] = jnp.stack(duals)
     along_ref[...] = jnp.stack(along)
-    masked_ref[...] = gains * mask_ref[...][None]
+    masked = gains * mask_ref[...][None]
+    masked_ref[...] = masked
     turned_ref[...] = turn(gains)
+    power_ref[...] = masked[0] * masked[0] + masked[1] * masked[1]
 
 
 def finish_kernel(parts, terms, *refs):
@@ -321,27 +341,27 @@
             pltpu.VMEM((1, receptors), jnp.int32),
             pltpu.SemaphoreType.DMA((3,)),
         ],
-        compiler_params=pltpu.CompilerParams(vmem_limit_bytes=16 * MIB),
+        compiler_params=pltpu.CompilerParams(vmem_limit_bytes=4 * MIB),
         cost_estimate=pl.CostEstimate(flops=1 << 36, bytes_accessed=1 << 28, transcendentals=0),
         name="setup",
     )(*[pltpu.with_memory_space_constraint(one, pltpu.HBM) for one in small])
 
-    def part(name, start, length, masked, turned):
+    def part(name, start, length, operands):
         return pl.pallas_call(
             functools.partial(part_kernel, start, True),
             out_shape=sums_shape(length),
-            in_specs=whole_vmem(4),
+            in_specs=whole_vmem(len(operands)),
             out_specs=pl.BlockSpec(memory_space=pltpu.VMEM),
-            compiler_params=pltpu.CompilerParams(vmem_limit_bytes=32 * MIB),
+            compiler_params=pltpu.CompilerParams(vmem_limit_bytes=3 * MIB),
             cost_estimate=cost(length),
             name=name,
-        )(model_block, vis_block, masked, turned)
-
-    def worker(name, ranges, results, masked, turned):
+        )(*operands)
+
+    def worker(name, ranges, results, fixed, now):
         def work(at, message, distance):
-            message, one, two = lax.optimization_barrier((message, masked, turned))
+            message, current = lax.optimization_barrier((message, now))
             got = exchange(message, "tm", distance)
-            result = part(f"{name}{at}", *ranges[at], one, two)
+            result = part(f"{name}{at}", *ranges[at], fixed[:2] + current[:2] + fixed[2:] + current[2:])
             got, result = lax.optimization_barrier((got, result))
             results.append(result)
             return got
@@ -354,13 +374,13 @@
             out_shape=outs,
             in_specs=whole_vmem(len(operands)),
             out_specs=whole_vmem(len(outs)),
-            compiler_params=pltpu.CompilerParams(vmem_limit_bytes=16 * MIB),
+            compiler_params=pltpu.CompilerParams(vmem_limit_bytes=4 * MIB),
             name=name,
         )(*operands)
 
-    beside = [(ROWS * a, ROWS * n) for a, n in cut(units, [11.0] * (steps - 1) + [10.0])]
+    beside = [(ROWS * a, ROWS * n) for a, n in cut(units, [13.0] * (steps - 1) + [6.0])]
     sums = []
-    held, own, got = time_exchange(merged, distances, weights, worker("first", beside, sums, masked, turned))
+    held, own, got = time_exchange(merged, distances, weights, worker("first", beside, sums, [model_block, vis_block], [masked, turned]))
     operands = sums + own + held + [got, merged, gains, mask]
     (payload,) = small_kernel(
         functools.partial(middle_kernel, len(sums), len(held)),
@@ -368,16 +388,30 @@
         operands,
         [jax.ShapeDtypeStruct((1, 5, directions, receptors), f32)],
     )
+    payload, model_now = lax.optimization_barrier((payload, model_block))
     gathered = freq_gather(payload)
-    gains, duals, along_freq, masked, turned = small_kernel(
+    model_wide, model_square = pl.pallas_call(
+        widen_kernel,
+        out_shape=[
+            jax.ShapeDtypeStruct(model_block.shape, f32),
+            jax.ShapeDtypeStruct((directions, receptors, receptors), f32),
+        ],
+        in_specs=whole_vmem(1),
+        out_specs=whole_vmem(2),
+        compiler_params=pltpu.CompilerParams(vmem_limit_bytes=3 * MIB),
+        cost_estimate=pl.CostEstimate(flops=28 * pairs * 96, bytes_accessed=12 * pairs * receptors, transcendentals=0),
+        name="widen",
+    )(model_now)
+    gathered, model_wide, model_square = lax.optimization_barrier((gathered, model_wide, model_square))
+    gains, duals, along_freq, masked, turned, power = small_kernel(
         functools.partial(update_kernel, freq_count),
         "update",
         gathered + [merged, mask],
-        [state] * 4 + [turned_shape],
+        [state] * 4 + [turned_shape, jax.ShapeDtypeStruct((directions, receptors), f32)],
     )
 
     sums = []
-    held, own, got = time_exchange(along_freq, distances, weights, worker("second", beside, sums, masked, turned))
+    held, own, got = time_exchange(along_freq, distances, weights, worker("second", beside, sums, [model_wide, vis_block, model_square], [masked, turned, power]))
     operands = sums + own + held + [got, gains, duals, mask]
     outputs = small_kernel(functools.partial(finish_kernel, len(sums), len(held)), "finish", operands, [state] * 3)
     return tuple(out[None, None] for out in outputs)

time: 37.2 us -> 36 us (0.968)
  waiting for transfers between devices: 4.21 us -> 2.53 us
  Pallas kernels: 18.6 us -> 19.1 us
    ppermute x9, waiting for transfers between devices: 4.21 us -> 2.53 us  [exchange(): lax.ppermute(array, axis, [(place, place ^ distance) for place in range(s...]
    pallas_call x0 -> x1, Pallas kernels: none -> 1.67 us  [per_device(): pl.pallas_call(widen_kernel, out_shape=[jax.ShapeDtypeStruct(model_block....]
    pallas_call x6, Pallas kernels: 16.4 us -> 15.3 us  [part(): pl.pallas_call(functools.partial(part_kernel, start, True), out_shape=sum...]
  transfers between devices with their start and end apart: 9 -> 9, of which waited for: 2 -> 2; matrix products, arithmetic and copies ran while one was open for 0% -> 0% of each run, Pallas kernels for 44% -> 47%
where the time goes in v4:
time: 36 us; the launch traced here: 35.8 us
  Pallas kernels  19.1 us (53%)
  starting transfers between devices  13.3 us (37%)
  waiting for transfers between devices  2.53 us (7%)
  between operations  0.78 us (2%)
    pallas_call x6, Pallas kernels, part(): pl.pallas_call(functools.partial(part_kernel, start, True), out_shape=sum...  15.3 us
    ppermute x9, starting transfers between devices, exchange(): lax.ppermute(array, axis, [(place, place ^ distance) for place in range(s...  13.3 us
    ppermute x9, waiting for transfers between devices, exchange(): lax.ppermute(array, axis, [(place, place ^ distance) for place in range(s...  2.53 us
    pallas_call x1, Pallas kernels, per_device(): pl.pallas_call(widen_kernel, out_shape=[jax.ShapeDtypeStruct(model_block....  1.67 us
    pallas_call x1, Pallas kernels, per_device(): pl.pallas_call(functools.partial(setup_kernel, ('tm', time_count, distanc...  1.09 us
    pallas_call x3, Pallas kernels, small_kernel(): pl.pallas_call(kernel, out_shape=outs, in_specs=whole_vmem(len(operands))...  1.07 us
  transfers between devices with their start and end apart: 9, of which 2 were waited for; matrix products, arithmetic and copies ran while one was open for 0% of the time, Pallas kernels for 47%

profile of v4, /device:TPU:1, one launch (start us, length us, event | category | flops | bytes accessed | tf_op | source)
XLA Modules:
  0.0 35.8 jit_solution(3080557679817887161)
XLA Ops:
  0.6 0.0 copy-start
  0.6 0.0 copy-start.1
  0.7 1.1 %setup.1 = (f32[2,8,512]{2,1,0:T(8,128)S(1)}, f32[2,8,512]{2,1,0:T(8,128)S(1)}, f32[2,8,512]{2,1,0:T(8,128)S(1)}, f32[512,128]{1,0:T(8,128)S(1)}, f32[1,512]{1,0...) custom-call(f32[2,8,512]{2,1,0:T(8,128)} %bitcast.42, ...), custom_call_target="tpu_custom_call" | custom-call | flops 68719476736 | bytes 268435456 | tf_op jit(solution)/shard_map/setup/pallas_call | solution.py:332
  1.8 3.2 %collective-permute-start = (f32[2,8,512]{2,1,0:T(8,128)S(1)}, f32[2,8,512]{2,1,0:T(8,128)S(1)}, u32[]{:S(2)}, u32[]{:S(2)}) collective-permute-start(f32[2,8,512]{2,1,0:T(8,128)S(1)} %get-tuple-element.71.refs_7_.refs_12_.refs_4_), channel_id=1, source_target_pairs={{0,4},{1,5},{2,6},{3,7},{4,0},{5,1},{6,2},{7,3},{8,12},{9,13},{10,... | collective-permute-start | bytes 98312 | tf_op jit(solution)/shard_map/ppermute | solution.py:37
  5.0 0.0 copy-done
  5.0 3.3 %first0.1.refs_0_ = f32[208,128]{1,0:T(8,128)S(1)} custom-call(bf16[8,2,512,512]{3,2,1,0:T(8,128)(2,1)S(1)} %bitcast.28, bf16[2,512,512]{2,1,0:T(8,128)(2,1)S(1)} %bitcast.32, f32[2,8,512]{2,1,0:T(8,128)S(1)} %get-tuple-element.86.refs_2_, f32[512,128]{1,0:T(8,128)S(1)} %get-tuple-element.87.refs_3_), custom_call_target="tpu_custom_call" | custom-call | flops 23855104 | bytes 3407872 | tf_op jit(solution)/shard_map/first0/pallas_call | solution.py:350
  8.2 0.0 collective-permute-done.refs_8_
  8.3 1.5 %collective-permute-start.1 = (f32[2,2,8,512]{3,2,1,0:T(8,128)S(1)}, f32[2,2,8,512]{3,2,1,0:T(8,128)S(1)}, u32[]{:S(2)}, u32[]{:S(2)}) collective-permute-start(f32[2,2,8,512]{3,2,1,0:T(8,128)S(1)} %pad_maximum_fusion), channel_id=1, source_target_pairs={{0,2},{1,3},{2,0},{3,1},{4,6},{5,7},{6,4},{7,5},{8,10},{9,11},{10,... | collective-permute-start | bytes 196616 | tf_op jit(solution)/shard_map/ppermute | solution.py:37
  9.8 3.3 %first1.1.refs_1_ = f32[208,128]{1,0:T(8,128)S(1)} custom-call(bf16[8,2,512,512]{3,2,1,0:T(8,128)(2,1)S(1)} %bitcast.29, bf16[2,512,512]{2,1,0:T(8,128)(2,1)S(1)} %bitcast.33, f32[2,8,512]{2,1,0:T(8,128)S(1)} %get-tuple-element.86.refs_2_, f32[512,128]{1,0:T(8,128)S(1)} %get-tuple-element.87.refs_3_), custom_call_target="tpu_custom_call" | custom-call | flops 23855104 | bytes 3407872 | tf_op jit(solution)/shard_map/first1/pallas_call | solution.py:350
  13.0 0.0 collective-permute-done.1
  13.1 1.1 %collective-permute-start.2 = (f32[2,8,512]{2,1,0:T(8,128)S(1)}, f32[2,8,512]{2,1,0:T(8,128)S(1)}, u32[]{:S(2)}, u32[]{:S(2)}) collective-permute-start(f32[2,8,512]{2,1,0:T(8,128)S(1)} %multiply_add_fusion.1), channel_id=1, source_target_pairs={{0,1},{1,0},{2,3},{3,2},{4,5},{5,4},{6,7},{7,6},{8,9},{9,8},{10,11... | collective-permute-start | bytes 98312 | tf_op jit(solution)/shard_map/ppermute | solution.py:37
  14.2 1.5 %first2.1.refs_2_ = f32[96,128]{1,0:T(8,128)S(1)} custom-call(bf16[8,2,512,512]{3,2,1,0:T(8,128)(2,1)S(1)} %bitcast.30, bf16[2,512,512]{2,1,0:T(8,128)(2,1)S(1)} %bitcast.34, f32[2,8,512]{2,1,0:T(8,128)S(1)} %get-tuple-element.86.refs_2_, f32[512,128]{1,0:T(8,128)S(1)} %get-tuple-element.87.refs_3_), custom_call_target="tpu_custom_call" | custom-call | flops 11010048 | bytes 1572864 | tf_op jit(solution)/shard_map/first2/pallas_call | solution.py:350
  15.8 0.0 collective-permute-done.2.refs_11_
  15.8 0.1 middle.1.refs_0_
  15.9 2.2 %collective-permute-start.5 = (f32[1,5,8,512]{3,2,1,0:T(8,128)S(1)}, f32[1,5,8,512]{3,2,1,0:T(8,128)S(1)}, u32[]{:S(2)}, u32[]{:S(2)}) collective-permute-start(f32[1,5,8,512]{3,2,1,0:T(8,128)S(1)} %middle.1.refs_0_), channel_id=1, source_target_pairs={{0,24},{8,16},{16,8},{24,0},{1,25},{9,17},{17,9},{25,1},{2,26},{10... | collective-permute-start | bytes 245768 | tf_op jit(solution)/shard_map/ppermute | solution.py:37
  18.1 0.2 collective-permute-start.4
  18.4 0.3 collective-permute-start.3
  18.6 1.7 %widen.1 = (f32[8,2,512,512]{3,2,1,0:T(8,128)S(1)}, f32[8,512,512]{2,1,0:T(8,128)S(1)}) custom-call(bf16[8,2,512,512]{3,2,1,0:T(8,128)(2,1)S(1)} %bitcast.31), custom_call_target="tpu_custom_call" | custom-call | flops 11010048 | bytes 25165824 | tf_op jit(solution)/shard_map/widen/pallas_call | solution.py:393
  20.3 0.6 %collective-permute-done.5.refs_3_ = f32[1,5,8,512]{3,2,1,0:T(8,128)S(1)} collective-permute-done((f32[1,5,8,512]{3,2,1,0:T(8,128)S(1)}, f32[1,5,8,512]{3,2,1,0:T(8,128)S(1)}, u32[]{:S(2)}, u32[]{:S(2)}) %collective-permute-start.5) | collective-permute-done | bytes 81952 | tf_op jit(solution)/shard_map/ppermute | solution.py:37
  20.9 1.9 %collective-permute-done.4.refs_2_ = f32[1,5,8,512]{3,2,1,0:T(8,128)S(1)} collective-permute-done((f32[1,5,8,512]{3,2,1,0:T(8,128)S(1)}, f32[1,5,8,512]{3,2,1,0:T(8,128)S(1)}, u32[]{:S(2)}, u32[]{:S(2)}) %collective-permute-start.4) | collective-permute-done | bytes 81952 | tf_op jit(solution)/shard_map/ppermute | solution.py:37
  22.8 0.0 collective-permute-done.3.refs_1_
  22.8 0.2 update.1
  23.0 2.3 %collective-permute-start.6 = (f32[2,8,512]{2,1,0:T(8,128)S(1)}, f32[2,8,512]{2,1,0:T(8,128)S(1)}, u32[]{:S(2)}, u32[]{:S(2)}) collective-permute-start(f32[2,8,512]{2,1,0:T(8,128)S(1)} %get-tuple-element.108.refs_7_), channel_id=1, source_target_pairs={{0,4},{1,5},{2,6},{3,7},{4,0},{5,1},{6,2},{7,3},{8,12},{9,13},{10,... | collective-permute-start | bytes 98312 | tf_op jit(solution)/shard_map/ppermute | solution.py:37
  25.3 2.9 %second0.1.refs_0_ = f32[208,128]{1,0:T(8,128)S(1)} custom-call(f32[8,2,512,512]{3,2,1,0:T(8,128)S(1)} %get-tuple-element.109.refs_0_, bf16[2,512,512]{2,1,0:T(8,128)(2,1)S(1)} %bitcast.35, f32[2,8,512]{2,1,0:T(8,128)S(1)} %get-tuple-element.123.refs_2_, f32[512,128]{1,0:T(8,128)S(1)} %get-tuple-element.124.refs_3_, ...), custom_call_target="tpu_custom_call" | custom-call | flops 23855104 | bytes 3407872 | tf_op jit(solution)/shard_map/second0/pallas_call | solution.py:350
  28.2 0.0 collective-permute-done.6.refs_8_
  28.2 0.8 %collective-permute-start.7 = (f32[2,2,8,512]{3,2,1,0:T(8,128)S(1)}, f32[2,2,8,512]{3,2,1,0:T(8,128)S(1)}, u32[]{:S(2)}, u32[]{:S(2)}) collective-permute-start(f32[2,2,8,512]{3,2,1,0:T(8,128)S(1)} %pad_maximum_fusion.1), channel_id=1, source_target_pairs={{0,2},{1,3},{2,0},{3,1},{4,6},{5,7},{6,4},{7,5},{8,10},{9,11},{10,... | collective-permute-start | bytes 196616 | tf_op jit(solution)/shard_map/ppermute | solution.py:37
  29.0 2.9 %second1.1.refs_1_ = f32[208,128]{1,0:T(8,128)S(1)} custom-call(f32[8,2,512,512]{3,2,1,0:T(8,128)S(1)} %get-tuple-element.109.refs_0_, bf16[2,512,512]{2,1,0:T(8,128)(2,1)S(1)} %bitcast.36, f32[2,8,512]{2,1,0:T(8,128)S(1)} %get-tuple-element.123.refs_2_, f32[512,128]{1,0:T(8,128)S(1)} %get-tuple-element.124.refs_3_, ...), custom_call_target="tpu_custom_call" | custom-call | flops 23855104 | bytes 3407872 | tf_op jit(solution)/shard_map/second1/pallas_call | solution.py:350
  31.9 0.0 collective-permute-done.7
  32.0 1.7 %collective-permute-start.8 = (f32[2,8,512]{2,1,0:T(8,128)S(1)}, f32[2,8,512]{2,1,0:T(8,128)S(1)}, u32[]{:S(2)}, u32[]{:S(2)}) collective-permute-start(f32[2,8,512]{2,1,0:T(8,128)S(1)} %multiply_add_fusion), channel_id=1, source_target_pairs={{0,1},{1,0},{2,3},{3,2},{4,5},{5,4},{6,7},{7,6},{8,9},{9,8},{10,11... | collective-permute-start | bytes 98312 | tf_op jit(solution)/shard_map/ppermute | solution.py:37
  33.7 1.4 %second2.1.refs_2_ = f32[96,128]{1,0:T(8,128)S(1)} custom-call(f32[8,2,512,512]{3,2,1,0:T(8,128)S(1)} %get-tuple-element.109.refs_0_, bf16[2,512,512]{2,1,0:T(8,128)(2,1)S(1)} %bitcast.37, f32[2,8,512]{2,1,0:T(8,128)S(1)} %get-tuple-element.123.refs_2_, f32[512,128]{1,0:T(8,128)S(1)} %get-tuple-element.124.refs_3_, ...), custom_call_target="tpu_custom_call" | custom-call | flops 11010048 | bytes 1572864 | tf_op jit(solution)/shard_map/second2/pallas_call | solution.py:350
  35.0 0.0 collective-permute-done.8.refs_11_
  35.1 0.8 %finish.1 = (f32[2,8,512]{2,1,0:T(8,128)}, f32[2,8,512]{2,1,0:T(8,128)}, f32[2,8,512]{2,1,0:T(8,128)}) custom-call(f32[208,128]{1,0:T(8,128)S(1)} %second0.1.refs_0_, f32[208,128]{1,0:T(8,128)S(1)} %second1.1.refs_1_, f32[96,128]{1,0:T(8,128)S(1)} %second2.1.refs_2_, f32[2,8,512]{2,1,0:T(8,128)S(1)} %get-tuple-element.89.refs_3_, ...), custom_call_target="tpu_custom_call" | custom-call | tf_op jit(solution)/shard_map/finish/pallas_call | solution.py:372
  (7 shorter events, 0.1 us)
Async XLA Ops:
  0.6 4.3 %copy-start = (bf16[1,8,2,512,512]{4,3,2,1,0:T(8,128)(2,1)S(1)}, bf16[1,8,2,512,512]{4,3,2,1,0:T(8,128)(2,1)}, u32[]{:S(2)}) copy-start(bf16[1,8,2,512,512]{4,3,2,1,0:T(8,128)(2,1)} %param.6) | copy-start | bytes 25165828
  0.6 4.3 %copy-start.1 = (bf16[1,1,2,512,512]{4,3,2,1,0:T(8,128)(2,1)S(1)}, bf16[1,1,2,512,512]{4,3,2,1,0:T(8,128)(2,1)}, u32[]{:S(2)}) copy-start(bf16[1,1,2,512,512]{4,3,2,1,0:T(8,128)(2,1)} %param.5) | copy-start | bytes 3145732
  1.8 6.5 %collective-permute-start = (f32[2,8,512]{2,1,0:T(8,128)S(1)}, f32[2,8,512]{2,1,0:T(8,128)S(1)}, u32[]{:S(2)}, u32[]{:S(2)}) collective-permute-start(f32[2,8,512]{2,1,0:T(8,128)S(1)} %get-tuple-element.71.refs_7_.refs_12_.refs_4_), channel_id=1, source_target_pairs={{0,4},{1,5},{2,6},{3,7},{4,0},{5,1},{6,2},{7,3},{8,12},{9,13},{10,... | collective-permute-start | bytes 98312 | tf_op jit(solution)/shard_map/ppermute | solution.py:37
  8.3 4.8 %collective-permute-start.1 = (f32[2,2,8,512]{3,2,1,0:T(8,128)S(1)}, f32[2,2,8,512]{3,2,1,0:T(8,128)S(1)}, u32[]{:S(2)}, u32[]{:S(2)}) collective-permute-start(f32[2,2,8,512]{3,2,1,0:T(8,128)S(1)} %pad_maximum_fusion), channel_id=1, source_target_pairs={{0,2},{1,3},{2,0},{3,1},{4,6},{5,7},{6,4},{7,5},{8,10},{9,11},{10,... | collective-permute-start | bytes 196616 | tf_op jit(solution)/shard_map/ppermute | solution.py:37
  13.1 2.7 %collective-permute-start.2 = (f32[2,8,512]{2,1,0:T(8,128)S(1)}, f32[2,8,512]{2,1,0:T(8,128)S(1)}, u32[]{:S(2)}, u32[]{:S(2)}) collective-permute-start(f32[2,8,512]{2,1,0:T(8,128)S(1)} %multiply_add_fusion.1), channel_id=1, source_target_pairs={{0,1},{1,0},{2,3},{3,2},{4,5},{5,4},{6,7},{7,6},{8,9},{9,8},{10,11... | collective-permute-start | bytes 98312 | tf_op jit(solution)/shard_map/ppermute | solution.py:37
  15.9 5.0 %collective-permute-start.5 = (f32[1,5,8,512]{3,2,1,0:T(8,128)S(1)}, f32[1,5,8,512]{3,2,1,0:T(8,128)S(1)}, u32[]{:S(2)}, u32[]{:S(2)}) collective-permute-start(f32[1,5,8,512]{3,2,1,0:T(8,128)S(1)} %middle.1.refs_0_), channel_id=1, source_target_pairs={{0,24},{8,16},{16,8},{24,0},{1,25},{9,17},{17,9},{25,1},{2,26},{10... | collective-permute-start | bytes 245768 | tf_op jit(solution)/shard_map/ppermute | solution.py:37
  18.1 4.7 %collective-permute-start.4 = (f32[1,5,8,512]{3,2,1,0:T(8,128)S(1)}, f32[1,5,8,512]{3,2,1,0:T(8,128)S(1)}, u32[]{:S(2)}, u32[]{:S(2)}) collective-permute-start(f32[1,5,8,512]{3,2,1,0:T(8,128)S(1)} %middle.1.refs_0_), channel_id=1, source_target_pairs={{0,16},{8,24},{16,0},{24,8},{1,17},{9,25},{17,1},{25,9},{2,18},{10... | collective-permute-start | bytes 245768 | tf_op jit(solution)/shard_map/ppermute | solution.py:37
  18.4 4.4 %collective-permute-start.3 = (f32[1,5,8,512]{3,2,1,0:T(8,128)S(1)}, f32[1,5,8,512]{3,2,1,0:T(8,128)S(1)}, u32[]{:S(2)}, u32[]{:S(2)}) collective-permute-start(f32[1,5,8,512]{3,2,1,0:T(8,128)S(1)} %middle.1.refs_0_), channel_id=1, source_target_pairs={{0,8},{8,0},{16,24},{24,16},{1,9},{9,1},{17,25},{25,17},{2,10},{10... | collective-permute-start | bytes 245768 | tf_op jit(solution)/shard_map/ppermute | solution.py:37
  23.0 5.2 %collective-permute-start.6 = (f32[2,8,512]{2,1,0:T(8,128)S(1)}, f32[2,8,512]{2,1,0:T(8,128)S(1)}, u32[]{:S(2)}, u32[]{:S(2)}) collective-permute-start(f32[2,8,512]{2,1,0:T(8,128)S(1)} %get-tuple-element.108.refs_7_), channel_id=1, source_target_pairs={{0,4},{1,5},{2,6},{3,7},{4,0},{5,1},{6,2},{7,3},{8,12},{9,13},{10,... | collective-permute-start | bytes 98312 | tf_op jit(solution)/shard_map/ppermute | solution.py:37
  28.2 3.7 %collective-permute-start.7 = (f32[2,2,8,512]{3,2,1,0:T(8,128)S(1)}, f32[2,2,8,512]{3,2,1,0:T(8,128)S(1)}, u32[]{:S(2)}, u32[]{:S(2)}) collective-permute-start(f32[2,2,8,512]{3,2,1,0:T(8,128)S(1)} %pad_maximum_fusion.1), channel_id=1, source_target_pairs={{0,2},{1,3},{2,0},{3,1},{4,6},{5,7},{6,4},{7,5},{8,10},{9,11},{10,... | collective-permute-start | bytes 196616 | tf_op jit(solution)/shard_map/ppermute | solution.py:37
  32.0 3.1 %collective-permute-start.8 = (f32[2,8,512]{2,1,0:T(8,128)S(1)}, f32[2,8,512]{2,1,0:T(8,128)S(1)}, u32[]{:S(2)}, u32[]{:S(2)}) collective-permute-start(f32[2,8,512]{2,1,0:T(8,128)S(1)} %multiply_add_fusion), channel_id=1, source_target_pairs={{0,1},{1,0},{2,3},{3,2},{4,5},{5,4},{6,7},{7,6},{8,9},{9,8},{10,11... | collective-permute-start | bytes 98312 | tf_op jit(solution)/shard_map/ppermute | solution.py:37

commit v5 on v4

--- a/solution.py
+++ b/solution.py
@@ -121,7 +121,7 @@
     return padded.T
 
 
-def sum_rows(rows, model_ref, vis_ref, masked_ref, turned_ref, square_ref=None, power_ref=None):
+def sum_rows(out_ref, out_rows, rows, model_ref, vis_ref, masked_ref, turned_ref, square_ref=None, power_ref=None):
     directions, blocks = model_ref.shape[0], model_ref.shape[3] // LANES
     turned = turned_ref[rows, :]
 
@@ -155,8 +155,6 @@
         real = vis_ref[0, rows, columns].astype(f32) - (whole[block] - by_imag[block])
         imag = vis_ref[1, rows, columns].astype(f32) - (whole[block] + by_real[block])
         residuals.append((real, imag + real, imag - real))
-    lane = lax.broadcasted_iota(jnp.int32, (ROWS, LANES), 1)
-    out = jnp.zeros((ROWS, LANES), f32)
     for k in range(directions):
         shared = by_gap = by_sum = curvature = None
         for block in range(blocks):
@@ -171,8 +169,8 @@
             else:
                 curvature = add(curvature, square_ref[k, rows, columns] * power_ref[k : k + 1, columns])
         for kind, total in enumerate((by_gap + shared, by_sum - shared, curvature)):
-            out = jnp.where(lane == kind * directions + k, jnp.sum(total, axis=1, keepdims=True), out)
-    return out
+            place = kind * directions + k
+            out_ref[out_rows, place : place + 1] = jnp.sum(total, axis=1, keepdims=True)
 
 
 def part_kernel(start, unroll, *refs):
@@ -181,7 +179,7 @@
     def step(at, carry):
         first = pl.multiple_of(at * ROWS, ROWS)
         rows = pl.ds(pl.multiple_of(start + first, ROWS), ROWS)
-        sums_ref[pl.ds(first, ROWS), :] = sum_rows(rows, *inputs)
+        sum_rows(sums_ref, pl.ds(first, ROWS), rows, *inputs)
         return carry
 
     lax.fori_loop(0, sums_ref.shape[0] // ROWS, step, 0, unroll=unroll)
@@ -322,6 +320,9 @@
     steps = len(distances)
     units = receptors // ROWS
 
+    def shares(first, middle, last):
+        return ([first] + [middle] * (steps - 2) + [last])[-steps:]
+
     def sums_shape(length):
         return jax.ShapeDtypeStruct((length, LANES), f32)
 
@@ -378,7 +379,7 @@
             name=name,
         )(*operands)
 
-    beside = [(ROWS * a, ROWS * n) for a, n in cut(units, [13.0] * (steps - 1) + [6.0])]
+    beside = [(ROWS * a, ROWS * n) for a, n in cut(units, shares(15.0, 13.0, 4.0))]
     sums = []
     held, own, got = time_exchange(merged, distances, weights, worker("first", beside, sums, [model_block, vis_block], [masked, turned]))
     operands = sums + own + held + [got, merged, gains, mask]
@@ -410,6 +411,7 @@
         [state] * 4 + [turned_shape, jax.ShapeDtypeStruct((directions, receptors), f32)],
     )
 
+    beside = [(ROWS * a, ROWS * n) for a, n in cut(units, shares(12.0, 14.0, 6.0))]
     sums = []
     held, own, got = time_exchange(along_freq, distances, weights, worker("second", beside, sums, [model_wide, vis_block, model_square], [masked, turned, power]))
     operands = sums + own + held + [got, gains, duals, mask]

time: 36 us -> 35.6 us (0.989)
  transfers between devices with their start and end apart: 9 -> 9, of which waited for: 2 -> 2; matrix products, arithmetic and copies ran while one was open for 0% -> 0% of each run, Pallas kernels for 47% -> 48%
where the time goes in v5:
time: 35.6 us; the launch traced here: 35.4 us
  Pallas kernels  19 us (53%)
  starting transfers between devices  13.2 us (37%)
  waiting for transfers between devices  2.4 us (7%)
  between operations  0.77 us (2%)
    pallas_call x6, Pallas kernels, part(): pl.pallas_call(functools.partial(part_kernel, start, True), out_shape=sum...  15.2 us
    ppermute x9, starting transfers between devices, exchange(): lax.ppermute(array, axis, [(place, place ^ distance) for place in range(s...  13.2 us
    ppermute x9, waiting for transfers between devices, exchange(): lax.ppermute(array, axis, [(place, place ^ distance) for place in range(s...  2.4 us
    pallas_call x1, Pallas kernels, per_device(): pl.pallas_call(widen_kernel, out_shape=[jax.ShapeDtypeStruct(model_block....  1.67 us
    pallas_call x1, Pallas kernels, per_device(): pl.pallas_call(functools.partial(setup_kernel, ('tm', time_count, distanc...  1.09 us
    pallas_call x3, Pallas kernels, small_kernel(): pl.pallas_call(kernel, out_shape=outs, in_specs=whole_vmem(len(operands))...  1.06 us
  transfers between devices with their start and end apart: 9, of which 2 were waited for; matrix products, arithmetic and copies ran while one was open for 0% of the time, Pallas kernels for 48%

profile of v5, /device:TPU:1, one launch (start us, length us, event | category | flops | bytes accessed | tf_op | source)
XLA Modules:
  0.0 35.4 jit_solution(1833006570047021828)
XLA Ops:
  0.6 0.0 copy-start
  0.6 0.0 copy-start.1
  0.7 1.1 %setup.1 = (f32[2,8,512]{2,1,0:T(8,128)S(1)}, f32[2,8,512]{2,1,0:T(8,128)S(1)}, f32[2,8,512]{2,1,0:T(8,128)S(1)}, f32[512,128]{1,0:T(8,128)S(1)}, f32[1,512]{1,0...) custom-call(f32[2,8,512]{2,1,0:T(8,128)} %bitcast.42, ...), custom_call_target="tpu_custom_call" | custom-call | flops 68719476736 | bytes 268435456 | tf_op jit(solution)/shard_map/setup/pallas_call | solution.py:333
  1.8 3.2 %collective-permute-start = (f32[2,8,512]{2,1,0:T(8,128)S(1)}, f32[2,8,512]{2,1,0:T(8,128)S(1)}, u32[]{:S(2)}, u32[]{:S(2)}) collective-permute-start(f32[2,8,512]{2,1,0:T(8,128)S(1)} %get-tuple-element.71.refs_7_.refs_12_.refs_4_), channel_id=1, source_target_pairs={{0,4},{1,5},{2,6},{3,7},{4,0},{5,1},{6,2},{7,3},{8,12},{9,13},{10,... | collective-permute-start | bytes 98312 | tf_op jit(solution)/shard_map/ppermute | solution.py:37
  5.0 0.0 copy-done
  5.0 3.7 %first0.1.refs_0_ = f32[240,128]{1,0:T(8,128)S(1)} custom-call(bf16[8,2,512,512]{3,2,1,0:T(8,128)(2,1)S(1)} %bitcast.28, bf16[2,512,512]{2,1,0:T(8,128)(2,1)S(1)} %bitcast.32, f32[2,8,512]{2,1,0:T(8,128)S(1)} %get-tuple-element.86.refs_2_, f32[512,128]{1,0:T(8,128)S(1)} %get-tuple-element.87.refs_3_), custom_call_target="tpu_custom_call" | custom-call | flops 27525120 | bytes 3932160 | tf_op jit(solution)/shard_map/first0/pallas_call | solution.py:351
  8.6 0.0 collective-permute-done.refs_8_
  8.6 1.5 %collective-permute-start.1 = (f32[2,2,8,512]{3,2,1,0:T(8,128)S(1)}, f32[2,2,8,512]{3,2,1,0:T(8,128)S(1)}, u32[]{:S(2)}, u32[]{:S(2)}) collective-permute-start(f32[2,2,8,512]{3,2,1,0:T(8,128)S(1)} %pad_maximum_fusion), channel_id=1, source_target_pairs={{0,2},{1,3},{2,0},{3,1},{4,6},{5,7},{6,4},{7,5},{8,10},{9,11},{10,... | collective-permute-start | bytes 196616 | tf_op jit(solution)/shard_map/ppermute | solution.py:37
  10.2 3.2 %first1.1.refs_1_ = f32[208,128]{1,0:T(8,128)S(1)} custom-call(bf16[8,2,512,512]{3,2,1,0:T(8,128)(2,1)S(1)} %bitcast.29, bf16[2,512,512]{2,1,0:T(8,128)(2,1)S(1)} %bitcast.33, f32[2,8,512]{2,1,0:T(8,128)S(1)} %get-tuple-element.86.refs_2_, f32[512,128]{1,0:T(8,128)S(1)} %get-tuple-element.87.refs_3_), custom_call_target="tpu_custom_call" | custom-call | flops 23855104 | bytes 3407872 | tf_op jit(solution)/shard_map/first1/pallas_call | solution.py:351
  13.3 0.0 collective-permute-done.1
  13.4 1.1 %collective-permute-start.2 = (f32[2,8,512]{2,1,0:T(8,128)S(1)}, f32[2,8,512]{2,1,0:T(8,128)S(1)}, u32[]{:S(2)}, u32[]{:S(2)}) collective-permute-start(f32[2,8,512]{2,1,0:T(8,128)S(1)} %multiply_add_fusion.1), channel_id=1, source_target_pairs={{0,1},{1,0},{2,3},{3,2},{4,5},{5,4},{6,7},{7,6},{8,9},{9,8},{10,11... | collective-permute-start | bytes 98312 | tf_op jit(solution)/shard_map/ppermute | solution.py:37
  14.5 1.0 %first2.1.refs_2_ = f32[64,128]{1,0:T(8,128)S(1)} custom-call(bf16[8,2,512,512]{3,2,1,0:T(8,128)(2,1)S(1)} %bitcast.30, bf16[2,512,512]{2,1,0:T(8,128)(2,1)S(1)} %bitcast.34, f32[2,8,512]{2,1,0:T(8,128)S(1)} %get-tuple-element.86.refs_2_, f32[512,128]{1,0:T(8,128)S(1)} %get-tuple-element.87.refs_3_), custom_call_target="tpu_custom_call" | custom-call | flops 7340032 | bytes 1048576 | tf_op jit(solution)/shard_map/first2/pallas_call | solution.py:351
  15.5 0.0 collective-permute-done.2.refs_11_
  15.5 0.1 middle.1.refs_0_
  15.7 2.2 %collective-permute-start.5 = (f32[1,5,8,512]{3,2,1,0:T(8,128)S(1)}, f32[1,5,8,512]{3,2,1,0:T(8,128)S(1)}, u32[]{:S(2)}, u32[]{:S(2)}) collective-permute-start(f32[1,5,8,512]{3,2,1,0:T(8,128)S(1)} %middle.1.refs_0_), channel_id=1, source_target_pairs={{0,24},{8,16},{16,8},{24,0},{1,25},{9,17},{17,9},{25,1},{2,26},{10... | collective-permute-start | bytes 245768 | tf_op jit(solution)/shard_map/ppermute | solution.py:37
  17.9 0.2 collective-permute-start.4
  18.1 0.3 collective-permute-start.3
  18.4 1.7 %widen.1 = (f32[8,2,512,512]{3,2,1,0:T(8,128)S(1)}, f32[8,512,512]{2,1,0:T(8,128)S(1)}) custom-call(bf16[8,2,512,512]{3,2,1,0:T(8,128)(2,1)S(1)} %bitcast.31), custom_call_target="tpu_custom_call" | custom-call | flops 11010048 | bytes 25165824 | tf_op jit(solution)/shard_map/widen/pallas_call | solution.py:394
  20.1 0.5 %collective-permute-done.5.refs_3_ = f32[1,5,8,512]{3,2,1,0:T(8,128)S(1)} collective-permute-done((f32[1,5,8,512]{3,2,1,0:T(8,128)S(1)}, f32[1,5,8,512]{3,2,1,0:T(8,128)S(1)}, u32[]{:S(2)}, u32[]{:S(2)}) %collective-permute-start.5) | collective-permute-done | bytes 81952 | tf_op jit(solution)/shard_map/ppermute | solution.py:37
  20.5 1.9 %collective-permute-done.4.refs_2_ = f32[1,5,8,512]{3,2,1,0:T(8,128)S(1)} collective-permute-done((f32[1,5,8,512]{3,2,1,0:T(8,128)S(1)}, f32[1,5,8,512]{3,2,1,0:T(8,128)S(1)}, u32[]{:S(2)}, u32[]{:S(2)}) %collective-permute-start.4) | collective-permute-done | bytes 81952 | tf_op jit(solution)/shard_map/ppermute | solution.py:37
  22.5 0.0 collective-permute-done.3.refs_1_
  22.5 0.2 update.1
  22.6 2.3 %collective-permute-start.6 = (f32[2,8,512]{2,1,0:T(8,128)S(1)}, f32[2,8,512]{2,1,0:T(8,128)S(1)}, u32[]{:S(2)}, u32[]{:S(2)}) collective-permute-start(f32[2,8,512]{2,1,0:T(8,128)S(1)} %get-tuple-element.108.refs_7_), channel_id=1, source_target_pairs={{0,4},{1,5},{2,6},{3,7},{4,0},{5,1},{6,2},{7,3},{8,12},{9,13},{10,... | collective-permute-start | bytes 98312 | tf_op jit(solution)/shard_map/ppermute | solution.py:37
  24.9 2.7 %second0.1.refs_0_ = f32[192,128]{1,0:T(8,128)S(1)} custom-call(f32[8,2,512,512]{3,2,1,0:T(8,128)S(1)} %get-tuple-element.109.refs_0_, bf16[2,512,512]{2,1,0:T(8,128)(2,1)S(1)} %bitcast.35, f32[2,8,512]{2,1,0:T(8,128)S(1)} %get-tuple-element.123.refs_2_, f32[512,128]{1,0:T(8,128)S(1)} %get-tuple-element.124.refs_3_, ...), custom_call_target="tpu_custom_call" | custom-call | flops 22020096 | bytes 3145728 | tf_op jit(solution)/shard_map/second0/pallas_call | solution.py:351
  27.6 0.0 collective-permute-done.6.refs_8_
  27.7 0.9 %collective-permute-start.7 = (f32[2,2,8,512]{3,2,1,0:T(8,128)S(1)}, f32[2,2,8,512]{3,2,1,0:T(8,128)S(1)}, u32[]{:S(2)}, u32[]{:S(2)}) collective-permute-start(f32[2,2,8,512]{3,2,1,0:T(8,128)S(1)} %pad_maximum_fusion.1), channel_id=1, source_target_pairs={{0,2},{1,3},{2,0},{3,1},{4,6},{5,7},{6,4},{7,5},{8,10},{9,11},{10,... | collective-permute-start | bytes 196616 | tf_op jit(solution)/shard_map/ppermute | solution.py:37
  28.5 3.2 %second1.1.refs_1_ = f32[224,128]{1,0:T(8,128)S(1)} custom-call(f32[8,2,512,512]{3,2,1,0:T(8,128)S(1)} %get-tuple-element.109.refs_0_, bf16[2,512,512]{2,1,0:T(8,128)(2,1)S(1)} %bitcast.36, f32[2,8,512]{2,1,0:T(8,128)S(1)} %get-tuple-element.123.refs_2_, f32[512,128]{1,0:T(8,128)S(1)} %get-tuple-element.124.refs_3_, ...), custom_call_target="tpu_custom_call" | custom-call | flops 25690112 | bytes 3670016 | tf_op jit(solution)/shard_map/second1/pallas_call | solution.py:351
  31.7 0.0 collective-permute-done.7
  31.8 1.5 %collective-permute-start.8 = (f32[2,8,512]{2,1,0:T(8,128)S(1)}, f32[2,8,512]{2,1,0:T(8,128)S(1)}, u32[]{:S(2)}, u32[]{:S(2)}) collective-permute-start(f32[2,8,512]{2,1,0:T(8,128)S(1)} %multiply_add_fusion), channel_id=1, source_target_pairs={{0,1},{1,0},{2,3},{3,2},{4,5},{5,4},{6,7},{7,6},{8,9},{9,8},{10,11... | collective-permute-start | bytes 98312 | tf_op jit(solution)/shard_map/ppermute | solution.py:37
  33.2 1.4 %second2.1.refs_2_ = f32[96,128]{1,0:T(8,128)S(1)} custom-call(f32[8,2,512,512]{3,2,1,0:T(8,128)S(1)} %get-tuple-element.109.refs_0_, bf16[2,512,512]{2,1,0:T(8,128)(2,1)S(1)} %bitcast.37, f32[2,8,512]{2,1,0:T(8,128)S(1)} %get-tuple-element.123.refs_2_, f32[512,128]{1,0:T(8,128)S(1)} %get-tuple-element.124.refs_3_, ...), custom_call_target="tpu_custom_call" | custom-call | flops 11010048 | bytes 1572864 | tf_op jit(solution)/shard_map/second2/pallas_call | solution.py:351
  34.6 0.0 collective-permute-done.8.refs_11_
  34.7 0.7 %finish.1 = (f32[2,8,512]{2,1,0:T(8,128)}, f32[2,8,512]{2,1,0:T(8,128)}, f32[2,8,512]{2,1,0:T(8,128)}) custom-call(f32[192,128]{1,0:T(8,128)S(1)} %second0.1.refs_0_, f32[224,128]{1,0:T(8,128)S(1)} %second1.1.refs_1_, f32[96,128]{1,0:T(8,128)S(1)} %second2.1.refs_2_, f32[2,8,512]{2,1,0:T(8,128)S(1)} %get-tuple-element.89.refs_3_, ...), custom_call_target="tpu_custom_call" | custom-call | tf_op jit(solution)/shard_map/finish/pallas_call | solution.py:373
  (7 shorter events, 0.1 us)
Async XLA Ops:
  0.6 4.3 %copy-start = (bf16[1,8,2,512,512]{4,3,2,1,0:T(8,128)(2,1)S(1)}, bf16[1,8,2,512,512]{4,3,2,1,0:T(8,128)(2,1)}, u32[]{:S(2)}) copy-start(bf16[1,8,2,512,512]{4,3,2,1,0:T(8,128)(2,1)} %param.6) | copy-start | bytes 25165828
  0.6 4.3 %copy-start.1 = (bf16[1,1,2,512,512]{4,3,2,1,0:T(8,128)(2,1)S(1)}, bf16[1,1,2,512,512]{4,3,2,1,0:T(8,128)(2,1)}, u32[]{:S(2)}) copy-start(bf16[1,1,2,512,512]{4,3,2,1,0:T(8,128)(2,1)} %param.5) | copy-start | bytes 3145732
  1.8 6.9 %collective-permute-start = (f32[2,8,512]{2,1,0:T(8,128)S(1)}, f32[2,8,512]{2,1,0:T(8,128)S(1)}, u32[]{:S(2)}, u32[]{:S(2)}) collective-permute-start(f32[2,8,512]{2,1,0:T(8,128)S(1)} %get-tuple-element.71.refs_7_.refs_12_.refs_4_), channel_id=1, source_target_pairs={{0,4},{1,5},{2,6},{3,7},{4,0},{5,1},{6,2},{7,3},{8,12},{9,13},{10,... | collective-permute-start | bytes 98312 | tf_op jit(solution)/shard_map/ppermute | solution.py:37
  8.6 4.7 %collective-permute-start.1 = (f32[2,2,8,512]{3,2,1,0:T(8,128)S(1)}, f32[2,2,8,512]{3,2,1,0:T(8,128)S(1)}, u32[]{:S(2)}, u32[]{:S(2)}) collective-permute-start(f32[2,2,8,512]{3,2,1,0:T(8,128)S(1)} %pad_maximum_fusion), channel_id=1, source_target_pairs={{0,2},{1,3},{2,0},{3,1},{4,6},{5,7},{6,4},{7,5},{8,10},{9,11},{10,... | collective-permute-start | bytes 196616 | tf_op jit(solution)/shard_map/ppermute | solution.py:37
  13.4 2.2 %collective-permute-start.2 = (f32[2,8,512]{2,1,0:T(8,128)S(1)}, f32[2,8,512]{2,1,0:T(8,128)S(1)}, u32[]{:S(2)}, u32[]{:S(2)}) collective-permute-start(f32[2,8,512]{2,1,0:T(8,128)S(1)} %multiply_add_fusion.1), channel_id=1, source_target_pairs={{0,1},{1,0},{2,3},{3,2},{4,5},{5,4},{6,7},{7,6},{8,9},{9,8},{10,11... | collective-permute-start | bytes 98312 | tf_op jit(solution)/shard_map/ppermute | solution.py:37
  15.7 4.9 %collective-permute-start.5 = (f32[1,5,8,512]{3,2,1,0:T(8,128)S(1)}, f32[1,5,8,512]{3,2,1,0:T(8,128)S(1)}, u32[]{:S(2)}, u32[]{:S(2)}) collective-permute-start(f32[1,5,8,512]{3,2,1,0:T(8,128)S(1)} %middle.1.refs_0_), channel_id=1, source_target_pairs={{0,24},{8,16},{16,8},{24,0},{1,25},{9,17},{17,9},{25,1},{2,26},{10... | collective-permute-start | bytes 245768 | tf_op jit(solution)/shard_map/ppermute | solution.py:37
  17.9 4.5 %collective-permute-start.4 = (f32[1,5,8,512]{3,2,1,0:T(8,128)S(1)}, f32[1,5,8,512]{3,2,1,0:T(8,128)S(1)}, u32[]{:S(2)}, u32[]{:S(2)}) collective-permute-start(f32[1,5,8,512]{3,2,1,0:T(8,128)S(1)} %middle.1.refs_0_), channel_id=1, source_target_pairs={{0,16},{8,24},{16,0},{24,8},{1,17},{9,25},{17,1},{25,9},{2,18},{10... | collective-permute-start | bytes 245768 | tf_op jit(solution)/shard_map/ppermute | solution.py:37
  18.1 4.3 %collective-permute-start.3 = (f32[1,5,8,512]{3,2,1,0:T(8,128)S(1)}, f32[1,5,8,512]{3,2,1,0:T(8,128)S(1)}, u32[]{:S(2)}, u32[]{:S(2)}) collective-permute-start(f32[1,5,8,512]{3,2,1,0:T(8,128)S(1)} %middle.1.refs_0_), channel_id=1, source_target_pairs={{0,8},{8,0},{16,24},{24,16},{1,9},{9,1},{17,25},{25,17},{2,10},{10... | collective-permute-start | bytes 245768 | tf_op jit(solution)/shard_map/ppermute | solution.py:37
  22.6 5.0 %collective-permute-start.6 = (f32[2,8,512]{2,1,0:T(8,128)S(1)}, f32[2,8,512]{2,1,0:T(8,128)S(1)}, u32[]{:S(2)}, u32[]{:S(2)}) collective-permute-start(f32[2,8,512]{2,1,0:T(8,128)S(1)} %get-tuple-element.108.refs_7_), channel_id=1, source_target_pairs={{0,4},{1,5},{2,6},{3,7},{4,0},{5,1},{6,2},{7,3},{8,12},{9,13},{10,... | collective-permute-start | bytes 98312 | tf_op jit(solution)/shard_map/ppermute | solution.py:37
  27.7 4.1 %collective-permute-start.7 = (f32[2,2,8,512]{3,2,1,0:T(8,128)S(1)}, f32[2,2,8,512]{3,2,1,0:T(8,128)S(1)}, u32[]{:S(2)}, u32[]{:S(2)}) collective-permute-start(f32[2,2,8,512]{3,2,1,0:T(8,128)S(1)} %pad_maximum_fusion.1), channel_id=1, source_target_pairs={{0,2},{1,3},{2,0},{3,1},{4,6},{5,7},{6,4},{7,5},{8,10},{9,11},{10,... | collective-permute-start | bytes 196616 | tf_op jit(solution)/shard_map/ppermute | solution.py:37
  31.8 2.9 %collective-permute-start.8 = (f32[2,8,512]{2,1,0:T(8,128)S(1)}, f32[2,8,512]{2,1,0:T(8,128)S(1)}, u32[]{:S(2)}, u32[]{:S(2)}) collective-permute-start(f32[2,8,512]{2,1,0:T(8,128)S(1)} %multiply_add_fusion), channel_id=1, source_target_pairs={{0,1},{1,0},{2,3},{3,2},{4,5},{5,4},{6,7},{7,6},{8,9},{9,8},{10,11... | collective-permute-start | bytes 98312 | tf_op jit(solution)/shard_map/ppermute | solution.py:37

commit v6 on v5

--- a/solution.py
+++ b/solution.py
@@ -121,7 +121,7 @@
     return padded.T
 
 
-def sum_rows(out_ref, out_rows, rows, model_ref, vis_ref, masked_ref, turned_ref, square_ref=None, power_ref=None):
+def sum_rows(rows, model_ref, vis_ref, masked_ref, turned_ref, square_ref=None, power_ref=None):
     directions, blocks = model_ref.shape[0], model_ref.shape[3] // LANES
     turned = turned_ref[rows, :]
 
@@ -155,6 +155,7 @@
         real = vis_ref[0, rows, columns].astype(f32) - (whole[block] - by_imag[block])
         imag = vis_ref[1, rows, columns].astype(f32) - (whole[block] + by_real[block])
         residuals.append((real, imag + real, imag - real))
+    found = []
     for k in range(directions):
         shared = by_gap = by_sum = curvature = None
         for block in range(blocks):
@@ -169,20 +170,29 @@
             else:
                 curvature = add(curvature, square_ref[k, rows, columns] * power_ref[k : k + 1, columns])
         for kind, total in enumerate((by_gap + shared, by_sum - shared, curvature)):
-            place = kind * directions + k
-            out_ref[out_rows, place : place + 1] = jnp.sum(total, axis=1, keepdims=True)
-
-
-def part_kernel(start, unroll, *refs):
+            found.append((kind * directions + k, jnp.sum(total, axis=1, keepdims=True)))
+    return found
+
+
+def part_kernel(start, late, *refs):
     *inputs, sums_ref = refs
-
-    def step(at, carry):
-        first = pl.multiple_of(at * ROWS, ROWS)
-        rows = pl.ds(pl.multiple_of(start + first, ROWS), ROWS)
-        sum_rows(sums_ref, pl.ds(first, ROWS), rows, *inputs)
-        return carry
-
-    lax.fori_loop(0, sums_ref.shape[0] // ROWS, step, 0, unroll=unroll)
+    lane = lax.broadcasted_iota(jnp.int32, (ROWS, LANES), 1)
+    waiting = None
+    for first in range(0, sums_ref.shape[0], ROWS):
+        here = pl.ds(first, ROWS)
+        found = sum_rows(pl.ds(start + first, ROWS), *inputs)
+        if not late:
+            for place, total in found:
+                sums_ref[here, place : place + 1] = total
+            continue
+        row = jnp.zeros((ROWS, LANES), f32)
+        for place, total in found:
+            row = jnp.where(lane == place, total, row)
+        if waiting is not None:
+            sums_ref[waiting[0], :] = waiting[1]
+        waiting = here, row
+    if waiting is not None:
+        sums_ref[waiting[0], :] = waiting[1]
 
 
 def widen_kernel(model_ref, wide_ref, square_ref):
@@ -349,7 +359,7 @@
 
     def part(name, start, length, operands):
         return pl.pallas_call(
-            functools.partial(part_kernel, start, True),
+            functools.partial(part_kernel, start, len(operands) > 4),
             out_shape=sums_shape(length),
             in_specs=whole_vmem(len(operands)),
             out_specs=pl.BlockSpec(memory_space=pltpu.VMEM),

time: 35.6 us -> 35.5 us (level)
  transfers between devices with their start and end apart: 9 -> 9, of which waited for: 2 -> 2; matrix products, arithmetic and copies ran while one was open for 0% -> 0% of each run, Pallas kernels for 48% -> 47%
where the time goes in v6:
time: 35.5 us; the launch traced here: 35.3 us
  Pallas kernels  18.8 us (53%)
  starting transfers between devices  13.2 us (37%)
  waiting for transfers between devices  2.4 us (7%)
  between operations  0.78 us (2%)
    pallas_call x6, Pallas kernels, part(): pl.pallas_call(functools.partial(part_kernel, start, len(operands) > 4),...  15 us
    ppermute x9, starting transfers between devices, exchange(): lax.ppermute(array, axis, [(place, place ^ distance) for place in range(s...  13.2 us
    ppermute x9, waiting for transfers between devices, exchange(): lax.ppermute(array, axis, [(place, place ^ distance) for place in range(s...  2.4 us
    pallas_call x1, Pallas kernels, per_device(): pl.pallas_call(widen_kernel, out_shape=[jax.ShapeDtypeStruct(model_block....  1.67 us
    pallas_call x1, Pallas kernels, per_device(): pl.pallas_call(functools.partial(setup_kernel, ('tm', time_count, distanc...  1.09 us
    pallas_call x3, Pallas kernels, small_kernel(): pl.pallas_call(kernel, out_shape=outs, in_specs=whole_vmem(len(operands))...  1.06 us
  transfers between devices with their start and end apart: 9, of which 2 were waited for; matrix products, arithmetic and copies ran while one was open for 0% of the time, Pallas kernels for 47%

profile of v6, /device:TPU:1, one launch (start us, length us, event | category | flops | bytes accessed | tf_op | source)
XLA Modules:
  0.0 35.3 jit_solution(10892338253226587766)
XLA Ops:
  0.6 0.0 copy-start
  0.6 0.0 copy-start.1
  0.7 1.1 %setup.1 = (f32[2,8,512]{2,1,0:T(8,128)S(1)}, f32[2,8,512]{2,1,0:T(8,128)S(1)}, f32[2,8,512]{2,1,0:T(8,128)S(1)}, f32[512,128]{1,0:T(8,128)S(1)}, f32[1,512]{1,0...) custom-call(f32[2,8,512]{2,1,0:T(8,128)} %bitcast.42, ...), custom_call_target="tpu_custom_call" | custom-call | flops 68719476736 | bytes 268435456 | tf_op jit(solution)/shard_map/setup/pallas_call | solution.py:343
  1.8 3.2 %collective-permute-start = (f32[2,8,512]{2,1,0:T(8,128)S(1)}, f32[2,8,512]{2,1,0:T(8,128)S(1)}, u32[]{:S(2)}, u32[]{:S(2)}) collective-permute-start(f32[2,8,512]{2,1,0:T(8,128)S(1)} %get-tuple-element.71.refs_7_.refs_12_.refs_4_), channel_id=1, source_target_pairs={{0,4},{1,5},{2,6},{3,7},{4,0},{5,1},{6,2},{7,3},{8,12},{9,13},{10,... | collective-permute-start | bytes 98312 | tf_op jit(solution)/shard_map/ppermute | solution.py:37
  5.0 0.0 copy-done.1
  5.0 3.7 %first0.1.refs_0_ = f32[240,128]{1,0:T(8,128)S(1)} custom-call(bf16[8,2,512,512]{3,2,1,0:T(8,128)(2,1)S(1)} %bitcast.28, bf16[2,512,512]{2,1,0:T(8,128)(2,1)S(1)} %bitcast.32, f32[2,8,512]{2,1,0:T(8,128)S(1)} %get-tuple-element.86.refs_2_, f32[512,128]{1,0:T(8,128)S(1)} %get-tuple-element.87.refs_3_), custom_call_target="tpu_custom_call" | custom-call | flops 27525120 | bytes 3932160 | tf_op jit(solution)/shard_map/first0/pallas_call | solution.py:361
  8.6 0.0 collective-permute-done.refs_8_
  8.6 1.5 %collective-permute-start.1 = (f32[2,2,8,512]{3,2,1,0:T(8,128)S(1)}, f32[2,2,8,512]{3,2,1,0:T(8,128)S(1)}, u32[]{:S(2)}, u32[]{:S(2)}) collective-permute-start(f32[2,2,8,512]{3,2,1,0:T(8,128)S(1)} %pad_maximum_fusion), channel_id=1, source_target_pairs={{0,2},{1,3},{2,0},{3,1},{4,6},{5,7},{6,4},{7,5},{8,10},{9,11},{10,... | collective-permute-start | bytes 196616 | tf_op jit(solution)/shard_map/ppermute | solution.py:37
  10.2 3.2 %first1.1.refs_1_ = f32[208,128]{1,0:T(8,128)S(1)} custom-call(bf16[8,2,512,512]{3,2,1,0:T(8,128)(2,1)S(1)} %bitcast.29, bf16[2,512,512]{2,1,0:T(8,128)(2,1)S(1)} %bitcast.33, f32[2,8,512]{2,1,0:T(8,128)S(1)} %get-tuple-element.86.refs_2_, f32[512,128]{1,0:T(8,128)S(1)} %get-tuple-element.87.refs_3_), custom_call_target="tpu_custom_call" | custom-call | flops 23855104 | bytes 3407872 | tf_op jit(solution)/shard_map/first1/pallas_call | solution.py:361
  13.3 0.0 collective-permute-done.1
  13.4 1.1 %collective-permute-start.2 = (f32[2,8,512]{2,1,0:T(8,128)S(1)}, f32[2,8,512]{2,1,0:T(8,128)S(1)}, u32[]{:S(2)}, u32[]{:S(2)}) collective-permute-start(f32[2,8,512]{2,1,0:T(8,128)S(1)} %multiply_add_fusion.1), channel_id=1, source_target_pairs={{0,1},{1,0},{2,3},{3,2},{4,5},{5,4},{6,7},{7,6},{8,9},{9,8},{10,11... | collective-permute-start | bytes 98312 | tf_op jit(solution)/shard_map/ppermute | solution.py:37
  14.5 1.0 %first2.1.refs_2_ = f32[64,128]{1,0:T(8,128)S(1)} custom-call(bf16[8,2,512,512]{3,2,1,0:T(8,128)(2,1)S(1)} %bitcast.30, bf16[2,512,512]{2,1,0:T(8,128)(2,1)S(1)} %bitcast.34, f32[2,8,512]{2,1,0:T(8,128)S(1)} %get-tuple-element.86.refs_2_, f32[512,128]{1,0:T(8,128)S(1)} %get-tuple-element.87.refs_3_), custom_call_target="tpu_custom_call" | custom-call | flops 7340032 | bytes 1048576 | tf_op jit(solution)/shard_map/first2/pallas_call | solution.py:361
  15.5 0.0 collective-permute-done.2.refs_11_
  15.5 0.1 middle.1.refs_0_
  15.7 2.2 %collective-permute-start.5 = (f32[1,5,8,512]{3,2,1,0:T(8,128)S(1)}, f32[1,5,8,512]{3,2,1,0:T(8,128)S(1)}, u32[]{:S(2)}, u32[]{:S(2)}) collective-permute-start(f32[1,5,8,512]{3,2,1,0:T(8,128)S(1)} %middle.1.refs_0_), channel_id=1, source_target_pairs={{0,24},{8,16},{16,8},{24,0},{1,25},{9,17},{17,9},{25,1},{2,26},{10... | collective-permute-start | bytes 245768 | tf_op jit(solution)/shard_map/ppermute | solution.py:37
  17.9 0.2 collective-permute-start.4
  18.1 0.3 collective-permute-start.3
  18.4 1.7 %widen.1 = (f32[8,2,512,512]{3,2,1,0:T(8,128)S(1)}, f32[8,512,512]{2,1,0:T(8,128)S(1)}) custom-call(bf16[8,2,512,512]{3,2,1,0:T(8,128)(2,1)S(1)} %bitcast.31), custom_call_target="tpu_custom_call" | custom-call | flops 11010048 | bytes 25165824 | tf_op jit(solution)/shard_map/widen/pallas_call | solution.py:404
  20.1 0.5 %collective-permute-done.5.refs_3_ = f32[1,5,8,512]{3,2,1,0:T(8,128)S(1)} collective-permute-done((f32[1,5,8,512]{3,2,1,0:T(8,128)S(1)}, f32[1,5,8,512]{3,2,1,0:T(8,128)S(1)}, u32[]{:S(2)}, u32[]{:S(2)}) %collective-permute-start.5) | collective-permute-done | bytes 81952 | tf_op jit(solution)/shard_map/ppermute | solution.py:37
  20.5 1.9 %collective-permute-done.4.refs_2_ = f32[1,5,8,512]{3,2,1,0:T(8,128)S(1)} collective-permute-done((f32[1,5,8,512]{3,2,1,0:T(8,128)S(1)}, f32[1,5,8,512]{3,2,1,0:T(8,128)S(1)}, u32[]{:S(2)}, u32[]{:S(2)}) %collective-permute-start.4) | collective-permute-done | bytes 81952 | tf_op jit(solution)/shard_map/ppermute | solution.py:37
  22.5 0.0 collective-permute-done.3.refs_1_
  22.5 0.2 update.1
  22.6 2.3 %collective-permute-start.6 = (f32[2,8,512]{2,1,0:T(8,128)S(1)}, f32[2,8,512]{2,1,0:T(8,128)S(1)}, u32[]{:S(2)}, u32[]{:S(2)}) collective-permute-start(f32[2,8,512]{2,1,0:T(8,128)S(1)} %get-tuple-element.108.refs_7_), channel_id=1, source_target_pairs={{0,4},{1,5},{2,6},{3,7},{4,0},{5,1},{6,2},{7,3},{8,12},{9,13},{10,... | collective-permute-start | bytes 98312 | tf_op jit(solution)/shard_map/ppermute | solution.py:37
  24.9 2.7 %second0.1.refs_0_ = f32[192,128]{1,0:T(8,128)S(1)} custom-call(f32[8,2,512,512]{3,2,1,0:T(8,128)S(1)} %get-tuple-element.109.refs_0_, bf16[2,512,512]{2,1,0:T(8,128)(2,1)S(1)} %bitcast.35, f32[2,8,512]{2,1,0:T(8,128)S(1)} %get-tuple-element.123.refs_2_, f32[512,128]{1,0:T(8,128)S(1)} %get-tuple-element.124.refs_3_, ...), custom_call_target="tpu_custom_call" | custom-call | flops 22020096 | bytes 3145728 | tf_op jit(solution)/shard_map/second0/pallas_call | solution.py:361
  27.6 0.0 collective-permute-done.6.refs_8_
  27.6 0.9 %collective-permute-start.7 = (f32[2,2,8,512]{3,2,1,0:T(8,128)S(1)}, f32[2,2,8,512]{3,2,1,0:T(8,128)S(1)}, u32[]{:S(2)}, u32[]{:S(2)}) collective-permute-start(f32[2,2,8,512]{3,2,1,0:T(8,128)S(1)} %pad_maximum_fusion.1), channel_id=1, source_target_pairs={{0,2},{1,3},{2,0},{3,1},{4,6},{5,7},{6,4},{7,5},{8,10},{9,11},{10,... | collective-permute-start | bytes 196616 | tf_op jit(solution)/shard_map/ppermute | solution.py:37
  28.5 3.1 %second1.1.refs_1_ = f32[224,128]{1,0:T(8,128)S(1)} custom-call(f32[8,2,512,512]{3,2,1,0:T(8,128)S(1)} %get-tuple-element.109.refs_0_, bf16[2,512,512]{2,1,0:T(8,128)(2,1)S(1)} %bitcast.36, f32[2,8,512]{2,1,0:T(8,128)S(1)} %get-tuple-element.123.refs_2_, f32[512,128]{1,0:T(8,128)S(1)} %get-tuple-element.124.refs_3_, ...), custom_call_target="tpu_custom_call" | custom-call | flops 25690112 | bytes 3670016 | tf_op jit(solution)/shard_map/second1/pallas_call | solution.py:361
  31.6 0.0 collective-permute-done.7
  31.6 1.5 %collective-permute-start.8 = (f32[2,8,512]{2,1,0:T(8,128)S(1)}, f32[2,8,512]{2,1,0:T(8,128)S(1)}, u32[]{:S(2)}, u32[]{:S(2)}) collective-permute-start(f32[2,8,512]{2,1,0:T(8,128)S(1)} %multiply_add_fusion), channel_id=1, source_target_pairs={{0,1},{1,0},{2,3},{3,2},{4,5},{5,4},{6,7},{7,6},{8,9},{9,8},{10,11... | collective-permute-start | bytes 98312 | tf_op jit(solution)/shard_map/ppermute | solution.py:37
  33.2 1.4 %second2.1.refs_2_ = f32[96,128]{1,0:T(8,128)S(1)} custom-call(f32[8,2,512,512]{3,2,1,0:T(8,128)S(1)} %get-tuple-element.109.refs_0_, bf16[2,512,512]{2,1,0:T(8,128)(2,1)S(1)} %bitcast.37, f32[2,8,512]{2,1,0:T(8,128)S(1)} %get-tuple-element.123.refs_2_, f32[512,128]{1,0:T(8,128)S(1)} %get-tuple-element.124.refs_3_, ...), custom_call_target="tpu_custom_call" | custom-call | flops 11010048 | bytes 1572864 | tf_op jit(solution)/shard_map/second2/pallas_call | solution.py:361
  34.5 0.0 collective-permute-done.8.refs_11_
  34.6 0.7 %finish.1 = (f32[2,8,512]{2,1,0:T(8,128)}, f32[2,8,512]{2,1,0:T(8,128)}, f32[2,8,512]{2,1,0:T(8,128)}) custom-call(f32[192,128]{1,0:T(8,128)S(1)} %second0.1.refs_0_, f32[224,128]{1,0:T(8,128)S(1)} %second1.1.refs_1_, f32[96,128]{1,0:T(8,128)S(1)} %second2.1.refs_2_, f32[2,8,512]{2,1,0:T(8,128)S(1)} %get-tuple-element.89.refs_3_, ...), custom_call_target="tpu_custom_call" | custom-call | tf_op jit(solution)/shard_map/finish/pallas_call | solution.py:383
  (7 shorter events, 0.1 us)
Async XLA Ops:
  0.6 4.3 %copy-start = (bf16[1,8,2,512,512]{4,3,2,1,0:T(8,128)(2,1)S(1)}, bf16[1,8,2,512,512]{4,3,2,1,0:T(8,128)(2,1)}, u32[]{:S(2)}) copy-start(bf16[1,8,2,512,512]{4,3,2,1,0:T(8,128)(2,1)} %param.6) | copy-start | bytes 25165828
  0.6 4.3 %copy-start.1 = (bf16[1,1,2,512,512]{4,3,2,1,0:T(8,128)(2,1)S(1)}, bf16[1,1,2,512,512]{4,3,2,1,0:T(8,128)(2,1)}, u32[]{:S(2)}) copy-start(bf16[1,1,2,512,512]{4,3,2,1,0:T(8,128)(2,1)} %param.5) | copy-start | bytes 3145732
  1.8 6.9 %collective-permute-start = (f32[2,8,512]{2,1,0:T(8,128)S(1)}, f32[2,8,512]{2,1,0:T(8,128)S(1)}, u32[]{:S(2)}, u32[]{:S(2)}) collective-permute-start(f32[2,8,512]{2,1,0:T(8,128)S(1)} %get-tuple-element.71.refs_7_.refs_12_.refs_4_), channel_id=1, source_target_pairs={{0,4},{1,5},{2,6},{3,7},{4,0},{5,1},{6,2},{7,3},{8,12},{9,13},{10,... | collective-permute-start | bytes 98312 | tf_op jit(solution)/shard_map/ppermute | solution.py:37
  8.6 4.7 %collective-permute-start.1 = (f32[2,2,8,512]{3,2,1,0:T(8,128)S(1)}, f32[2,2,8,512]{3,2,1,0:T(8,128)S(1)}, u32[]{:S(2)}, u32[]{:S(2)}) collective-permute-start(f32[2,2,8,512]{3,2,1,0:T(8,128)S(1)} %pad_maximum_fusion), channel_id=1, source_target_pairs={{0,2},{1,3},{2,0},{3,1},{4,6},{5,7},{6,4},{7,5},{8,10},{9,11},{10,... | collective-permute-start | bytes 196616 | tf_op jit(solution)/shard_map/ppermute | solution.py:37
  13.4 2.2 %collective-permute-start.2 = (f32[2,8,512]{2,1,0:T(8,128)S(1)}, f32[2,8,512]{2,1,0:T(8,128)S(1)}, u32[]{:S(2)}, u32[]{:S(2)}) collective-permute-start(f32[2,8,512]{2,1,0:T(8,128)S(1)} %multiply_add_fusion.1), channel_id=1, source_target_pairs={{0,1},{1,0},{2,3},{3,2},{4,5},{5,4},{6,7},{7,6},{8,9},{9,8},{10,11... | collective-permute-start | bytes 98312 | tf_op jit(solution)/shard_map/ppermute | solution.py:37
  15.7 4.9 %collective-permute-start.5 = (f32[1,5,8,512]{3,2,1,0:T(8,128)S(1)}, f32[1,5,8,512]{3,2,1,0:T(8,128)S(1)}, u32[]{:S(2)}, u32[]{:S(2)}) collective-permute-start(f32[1,5,8,512]{3,2,1,0:T(8,128)S(1)} %middle.1.refs_0_), channel_id=1, source_target_pairs={{0,24},{8,16},{16,8},{24,0},{1,25},{9,17},{17,9},{25,1},{2,26},{10... | collective-permute-start | bytes 245768 | tf_op jit(solution)/shard_map/ppermute | solution.py:37
  17.9 4.5 %collective-permute-start.4 = (f32[1,5,8,512]{3,2,1,0:T(8,128)S(1)}, f32[1,5,8,512]{3,2,1,0:T(8,128)S(1)}, u32[]{:S(2)}, u32[]{:S(2)}) collective-permute-start(f32[1,5,8,512]{3,2,1,0:T(8,128)S(1)} %middle.1.refs_0_), channel_id=1, source_target_pairs={{0,16},{8,24},{16,0},{24,8},{1,17},{9,25},{17,1},{25,9},{2,18},{10... | collective-permute-start | bytes 245768 | tf_op jit(solution)/shard_map/ppermute | solution.py:37
  18.1 4.3 %collective-permute-start.3 = (f32[1,5,8,512]{3,2,1,0:T(8,128)S(1)}, f32[1,5,8,512]{3,2,1,0:T(8,128)S(1)}, u32[]{:S(2)}, u32[]{:S(2)}) collective-permute-start(f32[1,5,8,512]{3,2,1,0:T(8,128)S(1)} %middle.1.refs_0_), channel_id=1, source_target_pairs={{0,8},{8,0},{16,24},{24,16},{1,9},{9,1},{17,25},{25,17},{2,10},{10... | collective-permute-start | bytes 245768 | tf_op jit(solution)/shard_map/ppermute | solution.py:37
  22.6 4.9 %collective-permute-start.6 = (f32[2,8,512]{2,1,0:T(8,128)S(1)}, f32[2,8,512]{2,1,0:T(8,128)S(1)}, u32[]{:S(2)}, u32[]{:S(2)}) collective-permute-start(f32[2,8,512]{2,1,0:T(8,128)S(1)} %get-tuple-element.108.refs_7_), channel_id=1, source_target_pairs={{0,4},{1,5},{2,6},{3,7},{4,0},{5,1},{6,2},{7,3},{8,12},{9,13},{10,... | collective-permute-start | bytes 98312 | tf_op jit(solution)/shard_map/ppermute | solution.py:37
  27.6 4.0 %collective-permute-start.7 = (f32[2,2,8,512]{3,2,1,0:T(8,128)S(1)}, f32[2,2,8,512]{3,2,1,0:T(8,128)S(1)}, u32[]{:S(2)}, u32[]{:S(2)}) collective-permute-start(f32[2,2,8,512]{3,2,1,0:T(8,128)S(1)} %pad_maximum_fusion.1), channel_id=1, source_target_pairs={{0,2},{1,3},{2,0},{3,1},{4,6},{5,7},{6,4},{7,5},{8,10},{9,11},{10,... | collective-permute-start | bytes 196616 | tf_op jit(solution)/shard_map/ppermute | solution.py:37
  31.6 2.9 %collective-permute-start.8 = (f32[2,8,512]{2,1,0:T(8,128)S(1)}, f32[2,8,512]{2,1,0:T(8,128)S(1)}, u32[]{:S(2)}, u32[]{:S(2)}) collective-permute-start(f32[2,8,512]{2,1,0:T(8,128)S(1)} %multiply_add_fusion), channel_id=1, source_target_pairs={{0,1},{1,0},{2,3},{3,2},{4,5},{5,4},{6,7},{7,6},{8,9},{9,8},{10,11... | collective-permute-start | bytes 98312 | tf_op jit(solution)/shard_map/ppermute | solution.py:37

commit v7 on v6

--- a/solution.py
+++ b/solution.py
@@ -327,6 +327,7 @@
 
     freq_count, time_count = lax.axis_size("freq"), lax.axis_size("tm")
     distances = [1 << b for b in reversed(range(time_count.bit_length() - 1))]
+    distances[-2:] = distances[-2:][::-1]
     steps = len(distances)
     units = receptors // ROWS
 
@@ -389,7 +390,7 @@
             name=name,
         )(*operands)
 
-    beside = [(ROWS * a, ROWS * n) for a, n in cut(units, shares(15.0, 13.0, 4.0))]
+    beside = [(ROWS * a, ROWS * n) for a, n in cut(units, shares(12.0, 5.0, 15.0))]
     sums = []
     held, own, got = time_exchange(merged, distances, weights, worker("first", beside, sums, [model_block, vis_block], [masked, turned]))
     operands = sums + own + held + [got, merged, gains, mask]
@@ -421,7 +422,7 @@
         [state] * 4 + [turned_shape, jax.ShapeDtypeStruct((directions, receptors), f32)],
     )
 
-    beside = [(ROWS * a, ROWS * n) for a, n in cut(units, shares(12.0, 14.0, 6.0))]
+    beside = [(ROWS * a, ROWS * n) for a, n in cut(units, shares(11.0, 6.0, 15.0))]
     sums = []
     held, own, got = time_exchange(along_freq, distances, weights, worker("second", beside, sums, [model_wide, vis_block, model_square], [masked, turned, power]))
     operands = sums + own + held + [got, gains, duals, mask]

time: 35.5 us -> 34.9 us (0.983)
  starting transfers between devices: 13.2 us -> 12.2 us
    ppermute x9, starting transfers between devices: 13.2 us -> 12.2 us  [exchange(): lax.ppermute(array, axis, [(place, place ^ distance) for place in range(s...]
  transfers between devices with their start and end apart: 9 -> 9, of which waited for: 2 -> 2; matrix products, arithmetic and copies ran while one was open for 0% -> 0% of each run, Pallas kernels for 47% -> 49%
where the time goes in v7:
time: 34.9 us; the launch traced here: 34.5 us
  Pallas kernels  19.1 us (55%)
  starting transfers between devices  12.2 us (35%)
  waiting for transfers between devices  2.26 us (6%)
  between operations  0.77 us (2%)
    pallas_call x6, Pallas kernels, part(): pl.pallas_call(functools.partial(part_kernel, start, len(operands) > 4),...  15.3 us
    ppermute x9, starting transfers between devices, exchange(): lax.ppermute(array, axis, [(place, place ^ distance) for place in range(s...  12.2 us
    ppermute x9, waiting for transfers between devices, exchange(): lax.ppermute(array, axis, [(place, place ^ distance) for place in range(s...  2.26 us
    pallas_call x1, Pallas kernels, per_device(): pl.pallas_call(widen_kernel, out_shape=[jax.ShapeDtypeStruct(model_block....  1.67 us
    pallas_call x1, Pallas kernels, per_device(): pl.pallas_call(functools.partial(setup_kernel, ('tm', time_count, distanc...  1.09 us
    pallas_call x3, Pallas kernels, small_kernel(): pl.pallas_call(kernel, out_shape=outs, in_specs=whole_vmem(len(operands))...  1.06 us
  transfers between devices with their start and end apart: 9, of which 2 were waited for; matrix products, arithmetic and copies ran while one was open for 0% of the time, Pallas kernels for 49%

profile of v7, /device:TPU:1, one launch (start us, length us, event | category | flops | bytes accessed | tf_op | source)
XLA Modules:
  0.0 34.5 jit_solution(3708531054137941742)
XLA Ops:
  0.6 0.0 copy-start
  0.6 0.0 copy-start.1
  0.7 1.1 %setup.1 = (f32[2,8,512]{2,1,0:T(8,128)S(1)}, f32[2,8,512]{2,1,0:T(8,128)S(1)}, f32[2,8,512]{2,1,0:T(8,128)S(1)}, f32[512,128]{1,0:T(8,128)S(1)}, f32[1,512]{1,0...) custom-call(f32[2,8,512]{2,1,0:T(8,128)} %bitcast.42, ...), custom_call_target="tpu_custom_call" | custom-call | flops 68719476736 | bytes 268435456 | tf_op jit(solution)/shard_map/setup/pallas_call | solution.py:344
  1.8 3.2 %collective-permute-start = (f32[2,8,512]{2,1,0:T(8,128)S(1)}, f32[2,8,512]{2,1,0:T(8,128)S(1)}, u32[]{:S(2)}, u32[]{:S(2)}) collective-permute-start(f32[2,8,512]{2,1,0:T(8,128)S(1)} %get-tuple-element.71.refs_7_.refs_12_.refs_4_), channel_id=1, source_target_pairs={{0,4},{1,5},{2,6},{3,7},{4,0},{5,1},{6,2},{7,3},{8,12},{9,13},{10,... | collective-permute-start | bytes 98312 | tf_op jit(solution)/shard_map/ppermute | solution.py:37
  5.0 0.0 copy-done
  5.0 2.9 %first0.1.refs_0_ = f32[192,128]{1,0:T(8,128)S(1)} custom-call(bf16[8,2,512,512]{3,2,1,0:T(8,128)(2,1)S(1)} %bitcast.28, bf16[2,512,512]{2,1,0:T(8,128)(2,1)S(1)} %bitcast.32, f32[2,8,512]{2,1,0:T(8,128)S(1)} %get-tuple-element.86.refs_2_, f32[512,128]{1,0:T(8,128)S(1)} %get-tuple-element.87.refs_3_), custom_call_target="tpu_custom_call" | custom-call | flops 22020096 | bytes 3145728 | tf_op jit(solution)/shard_map/first0/pallas_call | solution.py:362
  7.9 0.0 collective-permute-done.refs_8_
  7.9 1.0 %collective-permute-start.1 = (f32[2,2,8,512]{3,2,1,0:T(8,128)S(1)}, f32[2,2,8,512]{3,2,1,0:T(8,128)S(1)}, u32[]{:S(2)}, u32[]{:S(2)}) collective-permute-start(f32[2,2,8,512]{3,2,1,0:T(8,128)S(1)} %pad_maximum_fusion), channel_id=1, source_target_pairs={{0,1},{1,0},{2,3},{3,2},{4,5},{5,4},{6,7},{7,6},{8,9},{9,8},{10,11... | collective-permute-start | bytes 196616 | tf_op jit(solution)/shard_map/ppermute | solution.py:37
  8.9 1.3 %first1.1.refs_1_ = f32[80,128]{1,0:T(8,128)S(1)} custom-call(bf16[8,2,512,512]{3,2,1,0:T(8,128)(2,1)S(1)} %bitcast.29, bf16[2,512,512]{2,1,0:T(8,128)(2,1)S(1)} %bitcast.33, f32[2,8,512]{2,1,0:T(8,128)S(1)} %get-tuple-element.86.refs_2_, f32[512,128]{1,0:T(8,128)S(1)} %get-tuple-element.87.refs_3_), custom_call_target="tpu_custom_call" | custom-call | flops 9175040 | bytes 1310720 | tf_op jit(solution)/shard_map/first1/pallas_call | solution.py:362
  10.2 0.0 collective-permute-done.1
  10.2 1.4 %collective-permute-start.2 = (f32[2,8,512]{2,1,0:T(8,128)S(1)}, f32[2,8,512]{2,1,0:T(8,128)S(1)}, u32[]{:S(2)}, u32[]{:S(2)}) collective-permute-start(f32[2,8,512]{2,1,0:T(8,128)S(1)} %multiply_add_fusion.1), channel_id=1, source_target_pairs={{0,2},{1,3},{2,0},{3,1},{4,6},{5,7},{6,4},{7,5},{8,10},{9,11},{10,... | collective-permute-start | bytes 98312 | tf_op jit(solution)/shard_map/ppermute | solution.py:37
  11.6 3.6 %first2.1.refs_2_ = f32[240,128]{1,0:T(8,128)S(1)} custom-call(bf16[8,2,512,512]{3,2,1,0:T(8,128)(2,1)S(1)} %bitcast.30, bf16[2,512,512]{2,1,0:T(8,128)(2,1)S(1)} %bitcast.34, f32[2,8,512]{2,1,0:T(8,128)S(1)} %get-tuple-element.86.refs_2_, f32[512,128]{1,0:T(8,128)S(1)} %get-tuple-element.87.refs_3_), custom_call_target="tpu_custom_call" | custom-call | flops 27525120 | bytes 3932160 | tf_op jit(solution)/shard_map/first2/pallas_call | solution.py:362
  15.2 0.0 collective-permute-done.2.refs_11_
  15.3 0.1 middle.1.refs_0_
  15.4 2.2 %collective-permute-start.5 = (f32[1,5,8,512]{3,2,1,0:T(8,128)S(1)}, f32[1,5,8,512]{3,2,1,0:T(8,128)S(1)}, u32[]{:S(2)}, u32[]{:S(2)}) collective-permute-start(f32[1,5,8,512]{3,2,1,0:T(8,128)S(1)} %middle.1.refs_0_), channel_id=1, source_target_pairs={{0,24},{8,16},{16,8},{24,0},{1,25},{9,17},{17,9},{25,1},{2,26},{10... | collective-permute-start | bytes 245768 | tf_op jit(solution)/shard_map/ppermute | solution.py:37
  17.6 0.2 collective-permute-start.4
  17.8 0.3 collective-permute-start.3
  18.1 1.7 %widen.1 = (f32[8,2,512,512]{3,2,1,0:T(8,128)S(1)}, f32[8,512,512]{2,1,0:T(8,128)S(1)}) custom-call(bf16[8,2,512,512]{3,2,1,0:T(8,128)(2,1)S(1)} %bitcast.31), custom_call_target="tpu_custom_call" | custom-call | flops 11010048 | bytes 25165824 | tf_op jit(solution)/shard_map/widen/pallas_call | solution.py:405
  19.8 0.3 collective-permute-done.5.refs_3_
  20.1 1.9 %collective-permute-done.4.refs_2_ = f32[1,5,8,512]{3,2,1,0:T(8,128)S(1)} collective-permute-done((f32[1,5,8,512]{3,2,1,0:T(8,128)S(1)}, f32[1,5,8,512]{3,2,1,0:T(8,128)S(1)}, u32[]{:S(2)}, u32[]{:S(2)}) %collective-permute-start.4) | collective-permute-done | bytes 81952 | tf_op jit(solution)/shard_map/ppermute | solution.py:37
  22.0 0.0 collective-permute-done.3.refs_1_
  22.0 0.2 update.1
  22.2 2.3 %collective-permute-start.6 = (f32[2,8,512]{2,1,0:T(8,128)S(1)}, f32[2,8,512]{2,1,0:T(8,128)S(1)}, u32[]{:S(2)}, u32[]{:S(2)}) collective-permute-start(f32[2,8,512]{2,1,0:T(8,128)S(1)} %get-tuple-element.108.refs_7_), channel_id=1, source_target_pairs={{0,4},{1,5},{2,6},{3,7},{4,0},{5,1},{6,2},{7,3},{8,12},{9,13},{10,... | collective-permute-start | bytes 98312 | tf_op jit(solution)/shard_map/ppermute | solution.py:37
  24.5 2.6 %second0.1.refs_0_ = f32[176,128]{1,0:T(8,128)S(1)} custom-call(f32[8,2,512,512]{3,2,1,0:T(8,128)S(1)} %get-tuple-element.109.refs_0_, bf16[2,512,512]{2,1,0:T(8,128)(2,1)S(1)} %bitcast.35, f32[2,8,512]{2,1,0:T(8,128)S(1)} %get-tuple-element.123.refs_2_, f32[512,128]{1,0:T(8,128)S(1)} %get-tuple-element.124.refs_3_, ...), custom_call_target="tpu_custom_call" | custom-call | flops 20185088 | bytes 2883584 | tf_op jit(solution)/shard_map/second0/pallas_call | solution.py:362
  27.0 0.0 collective-permute-done.6.refs_8_
  27.0 1.5 %collective-permute-start.7 = (f32[2,2,8,512]{3,2,1,0:T(8,128)S(1)}, f32[2,2,8,512]{3,2,1,0:T(8,128)S(1)}, u32[]{:S(2)}, u32[]{:S(2)}) collective-permute-start(f32[2,2,8,512]{3,2,1,0:T(8,128)S(1)} %pad_maximum_fusion.1), channel_id=1, source_target_pairs={{0,1},{1,0},{2,3},{3,2},{4,5},{5,4},{6,7},{7,6},{8,9},{9,8},{10,11... | collective-permute-start | bytes 196616 | tf_op jit(solution)/shard_map/ppermute | solution.py:37
  28.5 1.4 %second1.1.refs_1_ = f32[96,128]{1,0:T(8,128)S(1)} custom-call(f32[8,2,512,512]{3,2,1,0:T(8,128)S(1)} %get-tuple-element.109.refs_0_, bf16[2,512,512]{2,1,0:T(8,128)(2,1)S(1)} %bitcast.36, f32[2,8,512]{2,1,0:T(8,128)S(1)} %get-tuple-element.123.refs_2_, f32[512,128]{1,0:T(8,128)S(1)} %get-tuple-element.124.refs_3_, ...), custom_call_target="tpu_custom_call" | custom-call | flops 11010048 | bytes 1572864 | tf_op jit(solution)/shard_map/second1/pallas_call | solution.py:362
  29.9 0.0 collective-permute-done.7
  30.0 0.2 collective-permute-start.8
  30.2 3.5 %second2.1.refs_2_ = f32[240,128]{1,0:T(8,128)S(1)} custom-call(f32[8,2,512,512]{3,2,1,0:T(8,128)S(1)} %get-tuple-element.109.refs_0_, bf16[2,512,512]{2,1,0:T(8,128)(2,1)S(1)} %bitcast.37, f32[2,8,512]{2,1,0:T(8,128)S(1)} %get-tuple-element.123.refs_2_, f32[512,128]{1,0:T(8,128)S(1)} %get-tuple-element.124.refs_3_, ...), custom_call_target="tpu_custom_call" | custom-call | flops 27525120 | bytes 3932160 | tf_op jit(solution)/shard_map/second2/pallas_call | solution.py:362
  33.7 0.0 collective-permute-done.8.refs_11_
  33.7 0.8 %finish.1 = (f32[2,8,512]{2,1,0:T(8,128)}, f32[2,8,512]{2,1,0:T(8,128)}, f32[2,8,512]{2,1,0:T(8,128)}) custom-call(f32[176,128]{1,0:T(8,128)S(1)} %second0.1.refs_0_, f32[96,128]{1,0:T(8,128)S(1)} %second1.1.refs_1_, f32[240,128]{1,0:T(8,128)S(1)} %second2.1.refs_2_, f32[2,8,512]{2,1,0:T(8,128)S(1)} %get-tuple-element.89.refs_3_, ...), custom_call_target="tpu_custom_call" | custom-call | tf_op jit(solution)/shard_map/finish/pallas_call | solution.py:384
  (7 shorter events, 0.1 us)
Async XLA Ops:
  0.6 4.3 %copy-start = (bf16[1,8,2,512,512]{4,3,2,1,0:T(8,128)(2,1)S(1)}, bf16[1,8,2,512,512]{4,3,2,1,0:T(8,128)(2,1)}, u32[]{:S(2)}) copy-start(bf16[1,8,2,512,512]{4,3,2,1,0:T(8,128)(2,1)} %param.6) | copy-start | bytes 25165828
  0.6 4.3 %copy-start.1 = (bf16[1,1,2,512,512]{4,3,2,1,0:T(8,128)(2,1)S(1)}, bf16[1,1,2,512,512]{4,3,2,1,0:T(8,128)(2,1)}, u32[]{:S(2)}) copy-start(bf16[1,1,2,512,512]{4,3,2,1,0:T(8,128)(2,1)} %param.5) | copy-start | bytes 3145732
  1.8 6.1 %collective-permute-start = (f32[2,8,512]{2,1,0:T(8,128)S(1)}, f32[2,8,512]{2,1,0:T(8,128)S(1)}, u32[]{:S(2)}, u32[]{:S(2)}) collective-permute-start(f32[2,8,512]{2,1,0:T(8,128)S(1)} %get-tuple-element.71.refs_7_.refs_12_.refs_4_), channel_id=1, source_target_pairs={{0,4},{1,5},{2,6},{3,7},{4,0},{5,1},{6,2},{7,3},{8,12},{9,13},{10,... | collective-permute-start | bytes 98312 | tf_op jit(solution)/shard_map/ppermute | solution.py:37
  7.9 2.3 %collective-permute-start.1 = (f32[2,2,8,512]{3,2,1,0:T(8,128)S(1)}, f32[2,2,8,512]{3,2,1,0:T(8,128)S(1)}, u32[]{:S(2)}, u32[]{:S(2)}) collective-permute-start(f32[2,2,8,512]{3,2,1,0:T(8,128)S(1)} %pad_maximum_fusion), channel_id=1, source_target_pairs={{0,1},{1,0},{2,3},{3,2},{4,5},{5,4},{6,7},{7,6},{8,9},{9,8},{10,11... | collective-permute-start | bytes 196616 | tf_op jit(solution)/shard_map/ppermute | solution.py:37
  10.2 5.0 %collective-permute-start.2 = (f32[2,8,512]{2,1,0:T(8,128)S(1)}, f32[2,8,512]{2,1,0:T(8,128)S(1)}, u32[]{:S(2)}, u32[]{:S(2)}) collective-permute-start(f32[2,8,512]{2,1,0:T(8,128)S(1)} %multiply_add_fusion.1), channel_id=1, source_target_pairs={{0,2},{1,3},{2,0},{3,1},{4,6},{5,7},{6,4},{7,5},{8,10},{9,11},{10,... | collective-permute-start | bytes 98312 | tf_op jit(solution)/shard_map/ppermute | solution.py:37
  15.4 4.7 %collective-permute-start.5 = (f32[1,5,8,512]{3,2,1,0:T(8,128)S(1)}, f32[1,5,8,512]{3,2,1,0:T(8,128)S(1)}, u32[]{:S(2)}, u32[]{:S(2)}) collective-permute-start(f32[1,5,8,512]{3,2,1,0:T(8,128)S(1)} %middle.1.refs_0_), channel_id=1, source_target_pairs={{0,24},{8,16},{16,8},{24,0},{1,25},{9,17},{17,9},{25,1},{2,26},{10... | collective-permute-start | bytes 245768 | tf_op jit(solution)/shard_map/ppermute | solution.py:37
  17.6 4.4 %collective-permute-start.4 = (f32[1,5,8,512]{3,2,1,0:T(8,128)S(1)}, f32[1,5,8,512]{3,2,1,0:T(8,128)S(1)}, u32[]{:S(2)}, u32[]{:S(2)}) collective-permute-start(f32[1,5,8,512]{3,2,1,0:T(8,128)S(1)} %middle.1.refs_0_), channel_id=1, source_target_pairs={{0,16},{8,24},{16,0},{24,8},{1,17},{9,25},{17,1},{25,9},{2,18},{10... | collective-permute-start | bytes 245768 | tf_op jit(solution)/shard_map/ppermute | solution.py:37
  17.8 4.2 %collective-permute-start.3 = (f32[1,5,8,512]{3,2,1,0:T(8,128)S(1)}, f32[1,5,8,512]{3,2,1,0:T(8,128)S(1)}, u32[]{:S(2)}, u32[]{:S(2)}) collective-permute-start(f32[1,5,8,512]{3,2,1,0:T(8,128)S(1)} %middle.1.refs_0_), channel_id=1, source_target_pairs={{0,8},{8,0},{16,24},{24,16},{1,9},{9,1},{17,25},{25,17},{2,10},{10... | collective-permute-start | bytes 245768 | tf_op jit(solution)/shard_map/ppermute | solution.py:37
  22.2 4.8 %collective-permute-start.6 = (f32[2,8,512]{2,1,0:T(8,128)S(1)}, f32[2,8,512]{2,1,0:T(8,128)S(1)}, u32[]{:S(2)}, u32[]{:S(2)}) collective-permute-start(f32[2,8,512]{2,1,0:T(8,128)S(1)} %get-tuple-element.108.refs_7_), channel_id=1, source_target_pairs={{0,4},{1,5},{2,6},{3,7},{4,0},{5,1},{6,2},{7,3},{8,12},{9,13},{10,... | collective-permute-start | bytes 98312 | tf_op jit(solution)/shard_map/ppermute | solution.py:37
  27.0 2.9 %collective-permute-start.7 = (f32[2,2,8,512]{3,2,1,0:T(8,128)S(1)}, f32[2,2,8,512]{3,2,1,0:T(8,128)S(1)}, u32[]{:S(2)}, u32[]{:S(2)}) collective-permute-start(f32[2,2,8,512]{3,2,1,0:T(8,128)S(1)} %pad_maximum_fusion.1), channel_id=1, source_target_pairs={{0,1},{1,0},{2,3},{3,2},{4,5},{5,4},{6,7},{7,6},{8,9},{9,8},{10,11... | collective-permute-start | bytes 196616 | tf_op jit(solution)/shard_map/ppermute | solution.py:37
  30.0 3.7 %collective-permute-start.8 = (f32[2,8,512]{2,1,0:T(8,128)S(1)}, f32[2,8,512]{2,1,0:T(8,128)S(1)}, u32[]{:S(2)}, u32[]{:S(2)}) collective-permute-start(f32[2,8,512]{2,1,0:T(8,128)S(1)} %multiply_add_fusion), channel_id=1, source_target_pairs={{0,2},{1,3},{2,0},{3,1},{4,6},{5,7},{6,4},{7,5},{8,10},{9,11},{10,... | collective-permute-start | bytes 98312 | tf_op jit(solution)/shard_map/ppermute | solution.py:37
